TPU v7x, 32 devices: a whole 2x2x4 slice. The times are simulated.
32 devices in a mesh: grp: 2 (over y), wide: 4 (over z), narrow: 4 (over x, core).
Axes of the slice: x: 2, y: 2, z: 4, core: 2. Of those that a mesh axis runs over, the one named last changes fastest.
Arguments:
- queries: bfloat16 [2, 128, 32, 128], P(None, ('grp', 'wide'), 'narrow'), parts along dimension 1
- key_cache: bfloat16 [2, 128, 64, 4, 128], P(None, ('grp', 'wide'), None, 'narrow'), parts along dimension 1
- cached_value_rows: bfloat16 [2, 128, 64, 4, 128], P(None, ('grp', 'wide'), None, 'narrow'), parts along dimension 1, may hold values from -5 to 5
- lengths: int32 [2, 128], P(None, ('grp', 'wide')), parts along dimension 1, may hold values from 8 to 64, as said below
- residual: bfloat16 [2, 128, 2048], P(None, ('grp', 'wide'), 'narrow'), parts along dimension 1, may hold values from -6 to 6
- w_out: bfloat16 [4096, 2048], P('narrow', 'wide'), may hold values from -0.09375 to 0.09375
- norm_gain: float32 [2048], replicated, may hold values from 0.1 to 1.9
- expert_ids: int32 [2, 128, 8], P(None, ('grp', 'wide')), parts along dimension 1, may hold values from 0 to 63, all different within a row; in each aligned block of 16 rows (0 to 15, 16 to 31, ..., all dimensions but the last counted through in order) at most 3 rows name the same one
- route_weights: float32 [2, 128, 8], P(None, ('grp', 'wide')), parts along dimension 1, may hold values from 0.05 to 1
- w_gate: bfloat16 [64, 2048, 1024], P('wide', None, 'narrow'), may hold values from -0.125 to 0.125
- w_up: bfloat16 [64, 2048, 1024], P('wide', None, 'narrow'), may hold values from -0.125 to 0.125
- w_down: bfloat16 [64, 1024, 2048], P('wide', 'narrow'), may hold values from -0.1875 to 0.1875
Outputs:
- layer_out: bfloat16 [2, 128, 2048], P(None, ('grp', 'wide'), 'narrow'), parts along dimension 1
There are 2 independent parts, one for each index of `grp`. A program takes and returns all parts, laid end to end along the dimension named above; an argument that names none is the same for every part. Nothing has to cross between parts.
Inputs may be any that keep to these rules, and one draw needn't show every extreme that they name: `expert_ids`: the 8 experts of a row differ. Among the rows of one device in one microbatch (16 rows, aligned blocks) no expert is named by more than 3 rows; every expert is named by some row. `lengths`: the first request of each microbatch uses all 64 positions.
All inputs are finite; a program needn't handle non-finite values.
Results may differ from a plain program's by a relative error of at most 0.015.
Values may be sent and summed in bfloat16 or wider, within the bound.
No kernel may reach another device: no remote copies, remote signals or barrier semaphores. Data moves between devices by JAX's collectives and lax.ppermute only.
A program may use at most 192 MiB of HBM per device.

v0:
```python
import math

import jax
import jax.numpy as jnp
from jax import lax
from jax.sharding import PartitionSpec as P

EXPERTS = 64
CAP = 3


def attend(query_rows, keys, values, valid_len):
    row_count, q_heads, head_size = query_rows.shape
    slot_count = keys.shape[1]
    kv_heads = keys.shape[2]
    flat_keys = keys.reshape(row_count, slot_count, kv_heads * head_size)
    flat_values = values.reshape(row_count, slot_count, kv_heads * head_size)
    position = jnp.arange(slot_count)
    usable = position[None, :] < valid_len[:, None]
    scores = jnp.einsum(
        "rgd,rcd->rgc", query_rows, flat_keys, preferred_element_type=jnp.float32
    ) / math.sqrt(head_size)
    scores = jnp.where(usable[:, None, :], scores, -1e30)
    largest = jnp.max(scores, axis=-1, keepdims=True)
    weight = jnp.exp(scores - largest)
    probs = (weight / jnp.sum(weight, axis=-1, keepdims=True)).astype(jnp.bfloat16)
    mixed = jnp.einsum("rgc,rcd->rgd", probs, flat_values, preferred_element_type=jnp.float32)
    results = mixed.astype(jnp.bfloat16)
    return results.reshape(row_count, q_heads * head_size)


def route_tables(chosen, weights, expert_count, capacity):
    row_count, top_count = chosen.shape
    pairs = chosen.reshape(-1)
    onehot = (pairs[:, None] == jnp.arange(expert_count)[None, :]).astype(jnp.int32)
    before = jnp.cumsum(onehot, axis=0) - onehot
    rank = jnp.sum(onehot * before, axis=1)
    slot = pairs * capacity + rank
    select = (slot[:, None] == jnp.arange(expert_count * capacity)[None, :]).astype(jnp.float32)
    select = select.reshape(row_count, top_count, expert_count * capacity)
    dispatch = jnp.sum(select, axis=1).astype(jnp.bfloat16)
    combine = jnp.sum(select * weights[:, :, None], axis=1)
    return (dispatch, combine)


def expert_block(pieces, norm_gain, w_gate, w_up, w_down):
    parts_count = pieces.shape[0]
    local_experts, model_width, hidden_width = w_gate.shape
    part_width = model_width // parts_count
    values = pieces.astype(jnp.float32)
    square = jnp.mean(values * values, axis=(0, 4), keepdims=True)
    gain_parts = norm_gain.reshape(parts_count, 1, 1, 1, part_width)
    normed = (values * lax.rsqrt(square + 1e-06) * gain_parts).astype(jnp.bfloat16)
    gate_parts = w_gate.reshape(local_experts, parts_count, part_width, hidden_width)
    up_parts = w_up.reshape(local_experts, parts_count, part_width, hidden_width)
    gate = jnp.einsum("nsjcd,jndf->sjcf", normed, gate_parts, preferred_element_type=jnp.float32)
    upper = jnp.einsum("nsjcd,jndf->sjcf", normed, up_parts, preferred_element_type=jnp.float32)
    hidden = (jax.nn.silu(gate) * upper).astype(jnp.bfloat16)
    narrow_count = lax.axis_size("narrow")
    down_parts = w_down.reshape(
        local_experts, w_down.shape[1], narrow_count, model_width // narrow_count
    )
    partial_out = jnp.einsum(
        "sjcf,jfnd->nsjcd", hidden, down_parts, preferred_element_type=jnp.float32
    )
    summed = lax.psum_scatter(
        partial_out.astype(jnp.bfloat16), "narrow", scatter_dimension=0, tiled=True
    ).astype(jnp.float32)[0]
    return lax.all_to_all(
        summed.astype(jnp.bfloat16), "wide", split_axis=0, concat_axis=0, tiled=True
    )


def local(
    queries,
    key_cache,
    cached_value_rows,
    lengths,
    residual,
    w_out,
    norm_gain,
    expert_ids,
    route_weights,
    w_gate,
    w_up,
    w_down,
):
    micro_count = queries.shape[0]
    wide_count = lax.axis_size("wide")
    local_experts = w_gate.shape[0]
    capacity = CAP
    attended = [
        attend(
            queries[index_values],
            key_cache[index_values],
            cached_value_rows[index_values],
            lengths[index_values],
        )
        for index_values in range(micro_count)
    ]
    terms = []
    for index_values in range(micro_count):
        columns = jnp.dot(
            lax.all_gather(attended[index_values], "wide", axis=0, tiled=True),
            w_out,
            preferred_element_type=jnp.float32,
        )
        terms.append(
            lax.all_to_all(
                columns.astype(jnp.bfloat16), "wide", split_axis=0, concat_axis=1, tiled=True
            ).astype(columns.dtype)
        )
    partial_sum = jnp.stack(terms)
    projected = lax.psum_scatter(
        partial_sum.astype(jnp.bfloat16), "narrow", scatter_dimension=2, tiled=True
    ).astype(jnp.float32)
    stream = (residual.astype(jnp.float32) + projected).astype(jnp.bfloat16)
    outputs = []
    for index_values in range(micro_count):
        dispatch, combine = route_tables(
            expert_ids[index_values], route_weights[index_values], EXPERTS, capacity
        )
        packed = lax.dot_general(
            dispatch,
            stream[index_values],
            (((0,), (0,)), ((), ())),
            preferred_element_type=jnp.float32,
        )
        packed = packed.astype(jnp.bfloat16).reshape(
            wide_count, local_experts, capacity, stream.shape[2]
        )
        back = (
            lambda rows_in: expert_block(
                lax.all_gather(rows_in[None], "narrow", axis=0, tiled=True),
                norm_gain,
                w_gate,
                w_up,
                w_down,
            )
        )(lax.all_to_all(packed, "wide", split_axis=0, concat_axis=0, tiled=True))
        returned = back.reshape(wide_count * local_experts * capacity, back.shape[3]).astype(
            jnp.float32
        )
        mixed = jnp.dot(combine, returned, precision=lax.Precision.HIGHEST)
        outputs.append((stream[index_values].astype(jnp.float32) + mixed).astype(jnp.bfloat16))
    return jnp.stack(outputs)


def solution(mesh):
    in_specs = (
        P(None, ("grp", "wide"), "narrow", None),
        P(None, ("grp", "wide"), None, "narrow", None),
        P(None, ("grp", "wide"), None, "narrow", None),
        P(None, ("grp", "wide")),
        P(None, ("grp", "wide"), "narrow"),
        P("narrow", "wide"),
        P(),
        P(None, ("grp", "wide"), None),
        P(None, ("grp", "wide"), None),
        P("wide", None, "narrow"),
        P("wide", None, "narrow"),
        P("wide", "narrow", None),
    )
    out_specs = P(None, ("grp", "wide"), "narrow")
    return jax.shard_map(local, mesh=mesh, in_specs=in_specs, out_specs=out_specs, check_vma=False)
```

profile of v0, /device:TPU:0, one launch (start us, length us, event | category | flops | bytes accessed | tf_op | source)
XLA Modules:
  0.0 230.5 jit_solution(13708473463227930907)
XLA Ops:
  7.4 1.2 fusion.34
  8.8 1.3 convolution_convert_fusion.5
  10.2 15.1 %all_gather.12 = bf16[64,1024]{1,0:T(8,128)(2,1)S(1)} all-gather(bf16[16,1024]{1,0:T(8,128)(2,1)S(1)} %bitcast.182), channel_id=1, replica_groups=mesh['grp'=2,'wide'=4,'narrow'=4] {'wide'}, dimensions={0}, use_global_device_ids=true | all-gather | bytes 163840 | tf_op jit(solution)/shard_map/all_gather | solution.py:104
  26.2 5.0 %all-to-all-start = ((bf16[4,16,512]{2,1,0:T(8,128)(2,1)}), bf16[4,16,512]{2,1,0:T(8,128)(2,1)S(1)}, u32[]{:S(2)}, u32[]{:S(2)}) async-start(bf16[4,16,512]{2,1,0:T(8,128)(2,1)} %bitcast.6), calls=%async_computation | async-start | bytes 131072 | tf_op jit(solution)/shard_map/all_to_all | solution.py:109
  32.5 1.3 convolution_convert_fusion.4
  33.9 13.9 %all_gather.13 = bf16[64,1024]{1,0:T(8,128)(2,1)S(1)} all-gather(bf16[16,1024]{1,0:T(8,128)(2,1)S(1)} %bitcast.183), channel_id=1, replica_groups=mesh['grp'=2,'wide'=4,'narrow'=4] {'wide'}, dimensions={0}, use_global_device_ids=true | all-gather | bytes 163840 | tf_op jit(solution)/shard_map/all_gather | solution.py:104
  51.0 4.6 %all-to-all-start.1 = ((bf16[4,16,512]{2,1,0:T(8,128)(2,1)}), bf16[4,16,512]{2,1,0:T(8,128)(2,1)S(1)}, u32[]{:S(2)}, u32[]{:S(2)}) async-start(bf16[4,16,512]{2,1,0:T(8,128)(2,1)} %bitcast.14), calls=%async_computation.1 | async-start | bytes 131072 | tf_op jit(solution)/shard_map/all_to_all | solution.py:109
  56.4 4.9 %all-to-all-done.1 = bf16[4,16,512]{2,1,0:T(8,128)(2,1)S(1)} async-done(((bf16[4,16,512]{2,1,0:T(8,128)(2,1)}), bf16[4,16,512]{2,1,0:T(8,128)(2,1)S(1)}, u32[]{:S(2)}, u32[]{:S(2)}) %all-to-all-start.1) | async-done | bytes 65568 | tf_op jit(solution)/shard_map/all_to_all | solution.py:109
  63.7 27.8 %reshape.174 = bf16[16,256,4,512]{3,2,1,0:T(4,128)(2,1)} reshape(bf16[16,256,2048]{2,1,0:T(8,128)(2,1)} %param.23) | data formatting | bytes 33554432 | tf_op jit(solution)/shard_map/reshape | solution.py:60
  93.6 3.4 %all-to-all-start.2 = ((bf16[4,16,3,512]{3,1,2,0:T(8,128)(2,1)}), bf16[4,16,3,512]{3,1,2,0:T(8,128)(2,1)S(1)}, u32[]{:S(2)}, u32[]{:S(2)}) async-start(bf16[4,16,3,512]{3,1,2,0:T(8,128)(2,1)} %copy.151), calls=%async_computation.3 | async-start | bytes 393216 | tf_op jit(solution)/shard_map/all_to_all | solution.py:140
  98.2 6.9 %all-to-all-done.2 = bf16[4,16,3,512]{3,1,2,0:T(8,128)(2,1)S(1)} async-done(((bf16[4,16,3,512]{3,1,2,0:T(8,128)(2,1)}), bf16[4,16,3,512]{3,1,2,0:T(8,128)(2,1)S(1)}, u32[]{:S(2)}, u32[]{:S(2)}) %all-to-all-start.2) | async-done | bytes 196640 | tf_op jit(solution)/shard_map/all_to_all | solution.py:140
  105.1 3.4 %all-to-all-start.4 = ((bf16[4,16,3,512]{3,1,2,0:T(8,128)(2,1)}), bf16[4,16,3,512]{3,1,2,0:T(8,128)(2,1)S(1)}, u32[]{:S(2)}, u32[]{:S(2)}) async-start(bf16[4,16,3,512]{3,1,2,0:T(8,128)(2,1)} %copy.164), calls=%async_computation.6 | async-start | bytes 393216 | tf_op jit(solution)/shard_map/all_to_all | solution.py:140
  108.5 8.6 %all-gather = bf16[16,16,3,512]{3,1,2,0:T(8,128)(2,1)S(1)} all-gather(bf16[4,16,3,512]{3,1,2,0:T(8,128)(2,1)S(1)} %all-to-all-done.2), channel_id=2, replica_groups=mesh['grp'=2,'wide'=4,'narrow'=4] {'narrow'}, dimensions={0}, use_global_device_ids=true | all-gather | bytes 983040 | tf_op jit(solution)/shard_map/all_gather | solution.py:134
  117.4 8.9 %all-gather.1 = bf16[16,16,3,512]{3,1,2,0:T(8,128)(2,1)S(1)} all-gather(bf16[4,16,3,512]{3,1,2,0:T(8,128)(2,1)S(1)} %all-to-all-done.4), channel_id=3, replica_groups=mesh['grp'=2,'wide'=4,'narrow'=4] {'narrow'}, dimensions={0}, use_global_device_ids=true | all-gather | bytes 983040 | tf_op jit(solution)/shard_map/all_gather | solution.py:134
  127.0 8.5 %convolution_bitcast_fusion.3 = f32[4,16,3,256]{3,0,2,1:T(4,128)S(1)} fusion(bf16[16,4,512,256,1]{3,2,1,4,0:T(8,128)(2,1)} %bitcast.170, bf16[4,4,16,3,512]{4,2,3,1,0:T(8,128)(2,1)S(1)} %get-tuple-element.9), kind=kOutput, calls=%fused_computation.27 | convolution fusion | flops 201326592 | bytes 17760256 | tf_op jit(solution)/shard_map/nsjcd,jndf->sjcf/dot_general | solution.py:56
  135.5 19.7 %fusion.21 = bf16[4,4,16,3,512]{4,1,0,3,2:T(4,128)(2,1)S(1)} fusion(bf16[16,256,4,512,1]{3,2,1,0,4:T(4,128)(2,1)} %bitcast.168, bf16[16,4,512,256,1]{3,2,1,4,0:T(8,128)(2,1)} %bitcast.172, bf16[4,4,16,3,512]{4,2,3,1,0:T(8,128)(2,1)S(1)} %get-tuple-element.9, f32[4,16,3,256]{3,0,2,1:T(4,128)S(1)} %convolution_bitcast_fusion.3), kind=kOutput, calls=%fused_computation.19 | convolution fusion | flops 403341312 | bytes 35323904 | tf_op jit(solution)/shard_map/sjcf,jfnd->nsjcd/dot_general | solution.py:63
  155.2 1.3 copy.158
  156.8 8.6 %convolution_bitcast_fusion.1 = f32[4,16,3,256]{3,0,2,1:T(4,128)S(1)} fusion(bf16[16,4,512,256,1]{3,2,1,4,0:T(8,128)(2,1)} %bitcast.171, bf16[4,4,16,3,512]{4,2,3,1,0:T(8,128)(2,1)S(1)} %get-tuple-element.10), kind=kOutput, calls=%fused_computation.24 | convolution fusion | flops 201326592 | bytes 17760256 | tf_op jit(solution)/shard_map/nsjcd,jndf->sjcf/dot_general | solution.py:56
  165.5 19.7 %fusion.18 = bf16[4,4,16,3,512]{4,1,0,3,2:T(4,128)(2,1)S(1)} fusion(bf16[16,256,4,512,1]{3,2,1,0,4:T(4,128)(2,1)} %bitcast.169, bf16[16,4,512,256,1]{3,2,1,4,0:T(8,128)(2,1)} %bitcast.173, bf16[4,4,16,3,512]{4,2,3,1,0:T(8,128)(2,1)S(1)} %get-tuple-element.10, f32[4,16,3,256]{3,0,2,1:T(4,128)S(1)} %convolution_bitcast_fusion.1), kind=kOutput, calls=%fused_computation.18 | convolution fusion | flops 403341312 | bytes 35323904 | tf_op jit(solution)/shard_map/sjcf,jfnd->nsjcd/dot_general | solution.py:63
  185.2 1.3 copy.171
  186.6 5.0 %all-to-all-start.3 = ((bf16[4,16,3,512]{3,1,2,0:T(8,128)(2,1)}), bf16[4,16,3,512]{3,1,2,0:T(8,128)(2,1)S(1)}, u32[]{:S(2)}, u32[]{:S(2)}) async-start(bf16[4,16,3,512]{3,1,2,0:T(8,128)(2,1)} %bitcast.180), calls=%async_computation.5 | async-start | bytes 393216 | tf_op jit(solution)/shard_map/all_to_all | solution.py:69
  191.6 18.8 %reduce-scatter.8.cloned.1.call-done = bf16[1,4,16,3,512]{4,2,3,1,0:T(8,128)(2,1)} async-done(((bf16[4,4,16,3,512]{4,2,3,1,0:T(8,128)(2,1)}), bf16[1,4,16,3,512]{4,2,3,1,0:T(8,128)(2,1)}) %reduce-scatter.8.cloned.1.call-update) | async-done | bytes 196624 | tf_op jit(solution)/shard_map/reduce_scatter | solution.py:66
  210.5 4.6 %all-to-all-start.5 = ((bf16[4,16,3,512]{3,1,2,0:T(8,128)(2,1)}), bf16[4,16,3,512]{3,1,2,0:T(8,128)(2,1)S(1)}, u32[]{:S(2)}, u32[]{:S(2)}) async-start(bf16[4,16,3,512]{3,1,2,0:T(8,128)(2,1)} %bitcast.181), calls=%async_computation.8 | async-start | bytes 393216 | tf_op jit(solution)/shard_map/all_to_all | solution.py:69
  215.4 7.2 %all-to-all-done.5 = bf16[4,16,3,512]{3,1,2,0:T(8,128)(2,1)S(1)} async-done(((bf16[4,16,3,512]{3,1,2,0:T(8,128)(2,1)}), bf16[4,16,3,512]{3,1,2,0:T(8,128)(2,1)S(1)}, u32[]{:S(2)}, u32[]{:S(2)}) %all-to-all-start.5) | async-done | bytes 196640 | tf_op jit(solution)/shard_map/all_to_all | solution.py:69
  (76 shorter events, 16.0 us)
Async XLA Ops:
  6.5 18.7 %copy-start = (bf16[1024,512]{1,0:T(8,128)(2,1)S(1)}, bf16[1024,512]{1,0:T(8,128)(2,1)}, u32[]{:S(2)}) copy-start(bf16[1024,512]{1,0:T(8,128)(2,1)} %param.17) | copy-start | bytes 3145732
  26.2 24.8 %all-to-all-start = ((bf16[4,16,512]{2,1,0:T(8,128)(2,1)}), bf16[4,16,512]{2,1,0:T(8,128)(2,1)S(1)}, u32[]{:S(2)}, u32[]{:S(2)}) async-start(bf16[4,16,512]{2,1,0:T(8,128)(2,1)} %bitcast.6), calls=%async_computation | async-start | bytes 131072 | tf_op jit(solution)/shard_map/all_to_all | solution.py:109
  51.0 10.3 %all-to-all-start.1 = ((bf16[4,16,512]{2,1,0:T(8,128)(2,1)}), bf16[4,16,512]{2,1,0:T(8,128)(2,1)S(1)}, u32[]{:S(2)}, u32[]{:S(2)}) async-start(bf16[4,16,512]{2,1,0:T(8,128)(2,1)} %bitcast.14), calls=%async_computation.1 | async-start | bytes 131072 | tf_op jit(solution)/shard_map/all_to_all | solution.py:109
  55.6 36.1 %reduce-scatter.4.cloned.1.call-start = ((), (), s32[]{:S(2)}) async-start(), calls=%async_computation.9 | async-start | bytes 163840 | tf_op jit(solution)/shard_map/reduce_scatter | solution.py:114
  63.7 28.0 %copy-start.2 = (bf16[2,16,512]{2,1,0:T(8,128)(2,1)S(1)}, bf16[2,16,512]{2,1,0:T(8,128)(2,1)}, u32[]{:S(2)}) copy-start(bf16[2,16,512]{2,1,0:T(8,128)(2,1)} %param.16) | copy-start | bytes 98308
  93.6 11.5 %all-to-all-start.2 = ((bf16[4,16,3,512]{3,1,2,0:T(8,128)(2,1)}), bf16[4,16,3,512]{3,1,2,0:T(8,128)(2,1)S(1)}, u32[]{:S(2)}, u32[]{:S(2)}) async-start(bf16[4,16,3,512]{3,1,2,0:T(8,128)(2,1)} %copy.151), calls=%async_computation.3 | async-start | bytes 393216 | tf_op jit(solution)/shard_map/all_to_all | solution.py:140
  105.1 12.3 %all-to-all-start.4 = ((bf16[4,16,3,512]{3,1,2,0:T(8,128)(2,1)}), bf16[4,16,3,512]{3,1,2,0:T(8,128)(2,1)S(1)}, u32[]{:S(2)}, u32[]{:S(2)}) async-start(bf16[4,16,3,512]{3,1,2,0:T(8,128)(2,1)} %copy.164), calls=%async_computation.6 | async-start | bytes 393216 | tf_op jit(solution)/shard_map/all_to_all | solution.py:140
  108.5 78.1 %reduce-scatter.6.cloned.1.call-start = ((), (), s32[]{:S(2)}) async-start(), calls=%async_computation.10 | async-start | bytes 983040 | tf_op jit(solution)/shard_map/reduce_scatter | solution.py:66
  156.6 53.9 %reduce-scatter.8.cloned.1.call-start = ((), (), s32[]{:S(2)}) async-start(), calls=%async_computation.11 | async-start | bytes 983040 | tf_op jit(solution)/shard_map/reduce_scatter | solution.py:66
  156.8 67.1 %copy-start.1 = (bf16[1024,512]{1,0:T(8,128)(2,1)S(1)}, bf16[1024,512]{1,0:T(8,128)(2,1)}, u32[]{:S(2)}) copy-start(bf16[1024,512]{1,0:T(8,128)(2,1)} %param.17) | copy-start | bytes 3145732
  186.6 23.9 %all-to-all-start.3 = ((bf16[4,16,3,512]{3,1,2,0:T(8,128)(2,1)}), bf16[4,16,3,512]{3,1,2,0:T(8,128)(2,1)S(1)}, u32[]{:S(2)}, u32[]{:S(2)}) async-start(bf16[4,16,3,512]{3,1,2,0:T(8,128)(2,1)} %bitcast.180), calls=%async_computation.5 | async-start | bytes 393216 | tf_op jit(solution)/shard_map/all_to_all | solution.py:69
  210.5 12.1 %all-to-all-start.5 = ((bf16[4,16,3,512]{3,1,2,0:T(8,128)(2,1)}), bf16[4,16,3,512]{3,1,2,0:T(8,128)(2,1)S(1)}, u32[]{:S(2)}, u32[]{:S(2)}) async-start(bf16[4,16,3,512]{3,1,2,0:T(8,128)(2,1)} %bitcast.181), calls=%async_computation.8 | async-start | bytes 393216 | tf_op jit(solution)/shard_map/all_to_all | solution.py:69
Sparse Core Ops, SparseCore 0:
  62.2 18.1 reduce-scatter.3
  156.7 23.7 reduce-scatter.5
  186.7 23.7 reduce-scatter.7
where the time goes:
time: 232 us; the launch traced here: 230 us
  matrix products  64.3 us (28%)
  blocking collectives  46.5 us (20%)
  waiting for transfers between devices  37.9 us (16%)
  local copies, waits for them, and re-layouts  36.9 us (16%)
  starting transfers between devices  26.2 us (11%)
  between operations  13.4 us (6%)
  other arithmetic  5.3 us (2%)
    dot_general x2, matrix products, expert_block(): jnp.einsum('sjcf,jfnd->nsjcd', hidden, down_parts, preferred_element_type...  39.4 us
    all_gather x2, blocking collectives, local(): lax.all_gather(attended[index_values], 'wide', axis=0, tiled=True)  29 us
    reshape x1, local copies, waits for them, and re-layouts, expert_block(): w_down.reshape(local_experts, w_down.shape[1], narrow_count, model_width...  27.8 us
    reduce_scatter x2, waiting for transfers between devices, expert_block(): lax.psum_scatter(partial_out.astype(jnp.bfloat16), 'narrow', scatter_dime...  18.9 us
    all_gather x2, blocking collectives, local(): lax.all_gather(rows_in[None], 'narrow', axis=0, tiled=True)  17.5 us
    dot_general x2, matrix products, expert_block(): jnp.einsum('nsjcd,jndf->sjcf', normed, gate_parts, preferred_element_type...  17.1 us
    all_to_all x2, starting transfers between devices, expert_block(): lax.all_to_all(summed.astype(jnp.bfloat16), 'wide', split_axis=0, concat_...  9.63 us
    all_to_all x2, starting transfers between devices, local(): lax.all_to_all(columns.astype(jnp.bfloat16), 'wide', split_axis=0, concat...  9.55 us
  transfers between devices with their start and end apart: 9, of which 4 were waited for; matrix products, arithmetic and copies ran while one was open for 29% of the time, Pallas kernels for 0%

commit v1 on v0

--- a/solution.py
+++ b/solution.py
@@ -3,6 +3,8 @@
 import jax
 import jax.numpy as jnp
 from jax import lax
+from jax.experimental import pallas as pl
+from jax.experimental.pallas import tpu as pltpu
 from jax.sharding import PartitionSpec as P
 
 EXPERTS = 64
@@ -146,6 +148,232 @@
     return jnp.stack(outputs)
 
 
+def flip_permute(value, axis, mask):
+    size = lax.axis_size(axis)
+    return lax.ppermute(value, axis, [(i, i ^ mask) for i in range(size)])
+
+
+def attend_kernel(len_ref, q_ref, k_ref, v_ref, ids_ref, wts_ref, out_ref, mixed_ref):
+    rows, heads = out_ref.shape[0], q_ref.shape[0] // out_ref.shape[0]
+    width = q_ref.shape[1]
+    slots = k_ref.shape[0] // rows
+    group = 256 // slots
+    micro, per_micro = len_ref.shape
+    row_request = lax.broadcasted_iota(jnp.int32, (group * heads, group * slots), 0) // heads
+    column = lax.broadcasted_iota(jnp.int32, (group * heads, group * slots), 1)
+    place = column - row_request * slots
+    for g in range(rows // group):
+        limit = jnp.zeros_like(place)
+        for i in range(group):
+            r = g * group + i
+            limit = jnp.where(row_request == i, len_ref[r // per_micro, r % per_micro], limit)
+        q = q_ref[g * group * heads:(g + 1) * group * heads, :]
+        k = k_ref[g * group * slots:(g + 1) * group * slots, :]
+        v = v_ref[g * group * slots:(g + 1) * group * slots, :]
+        scores = lax.dot_general(
+            q, k, (((1,), (1,)), ((), ())), preferred_element_type=jnp.float32
+        ) * (1.0 / math.sqrt(width))
+        usable = (place >= 0) & (place < limit)
+        scores = jnp.where(usable, scores, -1e30)
+        weight = jnp.exp(scores - jnp.max(scores, axis=-1, keepdims=True))
+        probs = (weight / jnp.sum(weight, axis=-1, keepdims=True)).astype(jnp.bfloat16)
+        mixed_ref[g * group * heads:(g + 1) * group * heads, :] = jnp.dot(
+            probs, v, preferred_element_type=jnp.float32
+        )
+    for h in range(heads):
+        out_ref[:, h * width:(h + 1) * width] = mixed_ref[
+            pl.ds(h, rows, stride=heads), :
+        ].astype(jnp.bfloat16)
+    lanes = 64
+    expert = lax.broadcasted_iota(jnp.int32, (lanes, per_micro), 0)
+    eye = (
+        lax.broadcasted_iota(jnp.int32, (per_micro, per_micro), 0)
+        == lax.broadcasted_iota(jnp.int32, (per_micro, per_micro), 1)
+    ).astype(jnp.bfloat16)
+    for m in range(micro):
+        total = jnp.zeros((lanes, per_micro), jnp.float32)
+        for t in range(ids_ref.shape[1]):
+            total += jnp.where(
+                expert == ids_ref[m, t:t + 1, :], wts_ref[m, t:t + 1, :], 0.0
+            )
+        high = total.astype(jnp.bfloat16)
+        low = (total - high.astype(jnp.float32)).astype(jnp.bfloat16)
+        both = jnp.concatenate([high, low], axis=0)
+        out_ref[m * per_micro:(m + 1) * per_micro, heads * width:] = lax.dot_general(
+            eye, both, (((1,), (1,)), ((), ())), preferred_element_type=jnp.float32
+        ).astype(jnp.bfloat16)
+
+
+def project_kernel(where_ref, own_ref, got1_ref, got2_ref, got3_ref, w_ref, res_ref,
+                   keep_ref, send_ref):
+    wide, narrow = where_ref[0], where_ref[1]
+    depth = w_ref.shape[0]
+    half = keep_ref.shape[1]
+    rows = own_ref.shape[0]
+    features = jnp.concatenate(
+        [r[:, :depth] for r in (own_ref, got1_ref, got2_ref, got3_ref)], axis=0
+    )
+    mine = pl.ds(pl.multiple_of((narrow & 1) * half, half), half)
+    other = pl.ds(pl.multiple_of((1 - (narrow & 1)) * half, half), half)
+    spot = pl.ds(pl.multiple_of((wide ^ narrow) * rows, rows), rows)
+    keep_ref[...] = jnp.dot(features, w_ref[:, mine], preferred_element_type=jnp.float32)
+    keep_ref[spot, :] += res_ref[:, mine].astype(jnp.float32)
+    part = jnp.dot(features, w_ref[:, other], preferred_element_type=jnp.float32)
+    part_rows = lax.broadcasted_iota(jnp.int32, part.shape, 0) // rows
+    extra = res_ref[:, other].astype(jnp.float32)
+    extra = jnp.concatenate([extra] * (part.shape[0] // rows), axis=0)
+    part = jnp.where(part_rows == (wide ^ narrow), part + extra, part)
+    send_ref[...] = part.astype(jnp.bfloat16)
+
+
+def expert_kernel(where_ref, mine_ref, other_ref, cw0_ref, cw1_ref, cw2_ref, cw3_ref,
+                  gain_ref, wg_ref, wu_ref, wd_ref, keep_ref, send_ref, stream_ref,
+                  x_ref, hid_ref):
+    wide, narrow = where_ref[0], where_ref[1]
+    core = narrow & 1
+    blocks, total, half = mine_ref.shape
+    rows = total // blocks
+    experts, depth, width = wg_ref.shape
+    square = jnp.zeros((total, 1), jnp.float32)
+    for s in range(blocks):
+        for piece, side in ((mine_ref, core), (other_ref, 1 - core)):
+            place = pl.multiple_of((wide ^ s) * (2 * half) + side * half, half)
+            lifted = jnp.concatenate(
+                [piece[s, (u ^ s) * rows:((u ^ s) + 1) * rows, :] for u in range(blocks)], axis=0
+            )
+            x_ref[:, pl.ds(place, half)] = lifted
+            value = lifted.astype(jnp.float32)
+            square += jnp.sum(value * value, axis=1, keepdims=True)
+    own = pl.multiple_of(narrow * (2 * half), 2 * half)
+    stream_ref[...] = x_ref[:rows, pl.ds(own, 2 * half)]
+    scale = lax.rsqrt(square * (1.0 / depth) + 1e-6)
+    for b in range(depth // 512):
+        cols = slice(b * 512, (b + 1) * 512)
+        x_ref[:, cols] = (
+            x_ref[:, cols].astype(jnp.float32) * scale * gain_ref[:, cols]
+        ).astype(jnp.bfloat16)
+    mix = jnp.concatenate([r[...] for r in (cw0_ref, cw1_ref, cw2_ref, cw3_ref)], axis=0)
+    lane = lax.broadcasted_iota(jnp.int32, (mix.shape[1], width), 0) % (mix.shape[1] // 2)
+
+    def one(e, carry):
+        gate = jnp.dot(x_ref[...], wg_ref[e], preferred_element_type=jnp.float32)
+        upper = jnp.dot(x_ref[...], wu_ref[e], preferred_element_type=jnp.float32)
+        pick = (lane == wide * experts + e).astype(jnp.bfloat16)
+        share = jnp.dot(mix, pick, preferred_element_type=jnp.float32)
+        hidden = gate / (1.0 + jnp.exp(-gate)) * upper * share
+        hid_ref[:, pl.ds(pl.multiple_of(e * width, width), width)] = hidden.astype(jnp.bfloat16)
+        return carry
+
+    lax.fori_loop(0, experts, one, 0)
+    block = 2 * half
+    for j in (1, 3, 0, 2):
+        out = jnp.dot(
+            hid_ref[...],
+            wd_ref[:, pl.ds(pl.multiple_of((narrow ^ j) * block, block), block)],
+            preferred_element_type=jnp.float32,
+        )
+        target = send_ref if j & 1 else keep_ref
+        target[:, (j >> 1) * block:((j >> 1) + 1) * block] = out.astype(target.dtype)
+
+
+def local_small(
+    queries,
+    key_cache,
+    cached_value_rows,
+    lengths,
+    residual,
+    w_out,
+    norm_gain,
+    expert_ids,
+    route_weights,
+    w_gate,
+    w_up,
+    w_down,
+):
+    micro, per_micro, heads, width = queries.shape
+    rows = micro * per_micro
+    depth, columns = w_out.shape
+    experts, model, hidden = w_gate.shape
+    half = columns // 2
+    vmem = pl.BlockSpec(memory_space=pltpu.VMEM)
+    smem = pl.BlockSpec(memory_space=pltpu.SMEM)
+    wide, narrow = lax.axis_index("wide"), lax.axis_index("narrow")
+    where = jnp.stack([wide, narrow]).astype(jnp.int32)
+    size = lax.axis_size("wide")
+    turned = lax.ppermute(
+        residual.reshape(rows, columns),
+        ("wide", "narrow"),
+        [(i, (i % size) * size + i // size) for i in range(size * size)],
+    )
+    payload = pl.pallas_call(
+        attend_kernel,
+        out_shape=jax.ShapeDtypeStruct((rows, depth + 128), jnp.bfloat16),
+        in_specs=[smem] + [vmem] * 5,
+        out_specs=vmem,
+        scratch_shapes=[pltpu.VMEM((rows * heads, width), jnp.float32)],
+        compiler_params=pltpu.CompilerParams(vmem_limit_bytes=8 * 2**20),
+    )(
+        lengths,
+        queries.reshape(rows * heads, width),
+        key_cache.reshape(-1, width),
+        cached_value_rows.reshape(-1, width),
+        expert_ids.transpose(0, 2, 1),
+        route_weights.transpose(0, 2, 1),
+    )
+    others = [flip_permute(payload, "wide", s) for s in (1, 2, 3)]
+    keep, send = pl.pallas_call(
+        project_kernel,
+        out_shape=(
+            jax.ShapeDtypeStruct((size * rows, half), jnp.float32),
+            jax.ShapeDtypeStruct((size * rows, half), jnp.bfloat16),
+        ),
+        in_specs=[smem] + [vmem] * 6,
+        out_specs=(vmem, vmem),
+        compiler_params=pltpu.CompilerParams(vmem_limit_bytes=8 * 2**20),
+    )(where, payload, *others, w_out, turned)
+    part = (keep + flip_permute(send, "narrow", 1).astype(jnp.float32)).astype(jnp.bfloat16)
+    stream = (
+        part.astype(jnp.float32) + flip_permute(part, "narrow", 2).astype(jnp.float32)
+    ).astype(jnp.bfloat16)
+    mine = jnp.stack([stream] + [flip_permute(stream, "wide", s) for s in (1, 2, 3)])
+    other = flip_permute(mine, "narrow", 1)
+    weights = [
+        pltpu.with_memory_space_constraint(w, pltpu.VMEM)
+        for w in (w_gate, w_up, w_down.reshape(experts * hidden, model))
+    ]
+    keep, send, own = pl.pallas_call(
+        expert_kernel,
+        out_shape=(
+            jax.ShapeDtypeStruct((size * rows, model // 2), jnp.float32),
+            jax.ShapeDtypeStruct((size * rows, model // 2), jnp.bfloat16),
+            jax.ShapeDtypeStruct((rows, columns), jnp.bfloat16),
+        ),
+        in_specs=[smem] + [vmem] * 10,
+        out_specs=(vmem, vmem, vmem),
+        scratch_shapes=[
+            pltpu.VMEM((size * rows, model), jnp.bfloat16),
+            pltpu.VMEM((size * rows, experts * hidden), jnp.bfloat16),
+        ],
+        compiler_params=pltpu.CompilerParams(vmem_limit_bytes=12 * 2**20),
+    )(
+        where,
+        mine,
+        other,
+        *[p[:, depth:] for p in [payload] + others],
+        norm_gain.reshape(1, model),
+        *weights,
+    )
+    total = keep + flip_permute(send, "narrow", 1).astype(jnp.float32)
+    total = total.reshape(size, rows, model // 2)
+    leave = total[1:].astype(jnp.bfloat16)
+    summed = total[0]
+    for s in (1, 2, 3):
+        summed = summed + flip_permute(leave[s - 1], "wide", s).astype(jnp.float32)
+    cross = flip_permute(summed[:, columns:].astype(jnp.bfloat16), "narrow", 2)
+    result = own.astype(jnp.float32) + summed[:, :columns] + cross.astype(jnp.float32)
+    return result.astype(jnp.bfloat16).reshape(micro, per_micro, columns)
+
+
 def solution(mesh):
     in_specs = (
         P(None, ("grp", "wide"), "narrow", None),
@@ -162,4 +390,6 @@
         P("wide", "narrow", None),
     )
     out_specs = P(None, ("grp", "wide"), "narrow")
-    return jax.shard_map(local, mesh=mesh, in_specs=in_specs, out_specs=out_specs, check_vma=False)
+    small = mesh.shape["wide"] == 4 and mesh.shape["narrow"] == 4
+    body = local_small if small else local
+    return jax.shard_map(body, mesh=mesh, in_specs=in_specs, out_specs=out_specs, check_vma=False)

time: 232 us -> 90.9 us (0.39)
  matrix products: 64.3 us -> 0 us
  blocking collectives: 46.5 us -> 0 us
  Pallas kernels: 0 us -> 16.2 us
  waiting for transfers between devices: 37.9 us -> 23.6 us
  between operations: 13.4 us -> 0.1 us
  local copies, waits for them, and re-layouts: 36.9 us -> 26.7 us
  starting transfers between devices: 26.2 us -> 20.9 us
  other arithmetic: 5.3 us -> 2.68 us
    dot_general x14 -> x0, matrix products: 64.3 us -> none  [the longest x2 39.4 us: expert_block(): jnp.einsum('sjcf,jfnd->nsjcd', hidden, down_parts, preferred_element_type...]
    all_gather x4 -> x0, blocking collectives: 46.5 us -> none  [the longest x2 29 us: local(): lax.all_gather(attended[index_values], 'wide', axis=0, tiled=True)]
    reshape x7 -> x0, local copies, waits for them, and re-layouts: 29.8 us -> none  [the longest x1 27.8 us: expert_block(): w_down.reshape(local_experts, w_down.shape[1], narrow_count, model_width...]
    all_to_all x6 -> x0, starting transfers between devices: 25.9 us -> none  [the longest x2 9.63 us: expert_block(): lax.all_to_all(summed.astype(jnp.bfloat16), 'wide', split_axis=0, concat_...]
    unnamed x8 -> x26, local copies, waits for them, and re-layouts: 0.03 us -> 24.2 us
    ppermute x0 -> x15, waiting for transfers between devices: none -> 23.6 us  [the longest x14 23.6 us: flip_permute(): return lax.ppermute(value, axis, [(i, i ^ mask) for i in range(size)])]
    ppermute x0 -> x15, starting transfers between devices: none -> 20.9 us  [the longest x14 19.5 us: flip_permute(): return lax.ppermute(value, axis, [(i, i ^ mask) for i in range(size)])]
    all_to_all x6 -> x0, waiting for transfers between devices: 19 us -> none  [the longest x2 7.17 us: expert_block(): lax.all_to_all(summed.astype(jnp.bfloat16), 'wide', split_axis=0, concat_...]
  transfers between devices with their start and end apart: 9 -> 15, of which waited for: 4 -> 12; matrix products, arithmetic and copies ran while one was open for 29% -> 3% of each run, Pallas kernels for 0% -> 0%
where the time goes in v1:
time: 90.9 us; the launch traced here: 90.2 us
  local copies, waits for them, and re-layouts  26.7 us (29%)
  waiting for transfers between devices  23.6 us (26%)
  starting transfers between devices  20.9 us (23%)
  Pallas kernels  16.2 us (18%)
  other arithmetic  2.68 us (3%)
    unnamed x26, local copies, waits for them, and re-layouts  24.2 us
    ppermute x14, waiting for transfers between devices, flip_permute(): return lax.ppermute(value, axis, [(i, i ^ mask) for i in range(size)])  23.6 us
    ppermute x14, starting transfers between devices, flip_permute(): return lax.ppermute(value, axis, [(i, i ^ mask) for i in range(size)])  19.5 us
    pallas_call x1, Pallas kernels, local_small(): pl.pallas_call(expert_kernel, out_shape=(jax.ShapeDtypeStruct((size * row...  12.1 us
    pallas_call x1, Pallas kernels, local_small(): pl.pallas_call(attend_kernel, out_shape=jax.ShapeDtypeStruct((rows, depth...  3.24 us
    slice x4, local copies, waits for them, and re-layouts, local_small(): p[:, depth:]  2.43 us
  transfers between devices with their start and end apart: 15, of which 12 were waited for; matrix products, arithmetic and copies ran while one was open for 3% of the time, Pallas kernels for 0%

profile of v1, /device:TPU:0, one launch (start us, length us, event | category | flops | bytes accessed | tf_op | source)
XLA Modules:
  0.0 90.2 jit_solution(11133136278274271529)
XLA Ops:
  0.0 1.0 %copy-done.4 = bf16[2,16,64,1,128]{4,2,3,1,0:T(8,128)(2,1)S(1)} copy-done((bf16[2,16,64,1,128]{4,2,3,1,0:T(8,128)(2,1)S(1)}, bf16[2,16,64,1,128]{4,2,3,1,0:T(8,128)(2,1)}, u32[]{:S(2)}) %copy-start.4) | copy-done | bytes 524312
  1.0 1.0 %copy-done.5 = bf16[2,16,64,1,128]{4,2,3,1,0:T(8,128)(2,1)S(1)} copy-done((bf16[2,16,64,1,128]{4,2,3,1,0:T(8,128)(2,1)S(1)}, bf16[2,16,64,1,128]{4,2,3,1,0:T(8,128)(2,1)}, u32[]{:S(2)}) %copy-start.5) | copy-done | bytes 524312
  5.0 3.2 %shard_map.118.own_ref = bf16[32,1152]{1,0:T(8,128)(2,1)S(1)} custom-call(s32[2,16]{1,0:T(2,128)S(1)} %copy-done.10, bf16[256,128]{1,0:T(8,128)(2,1)S(1)} %bitcast.18, bf16[2048,128]{1,0:T(8,128)(2,1)S(1)} %bitcast.16, bf16[2048,128]{1,0:T(8,128)(2,1)S(1)} %bitcast.17, s32[2,8,16]{2,1,0:T(8,128)S(1)} %bitcast.19, f32[2,8,16]{2,1,0:T(8,128)S(1)} %bitcast.20), custom_call_target="tpu_custom_call" | custom-call | tf_op jit(solution)/shard_map/pallas_call | solution.py:308
  8.2 5.1 %collective-permute-start.2 = (bf16[32,1152]{1,0:T(8,128)(2,1)S(1)}, bf16[32,1152]{1,0:T(8,128)(2,1)S(1)}, u32[]{:S(2)}, u32[]{:S(2)}) collective-permute-start(bf16[32,1152]{1,0:T(8,128)(2,1)S(1)} %shard_map.118.own_ref), channel_id=1, source_target_pairs={{0,12},{4,8},{8,4},{12,0},{1,13},{5,9},{9,5},{13,1},{2,14},{6,10},... | collective-permute-start | bytes 221192 | tf_op jit(solution)/shard_map/ppermute | solution.py:153
  14.0 1.4 %collective-permute-start.3 = (bf16[32,512]{1,0:T(8,128)(2,1)}, bf16[32,512]{1,0:T(8,128)(2,1)S(1)}, u32[]{:S(2)}, u32[]{:S(2)}) collective-permute-start(bf16[32,512]{1,0:T(8,128)(2,1)} %bitcast.26), channel_id=1, source_target_pairs={{0,0},{1,4},{2,8},{3,12},{4,1},{5,5},{6,9},{7,13},{8,2},{9,6},{10,... | collective-permute-start | bytes 98312 | tf_op jit(solution)/shard_map/ppermute | solution.py:303
  16.1 3.5 %collective-permute-done.1.got2_ref = bf16[32,1152]{1,0:T(8,128)(2,1)S(1)} collective-permute-done((bf16[32,1152]{1,0:T(8,128)(2,1)S(1)}, bf16[32,1152]{1,0:T(8,128)(2,1)S(1)}, u32[]{:S(2)}, u32[]{:S(2)}) %collective-permute-start.1) | collective-permute-done | bytes 73760 | tf_op jit(solution)/shard_map/ppermute | solution.py:153
  19.6 1.2 %copy-done.3 = bf16[1024,512]{1,0:T(8,128)(2,1)S(1)} copy-done((bf16[1024,512]{1,0:T(8,128)(2,1)S(1)}, bf16[1024,512]{1,0:T(8,128)(2,1)}, u32[]{:S(2)}) %copy-start.3) | copy-done | bytes 1048600
  21.9 1.1 %collective-permute-done.4 = bf16[128,256]{1,0:T(8,128)(2,1)S(1)} collective-permute-done((bf16[128,256]{1,0:T(8,128)(2,1)S(1)}, bf16[128,256]{1,0:T(8,128)(2,1)S(1)}, u32[]{:S(2)}, u32[]{:S(2)}) %collective-permute-start.4) | collective-permute-done | bytes 65568 | tf_op jit(solution)/shard_map/ppermute | solution.py:153
  23.1 4.0 %collective-permute-start.5 = (bf16[128,256]{1,0:T(8,128)(2,1)S(1)}, bf16[128,256]{1,0:T(8,128)(2,1)S(1)}, u32[]{:S(2)}, u32[]{:S(2)}) collective-permute-start(bf16[128,256]{1,0:T(8,128)(2,1)S(1)} %add_convert_fusion.1), channel_id=1, source_target_pairs={{0,2},{1,3},{2,0},{3,1},{4,6},{5,7},{6,4},{7,5},{8,10},{9,11},{10,... | collective-permute-start | bytes 196616 | tf_op jit(solution)/shard_map/ppermute | solution.py:153
  27.1 2.4 %collective-permute-done.5 = bf16[128,256]{1,0:T(8,128)(2,1)S(1)} collective-permute-done((bf16[128,256]{1,0:T(8,128)(2,1)S(1)}, bf16[128,256]{1,0:T(8,128)(2,1)S(1)}, u32[]{:S(2)}, u32[]{:S(2)}) %collective-permute-start.5) | collective-permute-done | bytes 65568 | tf_op jit(solution)/shard_map/ppermute | solution.py:153
  29.5 4.2 %collective-permute-start.8 = (bf16[128,256]{1,0:T(8,128)(2,1)S(1)}, bf16[128,256]{1,0:T(8,128)(2,1)S(1)}, u32[]{:S(2)}, u32[]{:S(2)}) collective-permute-start(bf16[128,256]{1,0:T(8,128)(2,1)S(1)} %add_convert_fusion), channel_id=1, source_target_pairs={{0,12},{4,8},{8,4},{12,0},{1,13},{5,9},{9,5},{13,1},{2,14},{6,10},... | collective-permute-start | bytes 196616 | tf_op jit(solution)/shard_map/ppermute | solution.py:153
  34.4 1.7 %collective-permute-done.8 = bf16[128,256]{1,0:T(8,128)(2,1)S(1)} collective-permute-done((bf16[128,256]{1,0:T(8,128)(2,1)S(1)}, bf16[128,256]{1,0:T(8,128)(2,1)S(1)}, u32[]{:S(2)}, u32[]{:S(2)}) %collective-permute-start.8) | collective-permute-done | bytes 65568 | tf_op jit(solution)/shard_map/ppermute | solution.py:153
  36.1 2.9 %collective-permute-done.7 = bf16[128,256]{1,0:T(8,128)(2,1)S(1)} collective-permute-done((bf16[128,256]{1,0:T(8,128)(2,1)S(1)}, bf16[128,256]{1,0:T(8,128)(2,1)S(1)}, u32[]{:S(2)}, u32[]{:S(2)}) %collective-permute-start.7) | collective-permute-done | bytes 65568 | tf_op jit(solution)/shard_map/ppermute | solution.py:153
  42.4 5.8 %copy-done = bf16[16,2048,256]{2,1,0:T(8,128)(2,1)S(1)} copy-done((bf16[16,2048,256]{2,1,0:T(8,128)(2,1)S(1)}, bf16[16,2048,256]{2,1,0:T(8,128)(2,1)}, u32[]{:S(2)}) %copy-start) | copy-done | bytes 16777240
  48.2 5.8 %copy-done.1 = bf16[16,2048,256]{2,1,0:T(8,128)(2,1)S(1)} copy-done((bf16[16,2048,256]{2,1,0:T(8,128)(2,1)S(1)}, bf16[16,2048,256]{2,1,0:T(8,128)(2,1)}, u32[]{:S(2)}) %copy-start.1) | copy-done | bytes 16777240
  53.9 5.8 %copy-done.2 = bf16[16,256,2048]{2,1,0:T(8,128)(2,1)S(1)} copy-done((bf16[16,256,2048]{2,1,0:T(8,128)(2,1)S(1)}, bf16[16,256,2048]{2,1,0:T(8,128)(2,1)}, u32[]{:S(2)}) %copy-start.2) | copy-done | bytes 16777240
  59.7 12.1 %shard_map.120 = (f32[128,1024]{1,0:T(8,128)}, bf16[128,1024]{1,0:T(8,128)(2,1)}, bf16[32,512]{1,0:T(8,128)(2,1)}) custom-call(s32[2]{0:T(128)} %copy-done.9, bf16[4,128,256]{2,1,0:T(8,128)(2,1)} %copy-done.11, bf16[4,128,256]{2,1,0:T(8,128)(2,1)} %copy-done.12, bf16[32,128]{1,0:T(8,128)(2,1)} %slice.51.cw0_ref, bf16[32,128]{1,0:T(8,128)(2,1)} %slice.52.cw1_ref, ...), custom_call_target="tpu_custom_call" | custom-call | tf_op jit(solution)/shard_map/pallas_call | solution.py:344
  72.3 1.4 %collective-permute-done.10 = bf16[128,1024]{1,0:T(8,128)(2,1)S(1)} collective-permute-done((bf16[128,1024]{1,0:T(8,128)(2,1)}, bf16[128,1024]{1,0:T(8,128)(2,1)S(1)}, u32[]{:S(2)}, u32[]{:S(2)}) %collective-permute-start.10) | collective-permute-done | bytes 262176 | tf_op jit(solution)/shard_map/ppermute | solution.py:153
  73.6 1.1 %fusion.4 = (bf16[128,1024]{1,0:T(8,128)(2,1)S(1)}, f32[128,1024]{1,0:T(8,128)S(1)}) fusion(f32[128,1024]{1,0:T(8,128)} %get-tuple-element.13, bf16[128,1024]{1,0:T(8,128)(2,1)S(1)} %collective-permute-done.10), kind=kLoop, calls=%fused_computation.12 | loop fusion | flops 393216 | bytes 1572864 | tf_op jit(solution)/shard_map/convert.1
  75.4 2.8 %collective-permute-start.13 = (bf16[32,1024]{1,0:T(8,128)(2,1)S(1)}, bf16[32,1024]{1,0:T(8,128)(2,1)S(1)}, u32[]{:S(2)}, u32[]{:S(2)}) collective-permute-start(bf16[32,1024]{1,0:T(8,128)(2,1)S(1)} %get-tuple-element.18), channel_id=1, source_target_pairs={{0,12},{4,8},{8,4},{12,0},{1,13},{5,9},{9,5},{13,1},{2,14},{6,10},... | collective-permute-start | bytes 196616 | tf_op jit(solution)/shard_map/ppermute | solution.py:153
  79.2 3.3 %collective-permute-done.13 = bf16[32,1024]{1,0:T(8,128)(2,1)S(1)} collective-permute-done((bf16[32,1024]{1,0:T(8,128)(2,1)S(1)}, bf16[32,1024]{1,0:T(8,128)(2,1)S(1)}, u32[]{:S(2)}, u32[]{:S(2)}) %collective-permute-start.13) | collective-permute-done | bytes 65568 | tf_op jit(solution)/shard_map/ppermute | solution.py:153
  82.6 2.2 %collective-permute-done.12 = bf16[32,1024]{1,0:T(8,128)(2,1)S(1)} collective-permute-done((bf16[32,1024]{1,0:T(8,128)(2,1)S(1)}, bf16[32,1024]{1,0:T(8,128)(2,1)S(1)}, u32[]{:S(2)}, u32[]{:S(2)}) %collective-permute-start.12) | collective-permute-done | bytes 65568 | tf_op jit(solution)/shard_map/ppermute | solution.py:153
  85.4 3.4 %collective-permute-done.14 = bf16[32,512]{1,0:T(8,128)(2,1)S(1)} collective-permute-done((bf16[32,512]{1,0:T(8,128)(2,1)S(1)}, bf16[32,512]{1,0:T(8,128)(2,1)S(1)}, u32[]{:S(2)}, u32[]{:S(2)}) %collective-permute-start.14) | collective-permute-done | bytes 32800 | tf_op jit(solution)/shard_map/ppermute | solution.py:153
  88.8 1.4 %fusion.3 = bf16[32,512]{1,0:T(8,128)(2,1)} fusion(f32[32,1024]{1,0:T(8,128)S(1)} %fusion.1, bf16[32,512]{1,0:T(8,128)(2,1)S(1)} %collective-permute-done.14, bf16[32,512]{1,0:T(8,128)(2,1)} %get-tuple-element.12), kind=kLoop, calls=%fused_computation.10 | loop fusion | flops 81920 | bytes 163840 | tf_op jit(solution)/shard_map/convert_element_type | solution.py:374
  (48 shorter events, 12.1 us)
Async XLA Ops:
  0.0 1.0 %copy-start.4 = (bf16[2,16,64,1,128]{4,2,3,1,0:T(8,128)(2,1)S(1)}, bf16[2,16,64,1,128]{4,2,3,1,0:T(8,128)(2,1)}, u32[]{:S(2)}) copy-start(bf16[2,16,64,1,128]{4,2,3,1,0:T(8,128)(2,1)} %param.13) | copy-start | bytes 1572868
  1.0 1.0 %copy-start.5 = (bf16[2,16,64,1,128]{4,2,3,1,0:T(8,128)(2,1)S(1)}, bf16[2,16,64,1,128]{4,2,3,1,0:T(8,128)(2,1)}, u32[]{:S(2)}) copy-start(bf16[2,16,64,1,128]{4,2,3,1,0:T(8,128)(2,1)} %param.14) | copy-start | bytes 1572868
  2.1 0.8 copy-start.6
  8.2 7.9 %collective-permute-start.2 = (bf16[32,1152]{1,0:T(8,128)(2,1)S(1)}, bf16[32,1152]{1,0:T(8,128)(2,1)S(1)}, u32[]{:S(2)}, u32[]{:S(2)}) collective-permute-start(bf16[32,1152]{1,0:T(8,128)(2,1)S(1)} %shard_map.118.own_ref), channel_id=1, source_target_pairs={{0,12},{4,8},{8,4},{12,0},{1,13},{5,9},{9,5},{13,1},{2,14},{6,10},... | collective-permute-start | bytes 221192 | tf_op jit(solution)/shard_map/ppermute | solution.py:153
  13.3 6.3 %collective-permute-start.1 = (bf16[32,1152]{1,0:T(8,128)(2,1)S(1)}, bf16[32,1152]{1,0:T(8,128)(2,1)S(1)}, u32[]{:S(2)}, u32[]{:S(2)}) collective-permute-start(bf16[32,1152]{1,0:T(8,128)(2,1)S(1)} %shard_map.118.own_ref), channel_id=1, source_target_pairs={{0,8},{4,12},{8,0},{12,4},{1,9},{5,13},{9,1},{13,5},{2,10},{6,14},... | collective-permute-start | bytes 221192 | tf_op jit(solution)/shard_map/ppermute | solution.py:153
  13.3 6.3 %collective-permute-start = (bf16[32,1152]{1,0:T(8,128)(2,1)S(1)}, bf16[32,1152]{1,0:T(8,128)(2,1)S(1)}, u32[]{:S(2)}, u32[]{:S(2)}) collective-permute-start(bf16[32,1152]{1,0:T(8,128)(2,1)S(1)} %shard_map.118.own_ref), channel_id=1, source_target_pairs={{0,4},{4,0},{8,12},{12,8},{1,5},{5,1},{9,13},{13,9},{2,6},{6,2},{1... | collective-permute-start | bytes 221192 | tf_op jit(solution)/shard_map/ppermute | solution.py:153
  14.0 1.5 %collective-permute-start.3 = (bf16[32,512]{1,0:T(8,128)(2,1)}, bf16[32,512]{1,0:T(8,128)(2,1)S(1)}, u32[]{:S(2)}, u32[]{:S(2)}) collective-permute-start(bf16[32,512]{1,0:T(8,128)(2,1)} %bitcast.26), channel_id=1, source_target_pairs={{0,0},{1,4},{2,8},{3,12},{4,1},{5,5},{6,9},{7,13},{8,2},{9,6},{10,... | collective-permute-start | bytes 98312 | tf_op jit(solution)/shard_map/ppermute | solution.py:303
  15.5 26.2 %copy-start.9 = (s32[2]{0:T(128)}, s32[2]{0:T(128)S(1)}, u32[]{:S(2)}) copy-start(s32[2]{0:T(128)S(1)} %pad_add_fusion.where_ref) | copy-start | bytes 28
  19.6 1.2 %copy-start.3 = (bf16[1024,512]{1,0:T(8,128)(2,1)S(1)}, bf16[1024,512]{1,0:T(8,128)(2,1)}, u32[]{:S(2)}) copy-start(bf16[1024,512]{1,0:T(8,128)(2,1)} %w_ref.1) | copy-start | bytes 3145732
  21.7 1.3 %collective-permute-start.4 = (bf16[128,256]{1,0:T(8,128)(2,1)S(1)}, bf16[128,256]{1,0:T(8,128)(2,1)S(1)}, u32[]{:S(2)}, u32[]{:S(2)}) collective-permute-start(bf16[128,256]{1,0:T(8,128)(2,1)S(1)} %get-tuple-element.11), channel_id=1, source_target_pairs={{0,1},{1,0},{2,3},{3,2},{4,5},{5,4},{6,7},{7,6},{8,9},{9,8},{10,11... | collective-permute-start | bytes 196616 | tf_op jit(solution)/shard_map/ppermute | solution.py:153
  23.1 6.4 %collective-permute-start.5 = (bf16[128,256]{1,0:T(8,128)(2,1)S(1)}, bf16[128,256]{1,0:T(8,128)(2,1)S(1)}, u32[]{:S(2)}, u32[]{:S(2)}) collective-permute-start(bf16[128,256]{1,0:T(8,128)(2,1)S(1)} %add_convert_fusion.1), channel_id=1, source_target_pairs={{0,2},{1,3},{2,0},{3,1},{4,6},{5,7},{6,4},{7,5},{8,10},{9,11},{10,... | collective-permute-start | bytes 196616 | tf_op jit(solution)/shard_map/ppermute | solution.py:153
  29.5 6.6 %collective-permute-start.8 = (bf16[128,256]{1,0:T(8,128)(2,1)S(1)}, bf16[128,256]{1,0:T(8,128)(2,1)S(1)}, u32[]{:S(2)}, u32[]{:S(2)}) collective-permute-start(bf16[128,256]{1,0:T(8,128)(2,1)S(1)} %add_convert_fusion), channel_id=1, source_target_pairs={{0,12},{4,8},{8,4},{12,0},{1,13},{5,9},{9,5},{13,1},{2,14},{6,10},... | collective-permute-start | bytes 196616 | tf_op jit(solution)/shard_map/ppermute | solution.py:153
  33.7 5.3 %collective-permute-start.7 = (bf16[128,256]{1,0:T(8,128)(2,1)S(1)}, bf16[128,256]{1,0:T(8,128)(2,1)S(1)}, u32[]{:S(2)}, u32[]{:S(2)}) collective-permute-start(bf16[128,256]{1,0:T(8,128)(2,1)S(1)} %add_convert_fusion), channel_id=1, source_target_pairs={{0,8},{4,12},{8,0},{12,4},{1,9},{5,13},{9,1},{13,5},{2,10},{6,14},... | collective-permute-start | bytes 196616 | tf_op jit(solution)/shard_map/ppermute | solution.py:153
  33.7 5.4 %collective-permute-start.6 = (bf16[128,256]{1,0:T(8,128)(2,1)S(1)}, bf16[128,256]{1,0:T(8,128)(2,1)S(1)}, u32[]{:S(2)}, u32[]{:S(2)}) collective-permute-start(bf16[128,256]{1,0:T(8,128)(2,1)S(1)} %add_convert_fusion), channel_id=1, source_target_pairs={{0,4},{4,0},{8,12},{12,8},{1,5},{5,1},{9,13},{13,9},{2,6},{6,2},{1... | collective-permute-start | bytes 196616 | tf_op jit(solution)/shard_map/ppermute | solution.py:153
  39.1 2.5 %copy-start.11 = (bf16[4,128,256]{2,1,0:T(8,128)(2,1)}, bf16[4,128,256]{2,1,0:T(8,128)(2,1)S(1)}, u32[]{:S(2)}) copy-start(bf16[4,128,256]{2,1,0:T(8,128)(2,1)S(1)} %pad_maximum_fusion.mine_ref) | copy-start | bytes 786436
  39.2 2.5 %collective-permute-start.9 = (bf16[4,128,256]{2,1,0:T(8,128)(2,1)S(1)}, bf16[4,128,256]{2,1,0:T(8,128)(2,1)S(1)}, u32[]{:S(2)}, u32[]{:S(2)}) collective-permute-start(bf16[4,128,256]{2,1,0:T(8,128)(2,1)S(1)} %pad_maximum_fusion.mine_ref), channel_id=1, source_target_pairs={{0,1},{1,0},{2,3},{3,2},{4,5},{5,4},{6,7},{7,6},{8,9},{9,8},{10,11... | collective-permute-start | bytes 786440 | tf_op jit(solution)/shard_map/ppermute | solution.py:153
  42.4 5.8 %copy-start = (bf16[16,2048,256]{2,1,0:T(8,128)(2,1)S(1)}, bf16[16,2048,256]{2,1,0:T(8,128)(2,1)}, u32[]{:S(2)}) copy-start(bf16[16,2048,256]{2,1,0:T(8,128)(2,1)} %wg_ref.1) | copy-start | bytes 50331652
  48.2 5.8 %copy-start.1 = (bf16[16,2048,256]{2,1,0:T(8,128)(2,1)S(1)}, bf16[16,2048,256]{2,1,0:T(8,128)(2,1)}, u32[]{:S(2)}) copy-start(bf16[16,2048,256]{2,1,0:T(8,128)(2,1)} %wu_ref.1) | copy-start | bytes 50331652
  53.9 5.8 %copy-start.2 = (bf16[16,256,2048]{2,1,0:T(8,128)(2,1)S(1)}, bf16[16,256,2048]{2,1,0:T(8,128)(2,1)}, u32[]{:S(2)}) copy-start(bf16[16,256,2048]{2,1,0:T(8,128)(2,1)} %param.23) | copy-start | bytes 50331652
  71.8 1.8 %collective-permute-start.10 = (bf16[128,1024]{1,0:T(8,128)(2,1)}, bf16[128,1024]{1,0:T(8,128)(2,1)S(1)}, u32[]{:S(2)}, u32[]{:S(2)}) collective-permute-start(bf16[128,1024]{1,0:T(8,128)(2,1)} %get-tuple-element.14), channel_id=1, source_target_pairs={{0,1},{1,0},{2,3},{3,2},{4,5},{5,4},{6,7},{7,6},{8,9},{9,8},{10,11... | collective-permute-start | bytes 786440 | tf_op jit(solution)/shard_map/ppermute | solution.py:153
  74.8 4.4 %collective-permute-start.11 = (bf16[32,1024]{1,0:T(8,128)(2,1)S(1)}, bf16[32,1024]{1,0:T(8,128)(2,1)S(1)}, u32[]{:S(2)}, u32[]{:S(2)}) collective-permute-start(bf16[32,1024]{1,0:T(8,128)(2,1)S(1)} %get-tuple-element.17), channel_id=1, source_target_pairs={{0,4},{4,0},{8,12},{12,8},{1,5},{5,1},{9,13},{13,9},{2,6},{6,2},{1... | collective-permute-start | bytes 196616 | tf_op jit(solution)/shard_map/ppermute | solution.py:153
  75.4 7.1 %collective-permute-start.13 = (bf16[32,1024]{1,0:T(8,128)(2,1)S(1)}, bf16[32,1024]{1,0:T(8,128)(2,1)S(1)}, u32[]{:S(2)}, u32[]{:S(2)}) collective-permute-start(bf16[32,1024]{1,0:T(8,128)(2,1)S(1)} %get-tuple-element.18), channel_id=1, source_target_pairs={{0,12},{4,8},{8,4},{12,0},{1,13},{5,9},{9,5},{13,1},{2,14},{6,10},... | collective-permute-start | bytes 196616 | tf_op jit(solution)/shard_map/ppermute | solution.py:153
  78.2 6.6 %collective-permute-start.12 = (bf16[32,1024]{1,0:T(8,128)(2,1)S(1)}, bf16[32,1024]{1,0:T(8,128)(2,1)S(1)}, u32[]{:S(2)}, u32[]{:S(2)}) collective-permute-start(bf16[32,1024]{1,0:T(8,128)(2,1)S(1)} %get-tuple-element.19), channel_id=1, source_target_pairs={{0,8},{4,12},{8,0},{12,4},{1,9},{5,13},{9,1},{13,5},{2,10},{6,14},... | collective-permute-start | bytes 196616 | tf_op jit(solution)/shard_map/ppermute | solution.py:153
  84.8 4.0 %collective-permute-start.14 = (bf16[32,512]{1,0:T(8,128)(2,1)S(1)}, bf16[32,512]{1,0:T(8,128)(2,1)S(1)}, u32[]{:S(2)}, u32[]{:S(2)}) collective-permute-start(bf16[32,512]{1,0:T(8,128)(2,1)S(1)} %slice.72), channel_id=1, source_target_pairs={{0,2},{1,3},{2,0},{3,1},{4,6},{5,7},{6,4},{7,5},{8,10},{9,11},{10,... | collective-permute-start | bytes 98312 | tf_op jit(solution)/shard_map/ppermute | solution.py:153
  (4 other events, 2.8 us)

commit v2 on v1

--- a/solution.py
+++ b/solution.py
@@ -153,7 +153,17 @@
     return lax.ppermute(value, axis, [(i, i ^ mask) for i in range(size)])
 
 
-def attend_kernel(len_ref, q_ref, k_ref, v_ref, ids_ref, wts_ref, out_ref, mixed_ref):
+def attend_kernel(*refs):
+    given, out_ref, mixed_ref, held, sems = refs[:6], refs[6], refs[7], refs[8:14], refs[14]
+    copies = [
+        pltpu.make_async_copy(source, target, sems.at[i])
+        for i, (source, target) in enumerate(zip(given, held))
+    ]
+    for copy in copies:
+        copy.start()
+    for copy in copies:
+        copy.wait()
+    len_ref, q_ref, k_ref, v_ref, ids_ref, wts_ref = held
     rows, heads = out_ref.shape[0], q_ref.shape[0] // out_ref.shape[0]
     width = q_ref.shape[1]
     slots = k_ref.shape[0] // rows
@@ -252,7 +262,7 @@
         x_ref[:, cols] = (
             x_ref[:, cols].astype(jnp.float32) * scale * gain_ref[:, cols]
         ).astype(jnp.bfloat16)
-    mix = jnp.concatenate([r[...] for r in (cw0_ref, cw1_ref, cw2_ref, cw3_ref)], axis=0)
+    mix = jnp.concatenate([r[:, -128:] for r in (cw0_ref, cw1_ref, cw2_ref, cw3_ref)], axis=0)
     lane = lax.broadcasted_iota(jnp.int32, (mix.shape[1], width), 0) % (mix.shape[1] // 2)
 
     def one(e, carry):
@@ -305,14 +315,7 @@
         ("wide", "narrow"),
         [(i, (i % size) * size + i // size) for i in range(size * size)],
     )
-    payload = pl.pallas_call(
-        attend_kernel,
-        out_shape=jax.ShapeDtypeStruct((rows, depth + 128), jnp.bfloat16),
-        in_specs=[smem] + [vmem] * 5,
-        out_specs=vmem,
-        scratch_shapes=[pltpu.VMEM((rows * heads, width), jnp.float32)],
-        compiler_params=pltpu.CompilerParams(vmem_limit_bytes=8 * 2**20),
-    )(
+    given = (
         lengths,
         queries.reshape(rows * heads, width),
         key_cache.reshape(-1, width),
@@ -320,6 +323,18 @@
         expert_ids.transpose(0, 2, 1),
         route_weights.transpose(0, 2, 1),
     )
+    payload = pl.pallas_call(
+        attend_kernel,
+        out_shape=jax.ShapeDtypeStruct((rows, depth + 128), jnp.bfloat16),
+        in_specs=[pl.BlockSpec(memory_space=pl.ANY)] * 6,
+        out_specs=vmem,
+        scratch_shapes=[pltpu.VMEM((rows * heads, width), jnp.float32)]
+        + [pltpu.SMEM(given[0].shape, given[0].dtype)]
+        + [pltpu.VMEM(g.shape, g.dtype) for g in given[1:]]
+        + [pltpu.SemaphoreType.DMA((6,))],
+        cost_estimate=pl.CostEstimate(flops=2 * 10**10, bytes_accessed=10**8, transcendentals=0),
+        compiler_params=pltpu.CompilerParams(vmem_limit_bytes=6 * 2**20),
+    )(*[pltpu.with_memory_space_constraint(g, pltpu.HBM) for g in given])
     others = [flip_permute(payload, "wide", s) for s in (1, 2, 3)]
     keep, send = pl.pallas_call(
         project_kernel,
@@ -329,7 +344,8 @@
         ),
         in_specs=[smem] + [vmem] * 6,
         out_specs=(vmem, vmem),
-        compiler_params=pltpu.CompilerParams(vmem_limit_bytes=8 * 2**20),
+        cost_estimate=pl.CostEstimate(flops=2 * 10**10, bytes_accessed=10**8, transcendentals=0),
+        compiler_params=pltpu.CompilerParams(vmem_limit_bytes=6 * 2**20),
     )(where, payload, *others, w_out, turned)
     part = (keep + flip_permute(send, "narrow", 1).astype(jnp.float32)).astype(jnp.bfloat16)
     stream = (
@@ -359,7 +375,8 @@
         where,
         mine,
         other,
-        *[p[:, depth:] for p in [payload] + others],
+        payload,
+        *others,
         norm_gain.reshape(1, model),
         *weights,
     )

time: 90.9 us -> 66.7 us (0.73)
  local copies, waits for them, and re-layouts: 26.7 us -> 0.82 us
  waiting for transfers between devices: 23.6 us -> 25.7 us
  starting transfers between devices: 20.9 us -> 19.7 us
  Pallas kernels: 16.2 us -> 17.2 us
    unnamed x26 -> x42, local copies, waits for them, and re-layouts: 24.2 us -> 0.8 us
    slice x4 -> x0, local copies, waits for them, and re-layouts: 2.43 us -> none  [local_small(): p[:, depth:]]
    ppermute x14, waiting for transfers between devices: 23.6 us -> 25.7 us  [flip_permute(): return lax.ppermute(value, axis, [(i, i ^ mask) for i in range(size)])]
  transfers between devices with their start and end apart: 15 -> 15, of which waited for: 12 -> 13; matrix products, arithmetic and copies ran while one was open for 3% -> 0% of each run, Pallas kernels for 0% -> 0%
where the time goes in v2:
time: 66.7 us; the launch traced here: 66.5 us
  waiting for transfers between devices  25.7 us (39%)
  starting transfers between devices  19.7 us (30%)
  Pallas kernels  17.2 us (26%)
  other arithmetic  2.68 us (4%)
  local copies, waits for them, and re-layouts  0.82 us (1%)
    ppermute x14, waiting for transfers between devices, flip_permute(): return lax.ppermute(value, axis, [(i, i ^ mask) for i in range(size)])  25.7 us
    ppermute x14, starting transfers between devices, flip_permute(): return lax.ppermute(value, axis, [(i, i ^ mask) for i in range(size)])  19.1 us
    pallas_call x1, Pallas kernels, local_small(): pl.pallas_call(expert_kernel, out_shape=(jax.ShapeDtypeStruct((size * row...  12.2 us
    pallas_call x1, Pallas kernels, local_small(): pl.pallas_call(attend_kernel, out_shape=jax.ShapeDtypeStruct((rows, depth...  4.09 us
    convert_element_type x1, other arithmetic, local_small(): return result.astype(jnp.bfloat16).reshape(micro, per_micro, columns)  1.39 us
  transfers between devices with their start and end apart: 15, of which 13 were waited for; matrix products, arithmetic and copies ran while one was open for 0% of the time, Pallas kernels for 0%

profile of v2, /device:TPU:0, one launch (start us, length us, event | category | flops | bytes accessed | tf_op | source)
XLA Modules:
  0.0 66.5 jit_solution(18368820544592356023)
XLA Ops:
  0.0 4.1 %shard_map.118.own_ref.cw0_ref = bf16[32,1152]{1,0:T(8,128)(2,1)S(1)} custom-call(s32[2,16]{1,0:T(2,128)} %refs_0_.1, bf16[256,128]{1,0:T(8,128)(2,1)} %bitcast.29, bf16[2048,128]{1,0:T(8,128)(2,1)} %bitcast.27, bf16[2048,128]{1,0:T(8,128)(2,1)} %bitcast.28, s32[2,8,16]{2,1,0:T(8,128)} %bitcast.31, f32[2,8,16]{2,1,0:T(8,128)} %bitcast.32), custom_call_target="tpu_custom_call" | custom-call | flops 20000000000 | bytes 100000000 | tf_op jit(solution)/shard_map/pallas_call | solution.py:326
  4.1 5.1 %collective-permute-start.2 = (bf16[32,1152]{1,0:T(8,128)(2,1)S(1)}, bf16[32,1152]{1,0:T(8,128)(2,1)S(1)}, u32[]{:S(2)}, u32[]{:S(2)}) collective-permute-start(bf16[32,1152]{1,0:T(8,128)(2,1)S(1)} %shard_map.118.own_ref.cw0_ref), channel_id=1, source_target_pairs={{0,12},{4,8},{8,4},{12,0},{1,13},{5,9},{9,5},{13,1},{2,14},{6,10},... | collective-permute-start | bytes 221192 | tf_op jit(solution)/shard_map/ppermute | solution.py:153
  9.9 0.7 collective-permute-start.3
  10.7 1.2 %collective-permute-done.2.got3_ref.cw3_ref = bf16[32,1152]{1,0:T(8,128)(2,1)S(1)} collective-permute-done((bf16[32,1152]{1,0:T(8,128)(2,1)S(1)}, bf16[32,1152]{1,0:T(8,128)(2,1)S(1)}, u32[]{:S(2)}, u32[]{:S(2)}) %collective-permute-start.2) | collective-permute-done | bytes 73760 | tf_op jit(solution)/shard_map/ppermute | solution.py:153
  12.0 3.5 %collective-permute-done.1.got2_ref.cw2_ref = bf16[32,1152]{1,0:T(8,128)(2,1)S(1)} collective-permute-done((bf16[32,1152]{1,0:T(8,128)(2,1)S(1)}, bf16[32,1152]{1,0:T(8,128)(2,1)S(1)}, u32[]{:S(2)}, u32[]{:S(2)}) %collective-permute-start.1) | collective-permute-done | bytes 73760 | tf_op jit(solution)/shard_map/ppermute | solution.py:153
  15.6 0.9 %shard_map.119 = (f32[128,256]{1,0:T(8,128)S(1)}, bf16[128,256]{1,0:T(8,128)(2,1)S(1)}) custom-call(s32[2]{0:T(128)S(1)} %pad_add_fusion.where_ref, bf16[32,1152]{1,0:T(8,128)(2,1)S(1)} %shard_map.118.own_ref.cw0_ref, bf16[32,1152]{1,0:T(8,128)(2,1)S(1)} %collective-permute-done.got1_ref.cw1_ref, ...), custom_call_target="tpu_custom_call" | custom-call | flops 20000000000 | bytes 100000000 | tf_op jit(solution)/shard_map/pallas_call | solution.py:339
  16.7 1.1 %collective-permute-done.4 = bf16[128,256]{1,0:T(8,128)(2,1)S(1)} collective-permute-done((bf16[128,256]{1,0:T(8,128)(2,1)S(1)}, bf16[128,256]{1,0:T(8,128)(2,1)S(1)}, u32[]{:S(2)}, u32[]{:S(2)}) %collective-permute-start.4) | collective-permute-done | bytes 65568 | tf_op jit(solution)/shard_map/ppermute | solution.py:153
  17.8 3.8 %collective-permute-start.5 = (bf16[128,256]{1,0:T(8,128)(2,1)S(1)}, bf16[128,256]{1,0:T(8,128)(2,1)S(1)}, u32[]{:S(2)}, u32[]{:S(2)}) collective-permute-start(bf16[128,256]{1,0:T(8,128)(2,1)S(1)} %add_convert_fusion.1), channel_id=1, source_target_pairs={{0,2},{1,3},{2,0},{3,1},{4,6},{5,7},{6,4},{7,5},{8,10},{9,11},{10,... | collective-permute-start | bytes 196616 | tf_op jit(solution)/shard_map/ppermute | solution.py:153
  21.6 2.4 %collective-permute-done.5 = bf16[128,256]{1,0:T(8,128)(2,1)S(1)} collective-permute-done((bf16[128,256]{1,0:T(8,128)(2,1)S(1)}, bf16[128,256]{1,0:T(8,128)(2,1)S(1)}, u32[]{:S(2)}, u32[]{:S(2)}) %collective-permute-start.5) | collective-permute-done | bytes 65568 | tf_op jit(solution)/shard_map/ppermute | solution.py:153
  24.0 4.2 %collective-permute-start.8 = (bf16[128,256]{1,0:T(8,128)(2,1)S(1)}, bf16[128,256]{1,0:T(8,128)(2,1)S(1)}, u32[]{:S(2)}, u32[]{:S(2)}) collective-permute-start(bf16[128,256]{1,0:T(8,128)(2,1)S(1)} %add_convert_fusion), channel_id=1, source_target_pairs={{0,12},{4,8},{8,4},{12,0},{1,13},{5,9},{9,5},{13,1},{2,14},{6,10},... | collective-permute-start | bytes 196616 | tf_op jit(solution)/shard_map/ppermute | solution.py:153
  28.9 1.7 %collective-permute-done.8 = bf16[128,256]{1,0:T(8,128)(2,1)S(1)} collective-permute-done((bf16[128,256]{1,0:T(8,128)(2,1)S(1)}, bf16[128,256]{1,0:T(8,128)(2,1)S(1)}, u32[]{:S(2)}, u32[]{:S(2)}) %collective-permute-start.8) | collective-permute-done | bytes 65568 | tf_op jit(solution)/shard_map/ppermute | solution.py:153
  30.6 2.9 %collective-permute-done.7 = bf16[128,256]{1,0:T(8,128)(2,1)S(1)} collective-permute-done((bf16[128,256]{1,0:T(8,128)(2,1)S(1)}, bf16[128,256]{1,0:T(8,128)(2,1)S(1)}, u32[]{:S(2)}, u32[]{:S(2)}) %collective-permute-start.7) | collective-permute-done | bytes 65568 | tf_op jit(solution)/shard_map/ppermute | solution.py:153
  33.8 1.5 %collective-permute-done.9.other_ref = bf16[4,128,256]{2,1,0:T(8,128)(2,1)S(1)} collective-permute-done((bf16[4,128,256]{2,1,0:T(8,128)(2,1)S(1)}, bf16[4,128,256]{2,1,0:T(8,128)(2,1)S(1)}, u32[]{:S(2)}, u32[]{:S(2)}) %collective-permute-start.9) | collective-permute-done | bytes 262176 | tf_op jit(solution)/shard_map/ppermute | solution.py:153
  35.3 0.7 %copy-done.7 = bf16[4,128,256]{2,1,0:T(8,128)(2,1)} copy-done((bf16[4,128,256]{2,1,0:T(8,128)(2,1)}, bf16[4,128,256]{2,1,0:T(8,128)(2,1)S(1)}, u32[]{:S(2)}) %copy-start.7) | copy-done | bytes 262168
  36.1 12.2 %shard_map.120 = (f32[128,1024]{1,0:T(8,128)}, bf16[128,1024]{1,0:T(8,128)(2,1)}, bf16[32,512]{1,0:T(8,128)(2,1)}) custom-call(s32[2]{0:T(128)} %copy-done.4, bf16[4,128,256]{2,1,0:T(8,128)(2,1)} %copy-done.6, bf16[4,128,256]{2,1,0:T(8,128)(2,1)} %copy-done.7, bf16[32,1152]{1,0:T(8,128)(2,1)} %copy-done, bf16[32,1152]{1,0:T(8,128)(2,1)} %copy-done.3, ...), custom_call_target="tpu_custom_call" | custom-call | tf_op jit(solution)/shard_map/pallas_call | solution.py:360
  48.5 1.6 %collective-permute-done.10 = bf16[128,1024]{1,0:T(8,128)(2,1)S(1)} collective-permute-done((bf16[128,1024]{1,0:T(8,128)(2,1)}, bf16[128,1024]{1,0:T(8,128)(2,1)S(1)}, u32[]{:S(2)}, u32[]{:S(2)}) %collective-permute-start.10) | collective-permute-done | bytes 262176 | tf_op jit(solution)/shard_map/ppermute | solution.py:153
  50.1 1.1 %fusion.4 = (bf16[128,1024]{1,0:T(8,128)(2,1)S(1)}, f32[128,1024]{1,0:T(8,128)S(1)}) fusion(f32[128,1024]{1,0:T(8,128)} %get-tuple-element.13, bf16[128,1024]{1,0:T(8,128)(2,1)S(1)} %collective-permute-done.10), kind=kLoop, calls=%fused_computation.12 | loop fusion | flops 393216 | bytes 1572864 | tf_op jit(solution)/shard_map/convert.1
  51.8 2.8 %collective-permute-start.13 = (bf16[32,1024]{1,0:T(8,128)(2,1)S(1)}, bf16[32,1024]{1,0:T(8,128)(2,1)S(1)}, u32[]{:S(2)}, u32[]{:S(2)}) collective-permute-start(bf16[32,1024]{1,0:T(8,128)(2,1)S(1)} %get-tuple-element.18), channel_id=1, source_target_pairs={{0,12},{4,8},{8,4},{12,0},{1,13},{5,9},{9,5},{13,1},{2,14},{6,10},... | collective-permute-start | bytes 196616 | tf_op jit(solution)/shard_map/ppermute | solution.py:153
  54.8 0.8 %collective-permute-done.11 = bf16[32,1024]{1,0:T(8,128)(2,1)S(1)} collective-permute-done((bf16[32,1024]{1,0:T(8,128)(2,1)S(1)}, bf16[32,1024]{1,0:T(8,128)(2,1)S(1)}, u32[]{:S(2)}, u32[]{:S(2)}) %collective-permute-start.11) | collective-permute-done | bytes 65568 | tf_op jit(solution)/shard_map/ppermute | solution.py:153
  55.5 3.4 %collective-permute-done.13 = bf16[32,1024]{1,0:T(8,128)(2,1)S(1)} collective-permute-done((bf16[32,1024]{1,0:T(8,128)(2,1)S(1)}, bf16[32,1024]{1,0:T(8,128)(2,1)S(1)}, u32[]{:S(2)}, u32[]{:S(2)}) %collective-permute-start.13) | collective-permute-done | bytes 65568 | tf_op jit(solution)/shard_map/ppermute | solution.py:153
  59.0 2.1 %collective-permute-done.12 = bf16[32,1024]{1,0:T(8,128)(2,1)S(1)} collective-permute-done((bf16[32,1024]{1,0:T(8,128)(2,1)S(1)}, bf16[32,1024]{1,0:T(8,128)(2,1)S(1)}, u32[]{:S(2)}, u32[]{:S(2)}) %collective-permute-start.12) | collective-permute-done | bytes 65568 | tf_op jit(solution)/shard_map/ppermute | solution.py:153
  61.1 0.7 %collective-permute-start.14 = (bf16[32,512]{1,0:T(8,128)(2,1)S(1)}, bf16[32,512]{1,0:T(8,128)(2,1)S(1)}, u32[]{:S(2)}, u32[]{:S(2)}) collective-permute-start(bf16[32,512]{1,0:T(8,128)(2,1)S(1)} %slice.52), channel_id=1, source_target_pairs={{0,2},{1,3},{2,0},{3,1},{4,6},{5,7},{6,4},{7,5},{8,10},{9,11},{10,... | collective-permute-start | bytes 98312 | tf_op jit(solution)/shard_map/ppermute | solution.py:153
  61.8 3.3 %collective-permute-done.14 = bf16[32,512]{1,0:T(8,128)(2,1)S(1)} collective-permute-done((bf16[32,512]{1,0:T(8,128)(2,1)S(1)}, bf16[32,512]{1,0:T(8,128)(2,1)S(1)}, u32[]{:S(2)}, u32[]{:S(2)}) %collective-permute-start.14) | collective-permute-done | bytes 32800 | tf_op jit(solution)/shard_map/ppermute | solution.py:153
  65.1 1.4 %fusion.3 = bf16[32,512]{1,0:T(8,128)(2,1)} fusion(f32[32,1024]{1,0:T(8,128)S(1)} %fusion.1, bf16[32,512]{1,0:T(8,128)(2,1)S(1)} %collective-permute-done.14, bf16[32,512]{1,0:T(8,128)(2,1)} %get-tuple-element.12), kind=kLoop, calls=%fused_computation.10 | loop fusion | flops 81920 | bytes 163840 | tf_op jit(solution)/shard_map/convert_element_type | solution.py:391
  (63 shorter events, 2.9 us)
Async XLA Ops:
  4.1 7.9 %collective-permute-start.2 = (bf16[32,1152]{1,0:T(8,128)(2,1)S(1)}, bf16[32,1152]{1,0:T(8,128)(2,1)S(1)}, u32[]{:S(2)}, u32[]{:S(2)}) collective-permute-start(bf16[32,1152]{1,0:T(8,128)(2,1)S(1)} %shard_map.118.own_ref.cw0_ref), channel_id=1, source_target_pairs={{0,12},{4,8},{8,4},{12,0},{1,13},{5,9},{9,5},{13,1},{2,14},{6,10},... | collective-permute-start | bytes 221192 | tf_op jit(solution)/shard_map/ppermute | solution.py:153
  9.2 6.3 %collective-permute-start.1 = (bf16[32,1152]{1,0:T(8,128)(2,1)S(1)}, bf16[32,1152]{1,0:T(8,128)(2,1)S(1)}, u32[]{:S(2)}, u32[]{:S(2)}) collective-permute-start(bf16[32,1152]{1,0:T(8,128)(2,1)S(1)} %shard_map.118.own_ref.cw0_ref), channel_id=1, source_target_pairs={{0,8},{4,12},{8,0},{12,4},{1,9},{5,13},{9,1},{13,5},{2,10},{6,14},... | collective-permute-start | bytes 221192 | tf_op jit(solution)/shard_map/ppermute | solution.py:153
  9.2 6.3 %collective-permute-start = (bf16[32,1152]{1,0:T(8,128)(2,1)S(1)}, bf16[32,1152]{1,0:T(8,128)(2,1)S(1)}, u32[]{:S(2)}, u32[]{:S(2)}) collective-permute-start(bf16[32,1152]{1,0:T(8,128)(2,1)S(1)} %shard_map.118.own_ref.cw0_ref), channel_id=1, source_target_pairs={{0,4},{4,0},{8,12},{12,8},{1,5},{5,1},{9,13},{13,9},{2,6},{6,2},{1... | collective-permute-start | bytes 221192 | tf_op jit(solution)/shard_map/ppermute | solution.py:153
  9.9 0.9 %collective-permute-start.3 = (bf16[32,512]{1,0:T(8,128)(2,1)S(1)}, bf16[32,512]{1,0:T(8,128)(2,1)S(1)}, u32[]{:S(2)}, u32[]{:S(2)}) collective-permute-start(bf16[32,512]{1,0:T(8,128)(2,1)S(1)} %bitcast.30), channel_id=1, source_target_pairs={{0,0},{1,4},{2,8},{3,12},{4,1},{5,5},{6,9},{7,13},{8,2},{9,6},{10,... | collective-permute-start | bytes 98312 | tf_op jit(solution)/shard_map/ppermute | solution.py:313
  10.5 25.5 %slice-start = ((s8[16777216]{0:T(1024)(128)(4,1)}), s8[4194304]{0:T(1024)(128)(4,1)S(1)}, s32[]{:S(2)}) async-start(s8[16777216]{0:T(1024)(128)(4,1)} %bitcast.15), calls=%async_computation | async-start | bytes 8388608
  10.6 25.5 %slice-start.4 = ((s8[16777216]{0:T(1024)(128)(4,1)}), s8[4194304]{0:T(1024)(128)(4,1)S(1)}, s32[]{:S(2)}) async-start(s8[16777216]{0:T(1024)(128)(4,1)} %bitcast.17), calls=%async_computation.4 | async-start | bytes 8388608
  10.6 25.4 %slice-start.8 = ((s8[16777216]{0:T(1024)(128)(4,1)}), s8[4194304]{0:T(1024)(128)(4,1)S(1)}, s32[]{:S(2)}) async-start(s8[16777216]{0:T(1024)(128)(4,1)} %bitcast.19), calls=%async_computation.8 | async-start | bytes 8388608
  10.7 25.4 %slice-start.3 = ((s8[16777216]{0:T(1024)(128)(4,1)}), s8[4194304]{0:T(1024)(128)(4,1)S(1)}, s32[]{:S(2)}) async-start(s8[16777216]{0:T(1024)(128)(4,1)} %bitcast.15), calls=%async_computation.3 | async-start | bytes 8388608
  10.7 25.4 %slice-start.5 = ((s8[16777216]{0:T(1024)(128)(4,1)}), s8[4194304]{0:T(1024)(128)(4,1)S(1)}, s32[]{:S(2)}) async-start(s8[16777216]{0:T(1024)(128)(4,1)} %bitcast.17), calls=%async_computation.5 | async-start | bytes 8388608
  10.7 25.4 %slice-start.6 = ((s8[16777216]{0:T(1024)(128)(4,1)}), s8[4194304]{0:T(1024)(128)(4,1)S(1)}, s32[]{:S(2)}) async-start(s8[16777216]{0:T(1024)(128)(4,1)} %bitcast.17), calls=%async_computation.6 | async-start | bytes 8388608
  10.7 25.4 %slice-start.7 = ((s8[16777216]{0:T(1024)(128)(4,1)}), s8[4194304]{0:T(1024)(128)(4,1)S(1)}, s32[]{:S(2)}) async-start(s8[16777216]{0:T(1024)(128)(4,1)} %bitcast.17), calls=%async_computation.7 | async-start | bytes 8388608
  10.7 25.4 %slice-start.9 = ((s8[16777216]{0:T(1024)(128)(4,1)}), s8[4194304]{0:T(1024)(128)(4,1)S(1)}, s32[]{:S(2)}) async-start(s8[16777216]{0:T(1024)(128)(4,1)} %bitcast.19), calls=%async_computation.9 | async-start | bytes 8388608
  10.7 25.4 %slice-start.10 = ((s8[16777216]{0:T(1024)(128)(4,1)}), s8[4194304]{0:T(1024)(128)(4,1)S(1)}, s32[]{:S(2)}) async-start(s8[16777216]{0:T(1024)(128)(4,1)} %bitcast.19), calls=%async_computation.10 | async-start | bytes 8388608
  16.5 1.3 %collective-permute-start.4 = (bf16[128,256]{1,0:T(8,128)(2,1)S(1)}, bf16[128,256]{1,0:T(8,128)(2,1)S(1)}, u32[]{:S(2)}, u32[]{:S(2)}) collective-permute-start(bf16[128,256]{1,0:T(8,128)(2,1)S(1)} %get-tuple-element.11), channel_id=1, source_target_pairs={{0,1},{1,0},{2,3},{3,2},{4,5},{5,4},{6,7},{7,6},{8,9},{9,8},{10,11... | collective-permute-start | bytes 196616 | tf_op jit(solution)/shard_map/ppermute | solution.py:153
  17.8 6.2 %collective-permute-start.5 = (bf16[128,256]{1,0:T(8,128)(2,1)S(1)}, bf16[128,256]{1,0:T(8,128)(2,1)S(1)}, u32[]{:S(2)}, u32[]{:S(2)}) collective-permute-start(bf16[128,256]{1,0:T(8,128)(2,1)S(1)} %add_convert_fusion.1), channel_id=1, source_target_pairs={{0,2},{1,3},{2,0},{3,1},{4,6},{5,7},{6,4},{7,5},{8,10},{9,11},{10,... | collective-permute-start | bytes 196616 | tf_op jit(solution)/shard_map/ppermute | solution.py:153
  24.0 6.6 %collective-permute-start.8 = (bf16[128,256]{1,0:T(8,128)(2,1)S(1)}, bf16[128,256]{1,0:T(8,128)(2,1)S(1)}, u32[]{:S(2)}, u32[]{:S(2)}) collective-permute-start(bf16[128,256]{1,0:T(8,128)(2,1)S(1)} %add_convert_fusion), channel_id=1, source_target_pairs={{0,12},{4,8},{8,4},{12,0},{1,13},{5,9},{9,5},{13,1},{2,14},{6,10},... | collective-permute-start | bytes 196616 | tf_op jit(solution)/shard_map/ppermute | solution.py:153
  28.3 5.3 %collective-permute-start.7 = (bf16[128,256]{1,0:T(8,128)(2,1)S(1)}, bf16[128,256]{1,0:T(8,128)(2,1)S(1)}, u32[]{:S(2)}, u32[]{:S(2)}) collective-permute-start(bf16[128,256]{1,0:T(8,128)(2,1)S(1)} %add_convert_fusion), channel_id=1, source_target_pairs={{0,8},{4,12},{8,0},{12,4},{1,9},{5,13},{9,1},{13,5},{2,10},{6,14},... | collective-permute-start | bytes 196616 | tf_op jit(solution)/shard_map/ppermute | solution.py:153
  28.3 5.4 %collective-permute-start.6 = (bf16[128,256]{1,0:T(8,128)(2,1)S(1)}, bf16[128,256]{1,0:T(8,128)(2,1)S(1)}, u32[]{:S(2)}, u32[]{:S(2)}) collective-permute-start(bf16[128,256]{1,0:T(8,128)(2,1)S(1)} %add_convert_fusion), channel_id=1, source_target_pairs={{0,4},{4,0},{8,12},{12,8},{1,5},{5,1},{9,13},{13,9},{2,6},{6,2},{1... | collective-permute-start | bytes 196616 | tf_op jit(solution)/shard_map/ppermute | solution.py:153
  33.7 1.6 %collective-permute-start.9 = (bf16[4,128,256]{2,1,0:T(8,128)(2,1)S(1)}, bf16[4,128,256]{2,1,0:T(8,128)(2,1)S(1)}, u32[]{:S(2)}, u32[]{:S(2)}) collective-permute-start(bf16[4,128,256]{2,1,0:T(8,128)(2,1)S(1)} %pad_maximum_fusion.mine_ref), channel_id=1, source_target_pairs={{0,1},{1,0},{2,3},{3,2},{4,5},{5,4},{6,7},{7,6},{8,9},{9,8},{10,11... | collective-permute-start | bytes 786440 | tf_op jit(solution)/shard_map/ppermute | solution.py:153
  48.3 1.7 %collective-permute-start.10 = (bf16[128,1024]{1,0:T(8,128)(2,1)}, bf16[128,1024]{1,0:T(8,128)(2,1)S(1)}, u32[]{:S(2)}, u32[]{:S(2)}) collective-permute-start(bf16[128,1024]{1,0:T(8,128)(2,1)} %get-tuple-element.14), channel_id=1, source_target_pairs={{0,1},{1,0},{2,3},{3,2},{4,5},{5,4},{6,7},{7,6},{8,9},{9,8},{10,11... | collective-permute-start | bytes 786440 | tf_op jit(solution)/shard_map/ppermute | solution.py:153
  51.2 4.3 %collective-permute-start.11 = (bf16[32,1024]{1,0:T(8,128)(2,1)S(1)}, bf16[32,1024]{1,0:T(8,128)(2,1)S(1)}, u32[]{:S(2)}, u32[]{:S(2)}) collective-permute-start(bf16[32,1024]{1,0:T(8,128)(2,1)S(1)} %get-tuple-element.17), channel_id=1, source_target_pairs={{0,4},{4,0},{8,12},{12,8},{1,5},{5,1},{9,13},{13,9},{2,6},{6,2},{1... | collective-permute-start | bytes 196616 | tf_op jit(solution)/shard_map/ppermute | solution.py:153
  51.8 7.2 %collective-permute-start.13 = (bf16[32,1024]{1,0:T(8,128)(2,1)S(1)}, bf16[32,1024]{1,0:T(8,128)(2,1)S(1)}, u32[]{:S(2)}, u32[]{:S(2)}) collective-permute-start(bf16[32,1024]{1,0:T(8,128)(2,1)S(1)} %get-tuple-element.18), channel_id=1, source_target_pairs={{0,12},{4,8},{8,4},{12,0},{1,13},{5,9},{9,5},{13,1},{2,14},{6,10},... | collective-permute-start | bytes 196616 | tf_op jit(solution)/shard_map/ppermute | solution.py:153
  54.6 6.5 %collective-permute-start.12 = (bf16[32,1024]{1,0:T(8,128)(2,1)S(1)}, bf16[32,1024]{1,0:T(8,128)(2,1)S(1)}, u32[]{:S(2)}, u32[]{:S(2)}) collective-permute-start(bf16[32,1024]{1,0:T(8,128)(2,1)S(1)} %get-tuple-element.19), channel_id=1, source_target_pairs={{0,8},{4,12},{8,0},{12,4},{1,9},{5,13},{9,1},{13,5},{2,10},{6,14},... | collective-permute-start | bytes 196616 | tf_op jit(solution)/shard_map/ppermute | solution.py:153
  61.1 4.0 %collective-permute-start.14 = (bf16[32,512]{1,0:T(8,128)(2,1)S(1)}, bf16[32,512]{1,0:T(8,128)(2,1)S(1)}, u32[]{:S(2)}, u32[]{:S(2)}) collective-permute-start(bf16[32,512]{1,0:T(8,128)(2,1)S(1)} %slice.52), channel_id=1, source_target_pairs={{0,2},{1,3},{2,0},{3,1},{4,6},{5,7},{6,4},{7,5},{8,10},{9,11},{10,... | collective-permute-start | bytes 98312 | tf_op jit(solution)/shard_map/ppermute | solution.py:153
  (12 other events, 128.2 us)

commit v3 on v2

--- a/solution.py
+++ b/solution.py
@@ -153,6 +153,11 @@
     return lax.ppermute(value, axis, [(i, i ^ mask) for i in range(size)])
 
 
+def spread(value):
+    got = {s: flip_permute(value, "wide", s) for s in (1, 3, 2)}
+    return [got[1], got[2], got[3]]
+
+
 def attend_kernel(*refs):
     given, out_ref, mixed_ref, held, sems = refs[:6], refs[6], refs[7], refs[8:14], refs[14]
     copies = [
@@ -172,23 +177,33 @@
     row_request = lax.broadcasted_iota(jnp.int32, (group * heads, group * slots), 0) // heads
     column = lax.broadcasted_iota(jnp.int32, (group * heads, group * slots), 1)
     place = column - row_request * slots
+    scores = []
+    limits = []
     for g in range(rows // group):
         limit = jnp.zeros_like(place)
         for i in range(group):
             r = g * group + i
             limit = jnp.where(row_request == i, len_ref[r // per_micro, r % per_micro], limit)
-        q = q_ref[g * group * heads:(g + 1) * group * heads, :]
-        k = k_ref[g * group * slots:(g + 1) * group * slots, :]
-        v = v_ref[g * group * slots:(g + 1) * group * slots, :]
-        scores = lax.dot_general(
-            q, k, (((1,), (1,)), ((), ())), preferred_element_type=jnp.float32
-        ) * (1.0 / math.sqrt(width))
-        usable = (place >= 0) & (place < limit)
-        scores = jnp.where(usable, scores, -1e30)
-        weight = jnp.exp(scores - jnp.max(scores, axis=-1, keepdims=True))
-        probs = (weight / jnp.sum(weight, axis=-1, keepdims=True)).astype(jnp.bfloat16)
+        limits.append(limit)
+        scores.append(
+            lax.dot_general(
+                q_ref[g * group * heads:(g + 1) * group * heads, :],
+                k_ref[g * group * slots:(g + 1) * group * slots, :],
+                (((1,), (1,)), ((), ())),
+                preferred_element_type=jnp.float32,
+            )
+        )
+    place = jnp.concatenate([place] * len(scores), axis=0)
+    usable = (place >= 0) & (place < jnp.concatenate(limits, axis=0))
+    scores = jnp.concatenate(scores, axis=0) * (1.0 / math.sqrt(width))
+    scores = jnp.where(usable, scores, -1e30)
+    weight = jnp.exp(scores - jnp.max(scores, axis=-1, keepdims=True))
+    probs = (weight / jnp.sum(weight, axis=-1, keepdims=True)).astype(jnp.bfloat16)
+    for g in range(rows // group):
         mixed_ref[g * group * heads:(g + 1) * group * heads, :] = jnp.dot(
-            probs, v, preferred_element_type=jnp.float32
+            probs[g * group * heads:(g + 1) * group * heads, :],
+            v_ref[g * group * slots:(g + 1) * group * slots, :],
+            preferred_element_type=jnp.float32,
         )
     for h in range(heads):
         out_ref[:, h * width:(h + 1) * width] = mixed_ref[
@@ -238,12 +253,24 @@
 
 def expert_kernel(where_ref, mine_ref, other_ref, cw0_ref, cw1_ref, cw2_ref, cw3_ref,
                   gain_ref, wg_ref, wu_ref, wd_ref, keep_ref, send_ref, stream_ref,
-                  x_ref, hid_ref):
+                  x_ref, hid_ref, down_ref, sems):
     wide, narrow = where_ref[0], where_ref[1]
     core = narrow & 1
     blocks, total, half = mine_ref.shape
     rows = total // blocks
     experts, depth, width = wg_ref.shape
+    block = 2 * half
+    order = (1, 3, 0, 2)
+
+    def fetch(i):
+        start = pl.multiple_of((narrow ^ order[i]) * block, block)
+        slot = i % down_ref.shape[0]
+        return pltpu.make_async_copy(
+            wd_ref.at[:, pl.ds(start, block)], down_ref.at[slot], sems.at[slot]
+        )
+
+    for i in range(down_ref.shape[0]):
+        fetch(i).start()
     square = jnp.zeros((total, 1), jnp.float32)
     for s in range(blocks):
         for piece, side in ((mine_ref, core), (other_ref, 1 - core)):
@@ -265,25 +292,21 @@
     mix = jnp.concatenate([r[:, -128:] for r in (cw0_ref, cw1_ref, cw2_ref, cw3_ref)], axis=0)
     lane = lax.broadcasted_iota(jnp.int32, (mix.shape[1], width), 0) % (mix.shape[1] // 2)
 
-    def one(e, carry):
+    for e in range(experts):
         gate = jnp.dot(x_ref[...], wg_ref[e], preferred_element_type=jnp.float32)
         upper = jnp.dot(x_ref[...], wu_ref[e], preferred_element_type=jnp.float32)
         pick = (lane == wide * experts + e).astype(jnp.bfloat16)
         share = jnp.dot(mix, pick, preferred_element_type=jnp.float32)
         hidden = gate / (1.0 + jnp.exp(-gate)) * upper * share
-        hid_ref[:, pl.ds(pl.multiple_of(e * width, width), width)] = hidden.astype(jnp.bfloat16)
-        return carry
-
-    lax.fori_loop(0, experts, one, 0)
-    block = 2 * half
-    for j in (1, 3, 0, 2):
-        out = jnp.dot(
-            hid_ref[...],
-            wd_ref[:, pl.ds(pl.multiple_of((narrow ^ j) * block, block), block)],
-            preferred_element_type=jnp.float32,
-        )
+        hid_ref[:, e * width:(e + 1) * width] = hidden.astype(jnp.bfloat16)
+    for i, j in enumerate(order):
+        slot = i % down_ref.shape[0]
+        fetch(i).wait()
+        out = jnp.dot(hid_ref[...], down_ref[slot], preferred_element_type=jnp.float32)
         target = send_ref if j & 1 else keep_ref
         target[:, (j >> 1) * block:((j >> 1) + 1) * block] = out.astype(target.dtype)
+        if i + down_ref.shape[0] < len(order):
+            fetch(i + down_ref.shape[0]).start()
 
 
 def local_small(
@@ -335,7 +358,7 @@
         cost_estimate=pl.CostEstimate(flops=2 * 10**10, bytes_accessed=10**8, transcendentals=0),
         compiler_params=pltpu.CompilerParams(vmem_limit_bytes=6 * 2**20),
     )(*[pltpu.with_memory_space_constraint(g, pltpu.HBM) for g in given])
-    others = [flip_permute(payload, "wide", s) for s in (1, 2, 3)]
+    others = spread(payload)
     keep, send = pl.pallas_call(
         project_kernel,
         out_shape=(
@@ -351,11 +374,13 @@
     stream = (
         part.astype(jnp.float32) + flip_permute(part, "narrow", 2).astype(jnp.float32)
     ).astype(jnp.bfloat16)
-    mine = jnp.stack([stream] + [flip_permute(stream, "wide", s) for s in (1, 2, 3)])
+    mine = jnp.stack([stream] + spread(stream))
     other = flip_permute(mine, "narrow", 1)
     weights = [
         pltpu.with_memory_space_constraint(w, pltpu.VMEM)
-        for w in (w_gate, w_up, w_down.reshape(experts * hidden, model))
+        for w in (w_gate, w_up)
+    ] + [
+        pltpu.with_memory_space_constraint(w_down.reshape(experts * hidden, model), pltpu.HBM)
     ]
     keep, send, own = pl.pallas_call(
         expert_kernel,
@@ -364,13 +389,15 @@
             jax.ShapeDtypeStruct((size * rows, model // 2), jnp.bfloat16),
             jax.ShapeDtypeStruct((rows, columns), jnp.bfloat16),
         ),
-        in_specs=[smem] + [vmem] * 10,
+        in_specs=[smem] + [vmem] * 9 + [pl.BlockSpec(memory_space=pl.ANY)],
         out_specs=(vmem, vmem, vmem),
         scratch_shapes=[
             pltpu.VMEM((size * rows, model), jnp.bfloat16),
             pltpu.VMEM((size * rows, experts * hidden), jnp.bfloat16),
+            pltpu.VMEM((3, experts * hidden, columns), jnp.bfloat16),
+            pltpu.SemaphoreType.DMA((3,)),
         ],
-        compiler_params=pltpu.CompilerParams(vmem_limit_bytes=12 * 2**20),
+        compiler_params=pltpu.CompilerParams(vmem_limit_bytes=20 * 2**20),
     )(
         where,
         mine,
@@ -384,7 +411,7 @@
     total = total.reshape(size, rows, model // 2)
     leave = total[1:].astype(jnp.bfloat16)
     summed = total[0]
-    for s in (1, 2, 3):
+    for s in (2, 1, 3):
         summed = summed + flip_permute(leave[s - 1], "wide", s).astype(jnp.float32)
     cross = flip_permute(summed[:, columns:].astype(jnp.bfloat16), "narrow", 2)
     result = own.astype(jnp.float32) + summed[:, :columns] + cross.astype(jnp.float32)

time: 66.7 us -> 61.5 us (0.922)
  Pallas kernels: 17.2 us -> 15.4 us
  other arithmetic: 2.68 us -> 0.89 us
  local copies, waits for them, and re-layouts: 0.82 us -> 0.08 us
    pallas_call x1, Pallas kernels: 4.09 us -> 2 us  [local_small(): pl.pallas_call(attend_kernel, out_shape=jax.ShapeDtypeStruct((rows, depth...]
    another operation x2, other arithmetic: 1.15 us -> 0.11 us
    convert_element_type x1, other arithmetic: 1.39 us -> 0.63 us  [local_small(): return result.astype(jnp.bfloat16).reshape(micro, per_micro, columns)]
    unnamed x42 -> x22, local copies, waits for them, and re-layouts: 0.8 us -> 0.05 us
where the time goes in v3:
time: 61.5 us; the launch traced here: 61.4 us
  waiting for transfers between devices  25.1 us (41%)
  starting transfers between devices  19.6 us (32%)
  Pallas kernels  15.4 us (25%)
  other arithmetic  0.89 us (1%)
    ppermute x14, waiting for transfers between devices, flip_permute(): return lax.ppermute(value, axis, [(i, i ^ mask) for i in range(size)])  25.1 us
    ppermute x14, starting transfers between devices, flip_permute(): return lax.ppermute(value, axis, [(i, i ^ mask) for i in range(size)])  18.9 us
    pallas_call x1, Pallas kernels, local_small(): pl.pallas_call(expert_kernel, out_shape=(jax.ShapeDtypeStruct((size * row...  12.6 us
    pallas_call x1, Pallas kernels, local_small(): pl.pallas_call(attend_kernel, out_shape=jax.ShapeDtypeStruct((rows, depth...  2 us
  transfers between devices with their start and end apart: 15, of which 13 were waited for; matrix products, arithmetic and copies ran while one was open for 0% of the time, Pallas kernels for 0%

profile of v3, /device:TPU:0, one launch (start us, length us, event | category | flops | bytes accessed | tf_op | source)
XLA Modules:
  0.0 61.4 jit_solution(1204863715838154009)
XLA Ops:
  0.0 2.0 %shard_map.118.own_ref.cw0_ref = bf16[32,1152]{1,0:T(8,128)(2,1)S(1)} custom-call(s32[2,16]{1,0:T(2,128)} %refs_0_.1, bf16[256,128]{1,0:T(8,128)(2,1)} %bitcast.27, bf16[2048,128]{1,0:T(8,128)(2,1)} %bitcast.25, bf16[2048,128]{1,0:T(8,128)(2,1)} %bitcast.26, s32[2,8,16]{2,1,0:T(8,128)} %bitcast.29, f32[2,8,16]{2,1,0:T(8,128)} %bitcast.30), custom_call_target="tpu_custom_call" | custom-call | flops 20000000000 | bytes 100000000 | tf_op jit(solution)/shard_map/pallas_call | solution.py:349
  2.0 5.1 %collective-permute-start.2 = (bf16[32,1152]{1,0:T(8,128)(2,1)S(1)}, bf16[32,1152]{1,0:T(8,128)(2,1)S(1)}, u32[]{:S(2)}, u32[]{:S(2)}) collective-permute-start(bf16[32,1152]{1,0:T(8,128)(2,1)S(1)} %shard_map.118.own_ref.cw0_ref), channel_id=1, source_target_pairs={{0,12},{4,8},{8,4},{12,0},{1,13},{5,9},{9,5},{13,1},{2,14},{6,10},... | collective-permute-start | bytes 221192 | tf_op jit(solution)/shard_map/ppermute | solution.py:153
  7.1 0.6 %collective-permute-start = (bf16[32,1152]{1,0:T(8,128)(2,1)S(1)}, bf16[32,1152]{1,0:T(8,128)(2,1)S(1)}, u32[]{:S(2)}, u32[]{:S(2)}) collective-permute-start(bf16[32,1152]{1,0:T(8,128)(2,1)S(1)} %shard_map.118.own_ref.cw0_ref), channel_id=1, source_target_pairs={{0,4},{4,0},{8,12},{12,8},{1,5},{5,1},{9,13},{13,9},{2,6},{6,2},{1... | collective-permute-start | bytes 221192 | tf_op jit(solution)/shard_map/ppermute | solution.py:153
  7.8 0.7 %collective-permute-start.3 = (bf16[32,512]{1,0:T(8,128)(2,1)S(1)}, bf16[32,512]{1,0:T(8,128)(2,1)S(1)}, u32[]{:S(2)}, u32[]{:S(2)}) collective-permute-start(bf16[32,512]{1,0:T(8,128)(2,1)S(1)} %bitcast.28), channel_id=1, source_target_pairs={{0,0},{1,4},{2,8},{3,12},{4,1},{5,5},{6,9},{7,13},{8,2},{9,6},{10,... | collective-permute-start | bytes 98312 | tf_op jit(solution)/shard_map/ppermute | solution.py:336
  8.6 1.3 %collective-permute-done.2.got3_ref.cw3_ref = bf16[32,1152]{1,0:T(8,128)(2,1)S(1)} collective-permute-done((bf16[32,1152]{1,0:T(8,128)(2,1)S(1)}, bf16[32,1152]{1,0:T(8,128)(2,1)S(1)}, u32[]{:S(2)}, u32[]{:S(2)}) %collective-permute-start.2) | collective-permute-done | bytes 73760 | tf_op jit(solution)/shard_map/ppermute | solution.py:153
  9.9 3.5 %collective-permute-done.1.got2_ref.cw2_ref = bf16[32,1152]{1,0:T(8,128)(2,1)S(1)} collective-permute-done((bf16[32,1152]{1,0:T(8,128)(2,1)S(1)}, bf16[32,1152]{1,0:T(8,128)(2,1)S(1)}, u32[]{:S(2)}, u32[]{:S(2)}) %collective-permute-start.1) | collective-permute-done | bytes 73760 | tf_op jit(solution)/shard_map/ppermute | solution.py:153
  13.4 0.9 %shard_map.119 = (f32[128,256]{1,0:T(8,128)S(1)}, bf16[128,256]{1,0:T(8,128)(2,1)S(1)}) custom-call(s32[2]{0:T(128)S(1)} %pad_add_fusion.where_ref, bf16[32,1152]{1,0:T(8,128)(2,1)S(1)} %shard_map.118.own_ref.cw0_ref, bf16[32,1152]{1,0:T(8,128)(2,1)S(1)} %collective-permute-done.got1_ref.cw1_ref, ...), custom_call_target="tpu_custom_call" | custom-call | flops 20000000000 | bytes 100000000 | tf_op jit(solution)/shard_map/pallas_call | solution.py:362
  14.5 1.2 %collective-permute-done.4 = bf16[128,256]{1,0:T(8,128)(2,1)S(1)} collective-permute-done((bf16[128,256]{1,0:T(8,128)(2,1)S(1)}, bf16[128,256]{1,0:T(8,128)(2,1)S(1)}, u32[]{:S(2)}, u32[]{:S(2)}) %collective-permute-start.4) | collective-permute-done | bytes 65568 | tf_op jit(solution)/shard_map/ppermute | solution.py:153
  15.7 3.8 %collective-permute-start.5 = (bf16[128,256]{1,0:T(8,128)(2,1)S(1)}, bf16[128,256]{1,0:T(8,128)(2,1)S(1)}, u32[]{:S(2)}, u32[]{:S(2)}) collective-permute-start(bf16[128,256]{1,0:T(8,128)(2,1)S(1)} %add_convert_fusion.1), channel_id=1, source_target_pairs={{0,2},{1,3},{2,0},{3,1},{4,6},{5,7},{6,4},{7,5},{8,10},{9,11},{10,... | collective-permute-start | bytes 196616 | tf_op jit(solution)/shard_map/ppermute | solution.py:153
  19.4 2.4 %collective-permute-done.5 = bf16[128,256]{1,0:T(8,128)(2,1)S(1)} collective-permute-done((bf16[128,256]{1,0:T(8,128)(2,1)S(1)}, bf16[128,256]{1,0:T(8,128)(2,1)S(1)}, u32[]{:S(2)}, u32[]{:S(2)}) %collective-permute-start.5) | collective-permute-done | bytes 65568 | tf_op jit(solution)/shard_map/ppermute | solution.py:153
  21.9 4.2 %collective-permute-start.8 = (bf16[128,256]{1,0:T(8,128)(2,1)S(1)}, bf16[128,256]{1,0:T(8,128)(2,1)S(1)}, u32[]{:S(2)}, u32[]{:S(2)}) collective-permute-start(bf16[128,256]{1,0:T(8,128)(2,1)S(1)} %add_convert_fusion), channel_id=1, source_target_pairs={{0,12},{4,8},{8,4},{12,0},{1,13},{5,9},{9,5},{13,1},{2,14},{6,10},... | collective-permute-start | bytes 196616 | tf_op jit(solution)/shard_map/ppermute | solution.py:153
  26.1 0.6 %collective-permute-start.6 = (bf16[128,256]{1,0:T(8,128)(2,1)S(1)}, bf16[128,256]{1,0:T(8,128)(2,1)S(1)}, u32[]{:S(2)}, u32[]{:S(2)}) collective-permute-start(bf16[128,256]{1,0:T(8,128)(2,1)S(1)} %add_convert_fusion), channel_id=1, source_target_pairs={{0,4},{4,0},{8,12},{12,8},{1,5},{5,1},{9,13},{13,9},{2,6},{6,2},{1... | collective-permute-start | bytes 196616 | tf_op jit(solution)/shard_map/ppermute | solution.py:153
  26.7 1.7 %collective-permute-done.8 = bf16[128,256]{1,0:T(8,128)(2,1)S(1)} collective-permute-done((bf16[128,256]{1,0:T(8,128)(2,1)S(1)}, bf16[128,256]{1,0:T(8,128)(2,1)S(1)}, u32[]{:S(2)}, u32[]{:S(2)}) %collective-permute-start.8) | collective-permute-done | bytes 65568 | tf_op jit(solution)/shard_map/ppermute | solution.py:153
  28.5 2.9 %collective-permute-done.7 = bf16[128,256]{1,0:T(8,128)(2,1)S(1)} collective-permute-done((bf16[128,256]{1,0:T(8,128)(2,1)S(1)}, bf16[128,256]{1,0:T(8,128)(2,1)S(1)}, u32[]{:S(2)}, u32[]{:S(2)}) %collective-permute-start.7) | collective-permute-done | bytes 65568 | tf_op jit(solution)/shard_map/ppermute | solution.py:153
  31.6 1.5 %collective-permute-done.9.other_ref = bf16[4,128,256]{2,1,0:T(8,128)(2,1)S(1)} collective-permute-done((bf16[4,128,256]{2,1,0:T(8,128)(2,1)S(1)}, bf16[4,128,256]{2,1,0:T(8,128)(2,1)S(1)}, u32[]{:S(2)}, u32[]{:S(2)}) %collective-permute-start.9) | collective-permute-done | bytes 262176 | tf_op jit(solution)/shard_map/ppermute | solution.py:153
  33.2 12.6 %shard_map.120 = (f32[128,1024]{1,0:T(8,128)S(1)}, bf16[128,1024]{1,0:T(8,128)(2,1)S(1)}, bf16[32,512]{1,0:T(8,128)(2,1)S(1)}) custom-call(s32[2]{0:T(128)S(1)} %pad_add_fusion.where_ref, bf16[4,128,256]{2,1,0:T(8,128)(2,1)S(1)} %pad_maximum_fusion.mine_ref, bf16[4,128,256]{2,1,0:T(8,128)(2,1)S(1)} %collective-permute-done.9.other_ref, ...), custom_call_target="tpu_custom_call" | custom-call | tf_op jit(solution)/shard_map/pallas_call | solution.py:385
  46.0 1.4 %collective-permute-done.10 = bf16[128,1024]{1,0:T(8,128)(2,1)S(1)} collective-permute-done((bf16[128,1024]{1,0:T(8,128)(2,1)S(1)}, bf16[128,1024]{1,0:T(8,128)(2,1)S(1)}, u32[]{:S(2)}, u32[]{:S(2)}) %collective-permute-start.10) | collective-permute-done | bytes 262176 | tf_op jit(solution)/shard_map/ppermute | solution.py:153
  47.5 1.9 %collective-permute-start.11 = (bf16[32,1024]{1,0:T(8,128)(2,1)S(1)}, bf16[32,1024]{1,0:T(8,128)(2,1)S(1)}, u32[]{:S(2)}, u32[]{:S(2)}) collective-permute-start(bf16[32,1024]{1,0:T(8,128)(2,1)S(1)} %get-tuple-element.17), channel_id=1, source_target_pairs={{0,8},{4,12},{8,0},{12,4},{1,9},{5,13},{9,1},{13,5},{2,10},{6,14},... | collective-permute-start | bytes 196616 | tf_op jit(solution)/shard_map/ppermute | solution.py:153
  49.4 1.1 %collective-permute-start.13 = (bf16[32,1024]{1,0:T(8,128)(2,1)S(1)}, bf16[32,1024]{1,0:T(8,128)(2,1)S(1)}, u32[]{:S(2)}, u32[]{:S(2)}) collective-permute-start(bf16[32,1024]{1,0:T(8,128)(2,1)S(1)} %get-tuple-element.18), channel_id=1, source_target_pairs={{0,12},{4,8},{8,4},{12,0},{1,13},{5,9},{9,5},{13,1},{2,14},{6,10},... | collective-permute-start | bytes 196616 | tf_op jit(solution)/shard_map/ppermute | solution.py:153
  51.1 3.9 %collective-permute-done.11 = bf16[32,1024]{1,0:T(8,128)(2,1)S(1)} collective-permute-done((bf16[32,1024]{1,0:T(8,128)(2,1)S(1)}, bf16[32,1024]{1,0:T(8,128)(2,1)S(1)}, u32[]{:S(2)}, u32[]{:S(2)}) %collective-permute-start.11) | collective-permute-done | bytes 65568 | tf_op jit(solution)/shard_map/ppermute | solution.py:153
  54.9 0.9 %collective-permute-done.13 = bf16[32,1024]{1,0:T(8,128)(2,1)S(1)} collective-permute-done((bf16[32,1024]{1,0:T(8,128)(2,1)S(1)}, bf16[32,1024]{1,0:T(8,128)(2,1)S(1)}, u32[]{:S(2)}, u32[]{:S(2)}) %collective-permute-start.13) | collective-permute-done | bytes 65568 | tf_op jit(solution)/shard_map/ppermute | solution.py:153
  55.8 0.9 %collective-permute-done.12 = bf16[32,1024]{1,0:T(8,128)(2,1)S(1)} collective-permute-done((bf16[32,1024]{1,0:T(8,128)(2,1)S(1)}, bf16[32,1024]{1,0:T(8,128)(2,1)S(1)}, u32[]{:S(2)}, u32[]{:S(2)}) %collective-permute-start.12) | collective-permute-done | bytes 65568 | tf_op jit(solution)/shard_map/ppermute | solution.py:153
  57.3 3.4 %collective-permute-done.14 = bf16[32,512]{1,0:T(8,128)(2,1)S(1)} collective-permute-done((bf16[32,512]{1,0:T(8,128)(2,1)S(1)}, bf16[32,512]{1,0:T(8,128)(2,1)S(1)}, u32[]{:S(2)}, u32[]{:S(2)}) %collective-permute-start.14) | collective-permute-done | bytes 32800 | tf_op jit(solution)/shard_map/ppermute | solution.py:153
  60.7 0.6 %fusion.3 = bf16[32,512]{1,0:T(8,128)(2,1)} fusion(f32[32,1024]{1,0:T(8,128)S(1)} %fusion.1, bf16[32,512]{1,0:T(8,128)(2,1)S(1)} %collective-permute-done.14, bf16[32,512]{1,0:T(8,128)(2,1)S(1)} %get-tuple-element.12), kind=kLoop, calls=%fused_computation.10 | loop fusion | flops 81920 | bytes 163840 | tf_op jit(solution)/shard_map/convert_element_type | solution.py:418
  (42 shorter events, 2.0 us)
Async XLA Ops:
  2.0 7.9 %collective-permute-start.2 = (bf16[32,1152]{1,0:T(8,128)(2,1)S(1)}, bf16[32,1152]{1,0:T(8,128)(2,1)S(1)}, u32[]{:S(2)}, u32[]{:S(2)}) collective-permute-start(bf16[32,1152]{1,0:T(8,128)(2,1)S(1)} %shard_map.118.own_ref.cw0_ref), channel_id=1, source_target_pairs={{0,12},{4,8},{8,4},{12,0},{1,13},{5,9},{9,5},{13,1},{2,14},{6,10},... | collective-permute-start | bytes 221192 | tf_op jit(solution)/shard_map/ppermute | solution.py:153
  7.1 6.3 %collective-permute-start.1 = (bf16[32,1152]{1,0:T(8,128)(2,1)S(1)}, bf16[32,1152]{1,0:T(8,128)(2,1)S(1)}, u32[]{:S(2)}, u32[]{:S(2)}) collective-permute-start(bf16[32,1152]{1,0:T(8,128)(2,1)S(1)} %shard_map.118.own_ref.cw0_ref), channel_id=1, source_target_pairs={{0,8},{4,12},{8,0},{12,4},{1,9},{5,13},{9,1},{13,5},{2,10},{6,14},... | collective-permute-start | bytes 221192 | tf_op jit(solution)/shard_map/ppermute | solution.py:153
  7.1 6.3 %collective-permute-start = (bf16[32,1152]{1,0:T(8,128)(2,1)S(1)}, bf16[32,1152]{1,0:T(8,128)(2,1)S(1)}, u32[]{:S(2)}, u32[]{:S(2)}) collective-permute-start(bf16[32,1152]{1,0:T(8,128)(2,1)S(1)} %shard_map.118.own_ref.cw0_ref), channel_id=1, source_target_pairs={{0,4},{4,0},{8,12},{12,8},{1,5},{5,1},{9,13},{13,9},{2,6},{6,2},{1... | collective-permute-start | bytes 221192 | tf_op jit(solution)/shard_map/ppermute | solution.py:153
  7.8 0.8 %collective-permute-start.3 = (bf16[32,512]{1,0:T(8,128)(2,1)S(1)}, bf16[32,512]{1,0:T(8,128)(2,1)S(1)}, u32[]{:S(2)}, u32[]{:S(2)}) collective-permute-start(bf16[32,512]{1,0:T(8,128)(2,1)S(1)} %bitcast.28), channel_id=1, source_target_pairs={{0,0},{1,4},{2,8},{3,12},{4,1},{5,5},{6,9},{7,13},{8,2},{9,6},{10,... | collective-permute-start | bytes 98312 | tf_op jit(solution)/shard_map/ppermute | solution.py:336
  8.4 24.7 %slice-start = ((s8[16777216]{0:T(1024)(128)(4,1)}), s8[4194304]{0:T(1024)(128)(4,1)S(1)}, s32[]{:S(2)}) async-start(s8[16777216]{0:T(1024)(128)(4,1)} %bitcast.15), calls=%async_computation | async-start | bytes 8388608
  8.5 24.7 %slice-start.4 = ((s8[16777216]{0:T(1024)(128)(4,1)}), s8[4194304]{0:T(1024)(128)(4,1)S(1)}, s32[]{:S(2)}) async-start(s8[16777216]{0:T(1024)(128)(4,1)} %bitcast.17), calls=%async_computation.4 | async-start | bytes 8388608
  8.5 24.6 %slice-start.1 = ((s8[16777216]{0:T(1024)(128)(4,1)}), s8[4194304]{0:T(1024)(128)(4,1)S(1)}, s32[]{:S(2)}) async-start(s8[16777216]{0:T(1024)(128)(4,1)} %bitcast.15), calls=%async_computation.1 | async-start | bytes 8388608
  8.5 24.6 %slice-start.2 = ((s8[16777216]{0:T(1024)(128)(4,1)}), s8[4194304]{0:T(1024)(128)(4,1)S(1)}, s32[]{:S(2)}) async-start(s8[16777216]{0:T(1024)(128)(4,1)} %bitcast.15), calls=%async_computation.2 | async-start | bytes 8388608
  8.5 24.6 %slice-start.3 = ((s8[16777216]{0:T(1024)(128)(4,1)}), s8[4194304]{0:T(1024)(128)(4,1)S(1)}, s32[]{:S(2)}) async-start(s8[16777216]{0:T(1024)(128)(4,1)} %bitcast.15), calls=%async_computation.3 | async-start | bytes 8388608
  8.6 24.6 %slice-start.5 = ((s8[16777216]{0:T(1024)(128)(4,1)}), s8[4194304]{0:T(1024)(128)(4,1)S(1)}, s32[]{:S(2)}) async-start(s8[16777216]{0:T(1024)(128)(4,1)} %bitcast.17), calls=%async_computation.5 | async-start | bytes 8388608
  8.6 24.6 %slice-start.6 = ((s8[16777216]{0:T(1024)(128)(4,1)}), s8[4194304]{0:T(1024)(128)(4,1)S(1)}, s32[]{:S(2)}) async-start(s8[16777216]{0:T(1024)(128)(4,1)} %bitcast.17), calls=%async_computation.6 | async-start | bytes 8388608
  8.6 24.6 %slice-start.7 = ((s8[16777216]{0:T(1024)(128)(4,1)}), s8[4194304]{0:T(1024)(128)(4,1)S(1)}, s32[]{:S(2)}) async-start(s8[16777216]{0:T(1024)(128)(4,1)} %bitcast.17), calls=%async_computation.7 | async-start | bytes 8388608
  8.6 24.6 %copy-start = (f32[2048]{0:T(1024)S(1)}, f32[2048]{0:T(1024)}, u32[]{:S(2)}) copy-start(f32[2048]{0:T(1024)} %param.18) | copy-start | bytes 24580
  14.3 1.3 %collective-permute-start.4 = (bf16[128,256]{1,0:T(8,128)(2,1)S(1)}, bf16[128,256]{1,0:T(8,128)(2,1)S(1)}, u32[]{:S(2)}, u32[]{:S(2)}) collective-permute-start(bf16[128,256]{1,0:T(8,128)(2,1)S(1)} %get-tuple-element.11), channel_id=1, source_target_pairs={{0,1},{1,0},{2,3},{3,2},{4,5},{5,4},{6,7},{7,6},{8,9},{9,8},{10,11... | collective-permute-start | bytes 196616 | tf_op jit(solution)/shard_map/ppermute | solution.py:153
  15.7 6.2 %collective-permute-start.5 = (bf16[128,256]{1,0:T(8,128)(2,1)S(1)}, bf16[128,256]{1,0:T(8,128)(2,1)S(1)}, u32[]{:S(2)}, u32[]{:S(2)}) collective-permute-start(bf16[128,256]{1,0:T(8,128)(2,1)S(1)} %add_convert_fusion.1), channel_id=1, source_target_pairs={{0,2},{1,3},{2,0},{3,1},{4,6},{5,7},{6,4},{7,5},{8,10},{9,11},{10,... | collective-permute-start | bytes 196616 | tf_op jit(solution)/shard_map/ppermute | solution.py:153
  21.9 6.6 %collective-permute-start.8 = (bf16[128,256]{1,0:T(8,128)(2,1)S(1)}, bf16[128,256]{1,0:T(8,128)(2,1)S(1)}, u32[]{:S(2)}, u32[]{:S(2)}) collective-permute-start(bf16[128,256]{1,0:T(8,128)(2,1)S(1)} %add_convert_fusion), channel_id=1, source_target_pairs={{0,12},{4,8},{8,4},{12,0},{1,13},{5,9},{9,5},{13,1},{2,14},{6,10},... | collective-permute-start | bytes 196616 | tf_op jit(solution)/shard_map/ppermute | solution.py:153
  26.1 5.3 %collective-permute-start.7 = (bf16[128,256]{1,0:T(8,128)(2,1)S(1)}, bf16[128,256]{1,0:T(8,128)(2,1)S(1)}, u32[]{:S(2)}, u32[]{:S(2)}) collective-permute-start(bf16[128,256]{1,0:T(8,128)(2,1)S(1)} %add_convert_fusion), channel_id=1, source_target_pairs={{0,8},{4,12},{8,0},{12,4},{1,9},{5,13},{9,1},{13,5},{2,10},{6,14},... | collective-permute-start | bytes 196616 | tf_op jit(solution)/shard_map/ppermute | solution.py:153
  26.1 5.4 %collective-permute-start.6 = (bf16[128,256]{1,0:T(8,128)(2,1)S(1)}, bf16[128,256]{1,0:T(8,128)(2,1)S(1)}, u32[]{:S(2)}, u32[]{:S(2)}) collective-permute-start(bf16[128,256]{1,0:T(8,128)(2,1)S(1)} %add_convert_fusion), channel_id=1, source_target_pairs={{0,4},{4,0},{8,12},{12,8},{1,5},{5,1},{9,13},{13,9},{2,6},{6,2},{1... | collective-permute-start | bytes 196616 | tf_op jit(solution)/shard_map/ppermute | solution.py:153
  31.5 1.6 %collective-permute-start.9 = (bf16[4,128,256]{2,1,0:T(8,128)(2,1)S(1)}, bf16[4,128,256]{2,1,0:T(8,128)(2,1)S(1)}, u32[]{:S(2)}, u32[]{:S(2)}) collective-permute-start(bf16[4,128,256]{2,1,0:T(8,128)(2,1)S(1)} %pad_maximum_fusion.mine_ref), channel_id=1, source_target_pairs={{0,1},{1,0},{2,3},{3,2},{4,5},{5,4},{6,7},{7,6},{8,9},{9,8},{10,11... | collective-permute-start | bytes 786440 | tf_op jit(solution)/shard_map/ppermute | solution.py:153
  45.8 1.6 %collective-permute-start.10 = (bf16[128,1024]{1,0:T(8,128)(2,1)S(1)}, bf16[128,1024]{1,0:T(8,128)(2,1)S(1)}, u32[]{:S(2)}, u32[]{:S(2)}) collective-permute-start(bf16[128,1024]{1,0:T(8,128)(2,1)S(1)} %get-tuple-element.14), channel_id=1, source_target_pairs={{0,1},{1,0},{2,3},{3,2},{4,5},{5,4},{6,7},{7,6},{8,9},{9,8},{10,11... | collective-permute-start | bytes 786440 | tf_op jit(solution)/shard_map/ppermute | solution.py:153
  47.5 7.4 %collective-permute-start.11 = (bf16[32,1024]{1,0:T(8,128)(2,1)S(1)}, bf16[32,1024]{1,0:T(8,128)(2,1)S(1)}, u32[]{:S(2)}, u32[]{:S(2)}) collective-permute-start(bf16[32,1024]{1,0:T(8,128)(2,1)S(1)} %get-tuple-element.17), channel_id=1, source_target_pairs={{0,8},{4,12},{8,0},{12,4},{1,9},{5,13},{9,1},{13,5},{2,10},{6,14},... | collective-permute-start | bytes 196616 | tf_op jit(solution)/shard_map/ppermute | solution.py:153
  49.4 6.4 %collective-permute-start.13 = (bf16[32,1024]{1,0:T(8,128)(2,1)S(1)}, bf16[32,1024]{1,0:T(8,128)(2,1)S(1)}, u32[]{:S(2)}, u32[]{:S(2)}) collective-permute-start(bf16[32,1024]{1,0:T(8,128)(2,1)S(1)} %get-tuple-element.18), channel_id=1, source_target_pairs={{0,12},{4,8},{8,4},{12,0},{1,13},{5,9},{9,5},{13,1},{2,14},{6,10},... | collective-permute-start | bytes 196616 | tf_op jit(solution)/shard_map/ppermute | solution.py:153
  50.5 6.3 %collective-permute-start.12 = (bf16[32,1024]{1,0:T(8,128)(2,1)S(1)}, bf16[32,1024]{1,0:T(8,128)(2,1)S(1)}, u32[]{:S(2)}, u32[]{:S(2)}) collective-permute-start(bf16[32,1024]{1,0:T(8,128)(2,1)S(1)} %get-tuple-element.19), channel_id=1, source_target_pairs={{0,4},{4,0},{8,12},{12,8},{1,5},{5,1},{9,13},{13,9},{2,6},{6,2},{1... | collective-permute-start | bytes 196616 | tf_op jit(solution)/shard_map/ppermute | solution.py:153
  56.8 4.0 %collective-permute-start.14 = (bf16[32,512]{1,0:T(8,128)(2,1)S(1)}, bf16[32,512]{1,0:T(8,128)(2,1)S(1)}, u32[]{:S(2)}, u32[]{:S(2)}) collective-permute-start(bf16[32,512]{1,0:T(8,128)(2,1)S(1)} %slice.52), channel_id=1, source_target_pairs={{0,2},{1,3},{2,0},{3,1},{4,6},{5,7},{6,4},{7,5},{8,10},{9,11},{10,... | collective-permute-start | bytes 98312 | tf_op jit(solution)/shard_map/ppermute | solution.py:153
  (2 other events, 21.2 us)

commit v4 on v3

--- a/solution.py
+++ b/solution.py
@@ -230,7 +230,7 @@
 
 
 def project_kernel(where_ref, own_ref, got1_ref, got2_ref, got3_ref, w_ref, res_ref,
-                   keep_ref, send_ref):
+                   keep_ref, send_ref, mix_ref):
     wide, narrow = where_ref[0], where_ref[1]
     depth = w_ref.shape[0]
     half = keep_ref.shape[1]
@@ -249,28 +249,20 @@
     extra = jnp.concatenate([extra] * (part.shape[0] // rows), axis=0)
     part = jnp.where(part_rows == (wide ^ narrow), part + extra, part)
     send_ref[...] = part.astype(jnp.bfloat16)
-
-
-def expert_kernel(where_ref, mine_ref, other_ref, cw0_ref, cw1_ref, cw2_ref, cw3_ref,
-                  gain_ref, wg_ref, wu_ref, wd_ref, keep_ref, send_ref, stream_ref,
-                  x_ref, hid_ref, down_ref, sems):
+    mix_ref[...] = jnp.concatenate(
+        [r[:, depth:] for r in (own_ref, got1_ref, got2_ref, got3_ref)], axis=0
+    )
+
+
+def expert_kernel(where_ref, mine_ref, other_ref, mix_ref, gain_ref,
+                  wg_ref, wu_ref, wd_ref, keep_ref, send_ref, stream_ref,
+                  x_ref, hid_ref):
     wide, narrow = where_ref[0], where_ref[1]
     core = narrow & 1
     blocks, total, half = mine_ref.shape
     rows = total // blocks
     experts, depth, width = wg_ref.shape
     block = 2 * half
-    order = (1, 3, 0, 2)
-
-    def fetch(i):
-        start = pl.multiple_of((narrow ^ order[i]) * block, block)
-        slot = i % down_ref.shape[0]
-        return pltpu.make_async_copy(
-            wd_ref.at[:, pl.ds(start, block)], down_ref.at[slot], sems.at[slot]
-        )
-
-    for i in range(down_ref.shape[0]):
-        fetch(i).start()
     square = jnp.zeros((total, 1), jnp.float32)
     for s in range(blocks):
         for piece, side in ((mine_ref, core), (other_ref, 1 - core)):
@@ -289,7 +281,7 @@
         x_ref[:, cols] = (
             x_ref[:, cols].astype(jnp.float32) * scale * gain_ref[:, cols]
         ).astype(jnp.bfloat16)
-    mix = jnp.concatenate([r[:, -128:] for r in (cw0_ref, cw1_ref, cw2_ref, cw3_ref)], axis=0)
+    mix = mix_ref[...]
     lane = lax.broadcasted_iota(jnp.int32, (mix.shape[1], width), 0) % (mix.shape[1] // 2)
 
     for e in range(experts):
@@ -299,14 +291,13 @@
         share = jnp.dot(mix, pick, preferred_element_type=jnp.float32)
         hidden = gate / (1.0 + jnp.exp(-gate)) * upper * share
         hid_ref[:, e * width:(e + 1) * width] = hidden.astype(jnp.bfloat16)
-    for i, j in enumerate(order):
-        slot = i % down_ref.shape[0]
-        fetch(i).wait()
-        out = jnp.dot(hid_ref[...], down_ref[slot], preferred_element_type=jnp.float32)
+    for j in (1, 3, 0, 2):
+        start = pl.multiple_of((narrow ^ j) * block, block)
+        out = jnp.dot(
+            hid_ref[...], wd_ref[:, pl.ds(start, block)], preferred_element_type=jnp.float32
+        )
         target = send_ref if j & 1 else keep_ref
         target[:, (j >> 1) * block:((j >> 1) + 1) * block] = out.astype(target.dtype)
-        if i + down_ref.shape[0] < len(order):
-            fetch(i + down_ref.shape[0]).start()
 
 
 def local_small(
@@ -355,19 +346,20 @@
         + [pltpu.SMEM(given[0].shape, given[0].dtype)]
         + [pltpu.VMEM(g.shape, g.dtype) for g in given[1:]]
         + [pltpu.SemaphoreType.DMA((6,))],
-        cost_estimate=pl.CostEstimate(flops=2 * 10**10, bytes_accessed=10**8, transcendentals=0),
+        cost_estimate=pl.CostEstimate(flops=20000000000, bytes_accessed=1000000, transcendentals=0),
         compiler_params=pltpu.CompilerParams(vmem_limit_bytes=6 * 2**20),
     )(*[pltpu.with_memory_space_constraint(g, pltpu.HBM) for g in given])
     others = spread(payload)
-    keep, send = pl.pallas_call(
+    keep, send, mix = pl.pallas_call(
         project_kernel,
         out_shape=(
             jax.ShapeDtypeStruct((size * rows, half), jnp.float32),
             jax.ShapeDtypeStruct((size * rows, half), jnp.bfloat16),
+            jax.ShapeDtypeStruct((size * rows, 128), jnp.bfloat16),
         ),
         in_specs=[smem] + [vmem] * 6,
-        out_specs=(vmem, vmem),
-        cost_estimate=pl.CostEstimate(flops=2 * 10**10, bytes_accessed=10**8, transcendentals=0),
+        out_specs=(vmem, vmem, vmem),
+        cost_estimate=pl.CostEstimate(flops=30000000000, bytes_accessed=1000000, transcendentals=0),
         compiler_params=pltpu.CompilerParams(vmem_limit_bytes=6 * 2**20),
     )(where, payload, *others, w_out, turned)
     part = (keep + flip_permute(send, "narrow", 1).astype(jnp.float32)).astype(jnp.bfloat16)
@@ -378,32 +370,25 @@
     other = flip_permute(mine, "narrow", 1)
     weights = [
         pltpu.with_memory_space_constraint(w, pltpu.VMEM)
-        for w in (w_gate, w_up)
-    ] + [
-        pltpu.with_memory_space_constraint(w_down.reshape(experts * hidden, model), pltpu.HBM)
+        for w in (w_gate, w_up, w_down.reshape(experts * hidden, model))
     ]
     keep, send, own = pl.pallas_call(
         expert_kernel,
         out_shape=(
-            jax.ShapeDtypeStruct((size * rows, model // 2), jnp.float32),
-            jax.ShapeDtypeStruct((size * rows, model // 2), jnp.bfloat16),
-            jax.ShapeDtypeStruct((rows, columns), jnp.bfloat16),
+            pltpu.VMEM((size * rows, model // 2), jnp.float32),
+            pltpu.VMEM((size * rows, model // 2), jnp.bfloat16),
+            pltpu.VMEM((rows, columns), jnp.bfloat16),
         ),
-        in_specs=[smem] + [vmem] * 9 + [pl.BlockSpec(memory_space=pl.ANY)],
+        in_specs=[smem] + [vmem] * 7,
         out_specs=(vmem, vmem, vmem),
         scratch_shapes=[
             pltpu.VMEM((size * rows, model), jnp.bfloat16),
             pltpu.VMEM((size * rows, experts * hidden), jnp.bfloat16),
-            pltpu.VMEM((3, experts * hidden, columns), jnp.bfloat16),
-            pltpu.SemaphoreType.DMA((3,)),
         ],
-        compiler_params=pltpu.CompilerParams(vmem_limit_bytes=20 * 2**20),
+        compiler_params=pltpu.CompilerParams(vmem_limit_bytes=11 * 2**20),
     )(
         where,
-        mine,
-        other,
-        payload,
-        *others,
+        *[pltpu.with_memory_space_constraint(p, pltpu.VMEM) for p in (mine, other, mix)],
         norm_gain.reshape(1, model),
         *weights,
     )

time: 61.5 us -> 57 us (0.927)
  Pallas kernels: 15.4 us -> 10.9 us
    pallas_call x1, Pallas kernels: 12.6 us -> 7.98 us  [local_small(): pl.pallas_call(expert_kernel, out_shape=(pltpu.VMEM((size * rows, model /...]
where the time goes in v4:
time: 57 us; the launch traced here: 56.8 us
  waiting for transfers between devices  25.1 us (44%)
  starting transfers between devices  19.6 us (34%)
  Pallas kernels  10.9 us (19%)
  other arithmetic  0.89 us (2%)
    ppermute x14, waiting for transfers between devices, flip_permute(): return lax.ppermute(value, axis, [(i, i ^ mask) for i in range(size)])  25.1 us
    ppermute x14, starting transfers between devices, flip_permute(): return lax.ppermute(value, axis, [(i, i ^ mask) for i in range(size)])  18.9 us
    pallas_call x1, Pallas kernels, local_small(): pl.pallas_call(expert_kernel, out_shape=(pltpu.VMEM((size * rows, model /...  7.98 us
    pallas_call x1, Pallas kernels, local_small(): pl.pallas_call(attend_kernel, out_shape=jax.ShapeDtypeStruct((rows, depth...  2 us
  transfers between devices with their start and end apart: 15, of which 13 were waited for; matrix products, arithmetic and copies ran while one was open for 0% of the time, Pallas kernels for 0%

profile of v4, /device:TPU:0, one launch (start us, length us, event | category | flops | bytes accessed | tf_op | source)
XLA Modules:
  0.0 56.8 jit_solution(4143291505116936112)
XLA Ops:
  0.0 2.0 %shard_map.118.own_ref = bf16[32,1152]{1,0:T(8,128)(2,1)S(1)} custom-call(s32[2,16]{1,0:T(2,128)} %refs_0_.1, bf16[256,128]{1,0:T(8,128)(2,1)} %bitcast.29, bf16[2048,128]{1,0:T(8,128)(2,1)} %bitcast.27, bf16[2048,128]{1,0:T(8,128)(2,1)} %bitcast.28, s32[2,8,16]{2,1,0:T(8,128)} %bitcast.31, f32[2,8,16]{2,1,0:T(8,128)} %bitcast.32), custom_call_target="tpu_custom_call" | custom-call | flops 20000000000 | bytes 1000000 | tf_op jit(solution)/shard_map/pallas_call | solution.py:340
  2.0 5.1 %collective-permute-start.2 = (bf16[32,1152]{1,0:T(8,128)(2,1)S(1)}, bf16[32,1152]{1,0:T(8,128)(2,1)S(1)}, u32[]{:S(2)}, u32[]{:S(2)}) collective-permute-start(bf16[32,1152]{1,0:T(8,128)(2,1)S(1)} %shard_map.118.own_ref), channel_id=1, source_target_pairs={{0,12},{4,8},{8,4},{12,0},{1,13},{5,9},{9,5},{13,1},{2,14},{6,10},... | collective-permute-start | bytes 221192 | tf_op jit(solution)/shard_map/ppermute | solution.py:153
  7.1 0.6 %collective-permute-start = (bf16[32,1152]{1,0:T(8,128)(2,1)S(1)}, bf16[32,1152]{1,0:T(8,128)(2,1)S(1)}, u32[]{:S(2)}, u32[]{:S(2)}) collective-permute-start(bf16[32,1152]{1,0:T(8,128)(2,1)S(1)} %shard_map.118.own_ref), channel_id=1, source_target_pairs={{0,4},{4,0},{8,12},{12,8},{1,5},{5,1},{9,13},{13,9},{2,6},{6,2},{1... | collective-permute-start | bytes 221192 | tf_op jit(solution)/shard_map/ppermute | solution.py:153
  7.8 0.7 %collective-permute-start.3 = (bf16[32,512]{1,0:T(8,128)(2,1)S(1)}, bf16[32,512]{1,0:T(8,128)(2,1)S(1)}, u32[]{:S(2)}, u32[]{:S(2)}) collective-permute-start(bf16[32,512]{1,0:T(8,128)(2,1)S(1)} %bitcast.30), channel_id=1, source_target_pairs={{0,0},{1,4},{2,8},{3,12},{4,1},{5,5},{6,9},{7,13},{8,2},{9,6},{10,... | collective-permute-start | bytes 98312 | tf_op jit(solution)/shard_map/ppermute | solution.py:327
  8.6 1.2 %collective-permute-done.2.got3_ref = bf16[32,1152]{1,0:T(8,128)(2,1)S(1)} collective-permute-done((bf16[32,1152]{1,0:T(8,128)(2,1)S(1)}, bf16[32,1152]{1,0:T(8,128)(2,1)S(1)}, u32[]{:S(2)}, u32[]{:S(2)}) %collective-permute-start.2) | collective-permute-done | bytes 73760 | tf_op jit(solution)/shard_map/ppermute | solution.py:153
  9.9 3.5 %collective-permute-done.1.got2_ref = bf16[32,1152]{1,0:T(8,128)(2,1)S(1)} collective-permute-done((bf16[32,1152]{1,0:T(8,128)(2,1)S(1)}, bf16[32,1152]{1,0:T(8,128)(2,1)S(1)}, u32[]{:S(2)}, u32[]{:S(2)}) %collective-permute-start.1) | collective-permute-done | bytes 73760 | tf_op jit(solution)/shard_map/ppermute | solution.py:153
  13.4 0.9 %shard_map.119 = (f32[128,256]{1,0:T(8,128)S(1)}, bf16[128,256]{1,0:T(8,128)(2,1)S(1)}, bf16[128,128]{1,0:T(8,128)(2,1)S(1)}) custom-call(s32[2]{0:T(128)S(1)} %pad_add_fusion.where_ref, bf16[32,1152]{1,0:T(8,128)(2,1)S(1)} %shard_map.118.own_ref, bf16[32,1152]{1,0:T(8,128)(2,1)S(1)} %collective-permute-done.got1_ref, ...), custom_call_target="tpu_custom_call" | custom-call | flops 30000001024 | bytes 1000000 | tf_op jit(solution)/shard_map/pallas_call | solution.py:353
  14.5 1.2 %collective-permute-done.4 = bf16[128,256]{1,0:T(8,128)(2,1)S(1)} collective-permute-done((bf16[128,256]{1,0:T(8,128)(2,1)S(1)}, bf16[128,256]{1,0:T(8,128)(2,1)S(1)}, u32[]{:S(2)}, u32[]{:S(2)}) %collective-permute-start.4) | collective-permute-done | bytes 65568 | tf_op jit(solution)/shard_map/ppermute | solution.py:153
  15.7 3.8 %collective-permute-start.5 = (bf16[128,256]{1,0:T(8,128)(2,1)S(1)}, bf16[128,256]{1,0:T(8,128)(2,1)S(1)}, u32[]{:S(2)}, u32[]{:S(2)}) collective-permute-start(bf16[128,256]{1,0:T(8,128)(2,1)S(1)} %add_convert_fusion.1), channel_id=1, source_target_pairs={{0,2},{1,3},{2,0},{3,1},{4,6},{5,7},{6,4},{7,5},{8,10},{9,11},{10,... | collective-permute-start | bytes 196616 | tf_op jit(solution)/shard_map/ppermute | solution.py:153
  19.4 2.4 %collective-permute-done.5 = bf16[128,256]{1,0:T(8,128)(2,1)S(1)} collective-permute-done((bf16[128,256]{1,0:T(8,128)(2,1)S(1)}, bf16[128,256]{1,0:T(8,128)(2,1)S(1)}, u32[]{:S(2)}, u32[]{:S(2)}) %collective-permute-start.5) | collective-permute-done | bytes 65568 | tf_op jit(solution)/shard_map/ppermute | solution.py:153
  21.9 4.2 %collective-permute-start.8 = (bf16[128,256]{1,0:T(8,128)(2,1)S(1)}, bf16[128,256]{1,0:T(8,128)(2,1)S(1)}, u32[]{:S(2)}, u32[]{:S(2)}) collective-permute-start(bf16[128,256]{1,0:T(8,128)(2,1)S(1)} %add_convert_fusion), channel_id=1, source_target_pairs={{0,12},{4,8},{8,4},{12,0},{1,13},{5,9},{9,5},{13,1},{2,14},{6,10},... | collective-permute-start | bytes 196616 | tf_op jit(solution)/shard_map/ppermute | solution.py:153
  26.1 0.6 %collective-permute-start.6 = (bf16[128,256]{1,0:T(8,128)(2,1)S(1)}, bf16[128,256]{1,0:T(8,128)(2,1)S(1)}, u32[]{:S(2)}, u32[]{:S(2)}) collective-permute-start(bf16[128,256]{1,0:T(8,128)(2,1)S(1)} %add_convert_fusion), channel_id=1, source_target_pairs={{0,4},{4,0},{8,12},{12,8},{1,5},{5,1},{9,13},{13,9},{2,6},{6,2},{1... | collective-permute-start | bytes 196616 | tf_op jit(solution)/shard_map/ppermute | solution.py:153
  26.8 1.7 %collective-permute-done.8 = bf16[128,256]{1,0:T(8,128)(2,1)S(1)} collective-permute-done((bf16[128,256]{1,0:T(8,128)(2,1)S(1)}, bf16[128,256]{1,0:T(8,128)(2,1)S(1)}, u32[]{:S(2)}, u32[]{:S(2)}) %collective-permute-start.8) | collective-permute-done | bytes 65568 | tf_op jit(solution)/shard_map/ppermute | solution.py:153
  28.5 2.9 %collective-permute-done.7 = bf16[128,256]{1,0:T(8,128)(2,1)S(1)} collective-permute-done((bf16[128,256]{1,0:T(8,128)(2,1)S(1)}, bf16[128,256]{1,0:T(8,128)(2,1)S(1)}, u32[]{:S(2)}, u32[]{:S(2)}) %collective-permute-start.7) | collective-permute-done | bytes 65568 | tf_op jit(solution)/shard_map/ppermute | solution.py:153
  31.6 1.5 %collective-permute-done.9.other_ref = bf16[4,128,256]{2,1,0:T(8,128)(2,1)S(1)} collective-permute-done((bf16[4,128,256]{2,1,0:T(8,128)(2,1)S(1)}, bf16[4,128,256]{2,1,0:T(8,128)(2,1)S(1)}, u32[]{:S(2)}, u32[]{:S(2)}) %collective-permute-start.9) | collective-permute-done | bytes 262176 | tf_op jit(solution)/shard_map/ppermute | solution.py:153
  33.2 8.0 %shard_map.120 = (f32[128,1024]{1,0:T(8,128)S(1)}, bf16[128,1024]{1,0:T(8,128)(2,1)S(1)}, bf16[32,512]{1,0:T(8,128)(2,1)S(1)}) custom-call(s32[2]{0:T(128)} %copy-done, bf16[4,128,256]{2,1,0:T(8,128)(2,1)S(1)} %pad_maximum_fusion.mine_ref, bf16[4,128,256]{2,1,0:T(8,128)(2,1)S(1)} %collective-permute-done.9.other_ref, ...), custom_call_target="tpu_custom_call" | custom-call | tf_op jit(solution)/shard_map/pallas_call | solution.py:375
  41.4 1.4 %collective-permute-done.10 = bf16[128,1024]{1,0:T(8,128)(2,1)S(1)} collective-permute-done((bf16[128,1024]{1,0:T(8,128)(2,1)S(1)}, bf16[128,1024]{1,0:T(8,128)(2,1)S(1)}, u32[]{:S(2)}, u32[]{:S(2)}) %collective-permute-start.10) | collective-permute-done | bytes 262176 | tf_op jit(solution)/shard_map/ppermute | solution.py:153
  43.0 1.9 %collective-permute-start.11 = (bf16[32,1024]{1,0:T(8,128)(2,1)S(1)}, bf16[32,1024]{1,0:T(8,128)(2,1)S(1)}, u32[]{:S(2)}, u32[]{:S(2)}) collective-permute-start(bf16[32,1024]{1,0:T(8,128)(2,1)S(1)} %get-tuple-element.19), channel_id=1, source_target_pairs={{0,8},{4,12},{8,0},{12,4},{1,9},{5,13},{9,1},{13,5},{2,10},{6,14},... | collective-permute-start | bytes 196616 | tf_op jit(solution)/shard_map/ppermute | solution.py:153
  44.8 1.1 %collective-permute-start.13 = (bf16[32,1024]{1,0:T(8,128)(2,1)S(1)}, bf16[32,1024]{1,0:T(8,128)(2,1)S(1)}, u32[]{:S(2)}, u32[]{:S(2)}) collective-permute-start(bf16[32,1024]{1,0:T(8,128)(2,1)S(1)} %get-tuple-element.20), channel_id=1, source_target_pairs={{0,12},{4,8},{8,4},{12,0},{1,13},{5,9},{9,5},{13,1},{2,14},{6,10},... | collective-permute-start | bytes 196616 | tf_op jit(solution)/shard_map/ppermute | solution.py:153
  46.5 3.9 %collective-permute-done.11 = bf16[32,1024]{1,0:T(8,128)(2,1)S(1)} collective-permute-done((bf16[32,1024]{1,0:T(8,128)(2,1)S(1)}, bf16[32,1024]{1,0:T(8,128)(2,1)S(1)}, u32[]{:S(2)}, u32[]{:S(2)}) %collective-permute-start.11) | collective-permute-done | bytes 65568 | tf_op jit(solution)/shard_map/ppermute | solution.py:153
  50.4 0.9 %collective-permute-done.13 = bf16[32,1024]{1,0:T(8,128)(2,1)S(1)} collective-permute-done((bf16[32,1024]{1,0:T(8,128)(2,1)S(1)}, bf16[32,1024]{1,0:T(8,128)(2,1)S(1)}, u32[]{:S(2)}, u32[]{:S(2)}) %collective-permute-start.13) | collective-permute-done | bytes 65568 | tf_op jit(solution)/shard_map/ppermute | solution.py:153
  51.2 0.9 %collective-permute-done.12 = bf16[32,1024]{1,0:T(8,128)(2,1)S(1)} collective-permute-done((bf16[32,1024]{1,0:T(8,128)(2,1)S(1)}, bf16[32,1024]{1,0:T(8,128)(2,1)S(1)}, u32[]{:S(2)}, u32[]{:S(2)}) %collective-permute-start.12) | collective-permute-done | bytes 65568 | tf_op jit(solution)/shard_map/ppermute | solution.py:153
  52.8 3.4 %collective-permute-done.14 = bf16[32,512]{1,0:T(8,128)(2,1)S(1)} collective-permute-done((bf16[32,512]{1,0:T(8,128)(2,1)S(1)}, bf16[32,512]{1,0:T(8,128)(2,1)S(1)}, u32[]{:S(2)}, u32[]{:S(2)}) %collective-permute-start.14) | collective-permute-done | bytes 32800 | tf_op jit(solution)/shard_map/ppermute | solution.py:153
  56.2 0.6 %fusion.3 = bf16[32,512]{1,0:T(8,128)(2,1)} fusion(f32[32,1024]{1,0:T(8,128)S(1)} %fusion.1, bf16[32,512]{1,0:T(8,128)(2,1)S(1)} %collective-permute-done.14, bf16[32,512]{1,0:T(8,128)(2,1)S(1)} %get-tuple-element.14), kind=kLoop, calls=%fused_computation.10 | loop fusion | flops 81920 | bytes 163840 | tf_op jit(solution)/shard_map/convert_element_type | solution.py:403
  (51 shorter events, 2.0 us)
Async XLA Ops:
  2.0 7.9 %collective-permute-start.2 = (bf16[32,1152]{1,0:T(8,128)(2,1)S(1)}, bf16[32,1152]{1,0:T(8,128)(2,1)S(1)}, u32[]{:S(2)}, u32[]{:S(2)}) collective-permute-start(bf16[32,1152]{1,0:T(8,128)(2,1)S(1)} %shard_map.118.own_ref), channel_id=1, source_target_pairs={{0,12},{4,8},{8,4},{12,0},{1,13},{5,9},{9,5},{13,1},{2,14},{6,10},... | collective-permute-start | bytes 221192 | tf_op jit(solution)/shard_map/ppermute | solution.py:153
  7.1 6.3 %collective-permute-start.1 = (bf16[32,1152]{1,0:T(8,128)(2,1)S(1)}, bf16[32,1152]{1,0:T(8,128)(2,1)S(1)}, u32[]{:S(2)}, u32[]{:S(2)}) collective-permute-start(bf16[32,1152]{1,0:T(8,128)(2,1)S(1)} %shard_map.118.own_ref), channel_id=1, source_target_pairs={{0,8},{4,12},{8,0},{12,4},{1,9},{5,13},{9,1},{13,5},{2,10},{6,14},... | collective-permute-start | bytes 221192 | tf_op jit(solution)/shard_map/ppermute | solution.py:153
  7.1 6.3 %collective-permute-start = (bf16[32,1152]{1,0:T(8,128)(2,1)S(1)}, bf16[32,1152]{1,0:T(8,128)(2,1)S(1)}, u32[]{:S(2)}, u32[]{:S(2)}) collective-permute-start(bf16[32,1152]{1,0:T(8,128)(2,1)S(1)} %shard_map.118.own_ref), channel_id=1, source_target_pairs={{0,4},{4,0},{8,12},{12,8},{1,5},{5,1},{9,13},{13,9},{2,6},{6,2},{1... | collective-permute-start | bytes 221192 | tf_op jit(solution)/shard_map/ppermute | solution.py:153
  7.8 0.9 %collective-permute-start.3 = (bf16[32,512]{1,0:T(8,128)(2,1)S(1)}, bf16[32,512]{1,0:T(8,128)(2,1)S(1)}, u32[]{:S(2)}, u32[]{:S(2)}) collective-permute-start(bf16[32,512]{1,0:T(8,128)(2,1)S(1)} %bitcast.30), channel_id=1, source_target_pairs={{0,0},{1,4},{2,8},{3,12},{4,1},{5,5},{6,9},{7,13},{8,2},{9,6},{10,... | collective-permute-start | bytes 98312 | tf_op jit(solution)/shard_map/ppermute | solution.py:327
  8.4 24.7 %slice-start = ((s8[16777216]{0:T(1024)(128)(4,1)}), s8[4194304]{0:T(1024)(128)(4,1)S(1)}, s32[]{:S(2)}) async-start(s8[16777216]{0:T(1024)(128)(4,1)} %bitcast.15), calls=%async_computation | async-start | bytes 8388608
  8.5 24.7 %slice-start.4 = ((s8[16777216]{0:T(1024)(128)(4,1)}), s8[4194304]{0:T(1024)(128)(4,1)S(1)}, s32[]{:S(2)}) async-start(s8[16777216]{0:T(1024)(128)(4,1)} %bitcast.17), calls=%async_computation.4 | async-start | bytes 8388608
  8.5 24.7 %slice-start.8 = ((s8[16777216]{0:T(1024)(128)(4,1)}), s8[4194304]{0:T(1024)(128)(4,1)S(1)}, s32[]{:S(2)}) async-start(s8[16777216]{0:T(1024)(128)(4,1)} %bitcast.19), calls=%async_computation.8 | async-start | bytes 8388608
  8.6 24.6 %slice-start.3 = ((s8[16777216]{0:T(1024)(128)(4,1)}), s8[4194304]{0:T(1024)(128)(4,1)S(1)}, s32[]{:S(2)}) async-start(s8[16777216]{0:T(1024)(128)(4,1)} %bitcast.15), calls=%async_computation.3 | async-start | bytes 8388608
  8.6 24.6 %slice-start.5 = ((s8[16777216]{0:T(1024)(128)(4,1)}), s8[4194304]{0:T(1024)(128)(4,1)S(1)}, s32[]{:S(2)}) async-start(s8[16777216]{0:T(1024)(128)(4,1)} %bitcast.17), calls=%async_computation.5 | async-start | bytes 8388608
  8.6 24.6 %slice-start.6 = ((s8[16777216]{0:T(1024)(128)(4,1)}), s8[4194304]{0:T(1024)(128)(4,1)S(1)}, s32[]{:S(2)}) async-start(s8[16777216]{0:T(1024)(128)(4,1)} %bitcast.17), calls=%async_computation.6 | async-start | bytes 8388608
  8.6 24.6 %slice-start.7 = ((s8[16777216]{0:T(1024)(128)(4,1)}), s8[4194304]{0:T(1024)(128)(4,1)S(1)}, s32[]{:S(2)}) async-start(s8[16777216]{0:T(1024)(128)(4,1)} %bitcast.17), calls=%async_computation.7 | async-start | bytes 8388608
  8.6 24.6 %slice-start.9 = ((s8[16777216]{0:T(1024)(128)(4,1)}), s8[4194304]{0:T(1024)(128)(4,1)S(1)}, s32[]{:S(2)}) async-start(s8[16777216]{0:T(1024)(128)(4,1)} %bitcast.19), calls=%async_computation.9 | async-start | bytes 8388608
  8.6 24.6 %slice-start.10 = ((s8[16777216]{0:T(1024)(128)(4,1)}), s8[4194304]{0:T(1024)(128)(4,1)S(1)}, s32[]{:S(2)}) async-start(s8[16777216]{0:T(1024)(128)(4,1)} %bitcast.19), calls=%async_computation.10 | async-start | bytes 8388608
  14.3 1.3 %collective-permute-start.4 = (bf16[128,256]{1,0:T(8,128)(2,1)S(1)}, bf16[128,256]{1,0:T(8,128)(2,1)S(1)}, u32[]{:S(2)}, u32[]{:S(2)}) collective-permute-start(bf16[128,256]{1,0:T(8,128)(2,1)S(1)} %get-tuple-element.12), channel_id=1, source_target_pairs={{0,1},{1,0},{2,3},{3,2},{4,5},{5,4},{6,7},{7,6},{8,9},{9,8},{10,11... | collective-permute-start | bytes 196616 | tf_op jit(solution)/shard_map/ppermute | solution.py:153
  15.7 6.2 %collective-permute-start.5 = (bf16[128,256]{1,0:T(8,128)(2,1)S(1)}, bf16[128,256]{1,0:T(8,128)(2,1)S(1)}, u32[]{:S(2)}, u32[]{:S(2)}) collective-permute-start(bf16[128,256]{1,0:T(8,128)(2,1)S(1)} %add_convert_fusion.1), channel_id=1, source_target_pairs={{0,2},{1,3},{2,0},{3,1},{4,6},{5,7},{6,4},{7,5},{8,10},{9,11},{10,... | collective-permute-start | bytes 196616 | tf_op jit(solution)/shard_map/ppermute | solution.py:153
  21.9 6.6 %collective-permute-start.8 = (bf16[128,256]{1,0:T(8,128)(2,1)S(1)}, bf16[128,256]{1,0:T(8,128)(2,1)S(1)}, u32[]{:S(2)}, u32[]{:S(2)}) collective-permute-start(bf16[128,256]{1,0:T(8,128)(2,1)S(1)} %add_convert_fusion), channel_id=1, source_target_pairs={{0,12},{4,8},{8,4},{12,0},{1,13},{5,9},{9,5},{13,1},{2,14},{6,10},... | collective-permute-start | bytes 196616 | tf_op jit(solution)/shard_map/ppermute | solution.py:153
  26.1 5.3 %collective-permute-start.7 = (bf16[128,256]{1,0:T(8,128)(2,1)S(1)}, bf16[128,256]{1,0:T(8,128)(2,1)S(1)}, u32[]{:S(2)}, u32[]{:S(2)}) collective-permute-start(bf16[128,256]{1,0:T(8,128)(2,1)S(1)} %add_convert_fusion), channel_id=1, source_target_pairs={{0,8},{4,12},{8,0},{12,4},{1,9},{5,13},{9,1},{13,5},{2,10},{6,14},... | collective-permute-start | bytes 196616 | tf_op jit(solution)/shard_map/ppermute | solution.py:153
  26.1 5.4 %collective-permute-start.6 = (bf16[128,256]{1,0:T(8,128)(2,1)S(1)}, bf16[128,256]{1,0:T(8,128)(2,1)S(1)}, u32[]{:S(2)}, u32[]{:S(2)}) collective-permute-start(bf16[128,256]{1,0:T(8,128)(2,1)S(1)} %add_convert_fusion), channel_id=1, source_target_pairs={{0,4},{4,0},{8,12},{12,8},{1,5},{5,1},{9,13},{13,9},{2,6},{6,2},{1... | collective-permute-start | bytes 196616 | tf_op jit(solution)/shard_map/ppermute | solution.py:153
  31.5 1.6 %collective-permute-start.9 = (bf16[4,128,256]{2,1,0:T(8,128)(2,1)S(1)}, bf16[4,128,256]{2,1,0:T(8,128)(2,1)S(1)}, u32[]{:S(2)}, u32[]{:S(2)}) collective-permute-start(bf16[4,128,256]{2,1,0:T(8,128)(2,1)S(1)} %pad_maximum_fusion.mine_ref), channel_id=1, source_target_pairs={{0,1},{1,0},{2,3},{3,2},{4,5},{5,4},{6,7},{7,6},{8,9},{9,8},{10,11... | collective-permute-start | bytes 786440 | tf_op jit(solution)/shard_map/ppermute | solution.py:153
  41.2 1.6 %collective-permute-start.10 = (bf16[128,1024]{1,0:T(8,128)(2,1)S(1)}, bf16[128,1024]{1,0:T(8,128)(2,1)S(1)}, u32[]{:S(2)}, u32[]{:S(2)}) collective-permute-start(bf16[128,1024]{1,0:T(8,128)(2,1)S(1)} %get-tuple-element.16), channel_id=1, source_target_pairs={{0,1},{1,0},{2,3},{3,2},{4,5},{5,4},{6,7},{7,6},{8,9},{9,8},{10,11... | collective-permute-start | bytes 786440 | tf_op jit(solution)/shard_map/ppermute | solution.py:153
  43.0 7.4 %collective-permute-start.11 = (bf16[32,1024]{1,0:T(8,128)(2,1)S(1)}, bf16[32,1024]{1,0:T(8,128)(2,1)S(1)}, u32[]{:S(2)}, u32[]{:S(2)}) collective-permute-start(bf16[32,1024]{1,0:T(8,128)(2,1)S(1)} %get-tuple-element.19), channel_id=1, source_target_pairs={{0,8},{4,12},{8,0},{12,4},{1,9},{5,13},{9,1},{13,5},{2,10},{6,14},... | collective-permute-start | bytes 196616 | tf_op jit(solution)/shard_map/ppermute | solution.py:153
  44.8 6.4 %collective-permute-start.13 = (bf16[32,1024]{1,0:T(8,128)(2,1)S(1)}, bf16[32,1024]{1,0:T(8,128)(2,1)S(1)}, u32[]{:S(2)}, u32[]{:S(2)}) collective-permute-start(bf16[32,1024]{1,0:T(8,128)(2,1)S(1)} %get-tuple-element.20), channel_id=1, source_target_pairs={{0,12},{4,8},{8,4},{12,0},{1,13},{5,9},{9,5},{13,1},{2,14},{6,10},... | collective-permute-start | bytes 196616 | tf_op jit(solution)/shard_map/ppermute | solution.py:153
  45.9 6.3 %collective-permute-start.12 = (bf16[32,1024]{1,0:T(8,128)(2,1)S(1)}, bf16[32,1024]{1,0:T(8,128)(2,1)S(1)}, u32[]{:S(2)}, u32[]{:S(2)}) collective-permute-start(bf16[32,1024]{1,0:T(8,128)(2,1)S(1)} %get-tuple-element.21), channel_id=1, source_target_pairs={{0,4},{4,0},{8,12},{12,8},{1,5},{5,1},{9,13},{13,9},{2,6},{6,2},{1... | collective-permute-start | bytes 196616 | tf_op jit(solution)/shard_map/ppermute | solution.py:153
  52.2 4.0 %collective-permute-start.14 = (bf16[32,512]{1,0:T(8,128)(2,1)S(1)}, bf16[32,512]{1,0:T(8,128)(2,1)S(1)}, u32[]{:S(2)}, u32[]{:S(2)}) collective-permute-start(bf16[32,512]{1,0:T(8,128)(2,1)S(1)} %slice.52), channel_id=1, source_target_pairs={{0,2},{1,3},{2,0},{3,1},{4,6},{5,7},{6,4},{7,5},{8,10},{9,11},{10,... | collective-permute-start | bytes 98312 | tf_op jit(solution)/shard_map/ppermute | solution.py:153
  (6 other events, 100.7 us)

commit v5 on v4

--- a/solution.py
+++ b/solution.py
@@ -291,13 +291,14 @@
         share = jnp.dot(mix, pick, preferred_element_type=jnp.float32)
         hidden = gate / (1.0 + jnp.exp(-gate)) * upper * share
         hid_ref[:, e * width:(e + 1) * width] = hidden.astype(jnp.bfloat16)
-    for j in (1, 3, 0, 2):
-        start = pl.multiple_of((narrow ^ j) * block, block)
-        out = jnp.dot(
-            hid_ref[...], wd_ref[:, pl.ds(start, block)], preferred_element_type=jnp.float32
-        )
-        target = send_ref if j & 1 else keep_ref
-        target[:, (j >> 1) * block:((j >> 1) + 1) * block] = out.astype(target.dtype)
+    side = (narrow >> 1) ^ core
+    for target, place in ((send_ref, 1 - side), (keep_ref, side)):
+        for k in range(2):
+            start = pl.multiple_of((2 * place + k) * block, block)
+            out = jnp.dot(
+                hid_ref[...], wd_ref[:, pl.ds(start, block)], preferred_element_type=jnp.float32
+            )
+            target[:, k * block:(k + 1) * block] = out.astype(target.dtype)
 
 
 def local_small(
@@ -392,14 +393,22 @@
         norm_gain.reshape(1, model),
         *weights,
     )
-    total = keep + flip_permute(send, "narrow", 1).astype(jnp.float32)
+    total = (keep + flip_permute(send, "narrow", 1).astype(jnp.float32)).astype(jnp.bfloat16)
     total = total.reshape(size, rows, model // 2)
-    leave = total[1:].astype(jnp.bfloat16)
-    summed = total[0]
-    for s in (2, 1, 3):
-        summed = summed + flip_permute(leave[s - 1], "wide", s).astype(jnp.float32)
-    cross = flip_permute(summed[:, columns:].astype(jnp.bfloat16), "narrow", 2)
-    result = own.astype(jnp.float32) + summed[:, :columns] + cross.astype(jnp.float32)
+    devices = range(size * size)
+    got = [
+        lax.ppermute(
+            total[s],
+            ("wide", "narrow"),
+            [(i, i ^ (s * size) ^ (2 if i & 1 else 0)) for i in devices],
+        ).astype(jnp.float32)
+        for s in (2, 1, 3, 0)
+    ]
+    summed = got[0] + got[1] + got[2] + got[3]
+    first = (narrow & 1) == 0
+    left, right = summed[:, :columns], summed[:, columns:]
+    cross = flip_permute(jnp.where(first, right, left).astype(jnp.bfloat16), "narrow", 1)
+    result = own.astype(jnp.float32) + jnp.where(first, left, right) + cross.astype(jnp.float32)
     return result.astype(jnp.bfloat16).reshape(micro, per_micro, columns)
 
 

time: 57 us -> 55.4 us (0.972)
  waiting for transfers between devices: 25.1 us -> 21.4 us
  starting transfers between devices: 19.6 us -> 21.8 us
    ppermute x14 -> x11, waiting for transfers between devices: 25.1 us -> 16.9 us  [flip_permute(): return lax.ppermute(value, axis, [(i, i ^ mask) for i in range(size)])]
    ppermute x0 -> x4, waiting for transfers between devices: none -> 4.5 us  [local_small(): lax.ppermute(total[s], ('wide', 'narrow'), [(i, i ^ s * size ^ (2 if i &...]
    ppermute x0 -> x4, starting transfers between devices: none -> 4.27 us  [local_small(): lax.ppermute(total[s], ('wide', 'narrow'), [(i, i ^ s * size ^ (2 if i &...]
    ppermute x14 -> x11, starting transfers between devices: 18.9 us -> 16.8 us  [flip_permute(): return lax.ppermute(value, axis, [(i, i ^ mask) for i in range(size)])]
  transfers between devices with their start and end apart: 15 -> 16, of which waited for: 13 -> 12; matrix products, arithmetic and copies ran while one was open for 0% -> 0% of each run, Pallas kernels for 0% -> 0%
where the time goes in v5:
time: 55.4 us; the launch traced here: 55.2 us
  starting transfers between devices  21.8 us (39%)
  waiting for transfers between devices  21.4 us (39%)
  Pallas kernels  10.8 us (19%)
  other arithmetic  0.88 us (2%)
    ppermute x11, waiting for transfers between devices, flip_permute(): return lax.ppermute(value, axis, [(i, i ^ mask) for i in range(size)])  16.9 us
    ppermute x11, starting transfers between devices, flip_permute(): return lax.ppermute(value, axis, [(i, i ^ mask) for i in range(size)])  16.8 us
    pallas_call x1, Pallas kernels, local_small(): pl.pallas_call(expert_kernel, out_shape=(pltpu.VMEM((size * rows, model /...  7.94 us
    ppermute x4, waiting for transfers between devices, local_small(): lax.ppermute(total[s], ('wide', 'narrow'), [(i, i ^ s * size ^ (2 if i &...  4.5 us
    ppermute x4, starting transfers between devices, local_small(): lax.ppermute(total[s], ('wide', 'narrow'), [(i, i ^ s * size ^ (2 if i &...  4.27 us
    pallas_call x1, Pallas kernels, local_small(): pl.pallas_call(attend_kernel, out_shape=jax.ShapeDtypeStruct((rows, depth...  2 us
  transfers between devices with their start and end apart: 16, of which 12 were waited for; matrix products, arithmetic and copies ran while one was open for 0% of the time, Pallas kernels for 0%

profile of v5, /device:TPU:0, one launch (start us, length us, event | category | flops | bytes accessed | tf_op | source)
XLA Modules:
  0.0 55.2 jit_solution(461459274945623986)
XLA Ops:
  0.0 2.0 %shard_map.118.own_ref = bf16[32,1152]{1,0:T(8,128)(2,1)S(1)} custom-call(s32[2,16]{1,0:T(2,128)} %refs_0_.1, bf16[256,128]{1,0:T(8,128)(2,1)} %bitcast.29, bf16[2048,128]{1,0:T(8,128)(2,1)} %bitcast.27, bf16[2048,128]{1,0:T(8,128)(2,1)} %bitcast.28, s32[2,8,16]{2,1,0:T(8,128)} %bitcast.31, f32[2,8,16]{2,1,0:T(8,128)} %bitcast.32), custom_call_target="tpu_custom_call" | custom-call | flops 20000000000 | bytes 1000000 | tf_op jit(solution)/shard_map/pallas_call | solution.py:341
  2.0 5.1 %collective-permute-start.2 = (bf16[32,1152]{1,0:T(8,128)(2,1)S(1)}, bf16[32,1152]{1,0:T(8,128)(2,1)S(1)}, u32[]{:S(2)}, u32[]{:S(2)}) collective-permute-start(bf16[32,1152]{1,0:T(8,128)(2,1)S(1)} %shard_map.118.own_ref), channel_id=1, source_target_pairs={{0,12},{4,8},{8,4},{12,0},{1,13},{5,9},{9,5},{13,1},{2,14},{6,10},... | collective-permute-start | bytes 221192 | tf_op jit(solution)/shard_map/ppermute | solution.py:153
  7.1 0.6 %collective-permute-start = (bf16[32,1152]{1,0:T(8,128)(2,1)S(1)}, bf16[32,1152]{1,0:T(8,128)(2,1)S(1)}, u32[]{:S(2)}, u32[]{:S(2)}) collective-permute-start(bf16[32,1152]{1,0:T(8,128)(2,1)S(1)} %shard_map.118.own_ref), channel_id=1, source_target_pairs={{0,4},{4,0},{8,12},{12,8},{1,5},{5,1},{9,13},{13,9},{2,6},{6,2},{1... | collective-permute-start | bytes 221192 | tf_op jit(solution)/shard_map/ppermute | solution.py:153
  7.8 0.7 %collective-permute-start.3 = (bf16[32,512]{1,0:T(8,128)(2,1)S(1)}, bf16[32,512]{1,0:T(8,128)(2,1)S(1)}, u32[]{:S(2)}, u32[]{:S(2)}) collective-permute-start(bf16[32,512]{1,0:T(8,128)(2,1)S(1)} %bitcast.30), channel_id=1, source_target_pairs={{0,0},{1,4},{2,8},{3,12},{4,1},{5,5},{6,9},{7,13},{8,2},{9,6},{10,... | collective-permute-start | bytes 98312 | tf_op jit(solution)/shard_map/ppermute | solution.py:328
  8.7 1.2 %collective-permute-done.2.got3_ref = bf16[32,1152]{1,0:T(8,128)(2,1)S(1)} collective-permute-done((bf16[32,1152]{1,0:T(8,128)(2,1)S(1)}, bf16[32,1152]{1,0:T(8,128)(2,1)S(1)}, u32[]{:S(2)}, u32[]{:S(2)}) %collective-permute-start.2) | collective-permute-done | bytes 73760 | tf_op jit(solution)/shard_map/ppermute | solution.py:153
  9.9 3.5 %collective-permute-done.1.got2_ref = bf16[32,1152]{1,0:T(8,128)(2,1)S(1)} collective-permute-done((bf16[32,1152]{1,0:T(8,128)(2,1)S(1)}, bf16[32,1152]{1,0:T(8,128)(2,1)S(1)}, u32[]{:S(2)}, u32[]{:S(2)}) %collective-permute-start.1) | collective-permute-done | bytes 73760 | tf_op jit(solution)/shard_map/ppermute | solution.py:153
  13.4 0.9 %shard_map.119 = (f32[128,256]{1,0:T(8,128)S(1)}, bf16[128,256]{1,0:T(8,128)(2,1)S(1)}, bf16[128,128]{1,0:T(8,128)(2,1)S(1)}) custom-call(s32[2]{0:T(128)S(1)} %pad_add_fusion.where_ref, bf16[32,1152]{1,0:T(8,128)(2,1)S(1)} %shard_map.118.own_ref, bf16[32,1152]{1,0:T(8,128)(2,1)S(1)} %collective-permute-done.got1_ref, ...), custom_call_target="tpu_custom_call" | custom-call | flops 30000001024 | bytes 1000000 | tf_op jit(solution)/shard_map/pallas_call | solution.py:354
  14.5 1.2 %collective-permute-done.4 = bf16[128,256]{1,0:T(8,128)(2,1)S(1)} collective-permute-done((bf16[128,256]{1,0:T(8,128)(2,1)S(1)}, bf16[128,256]{1,0:T(8,128)(2,1)S(1)}, u32[]{:S(2)}, u32[]{:S(2)}) %collective-permute-start.4) | collective-permute-done | bytes 65568 | tf_op jit(solution)/shard_map/ppermute | solution.py:153
  15.7 3.8 %collective-permute-start.5 = (bf16[128,256]{1,0:T(8,128)(2,1)S(1)}, bf16[128,256]{1,0:T(8,128)(2,1)S(1)}, u32[]{:S(2)}, u32[]{:S(2)}) collective-permute-start(bf16[128,256]{1,0:T(8,128)(2,1)S(1)} %add_convert_fusion.2), channel_id=1, source_target_pairs={{0,2},{1,3},{2,0},{3,1},{4,6},{5,7},{6,4},{7,5},{8,10},{9,11},{10,... | collective-permute-start | bytes 196616 | tf_op jit(solution)/shard_map/ppermute | solution.py:153
  19.4 2.4 %collective-permute-done.5 = bf16[128,256]{1,0:T(8,128)(2,1)S(1)} collective-permute-done((bf16[128,256]{1,0:T(8,128)(2,1)S(1)}, bf16[128,256]{1,0:T(8,128)(2,1)S(1)}, u32[]{:S(2)}, u32[]{:S(2)}) %collective-permute-start.5) | collective-permute-done | bytes 65568 | tf_op jit(solution)/shard_map/ppermute | solution.py:153
  21.9 4.2 %collective-permute-start.8 = (bf16[128,256]{1,0:T(8,128)(2,1)S(1)}, bf16[128,256]{1,0:T(8,128)(2,1)S(1)}, u32[]{:S(2)}, u32[]{:S(2)}) collective-permute-start(bf16[128,256]{1,0:T(8,128)(2,1)S(1)} %add_convert_fusion.1), channel_id=1, source_target_pairs={{0,12},{4,8},{8,4},{12,0},{1,13},{5,9},{9,5},{13,1},{2,14},{6,10},... | collective-permute-start | bytes 196616 | tf_op jit(solution)/shard_map/ppermute | solution.py:153
  26.1 0.6 %collective-permute-start.6 = (bf16[128,256]{1,0:T(8,128)(2,1)S(1)}, bf16[128,256]{1,0:T(8,128)(2,1)S(1)}, u32[]{:S(2)}, u32[]{:S(2)}) collective-permute-start(bf16[128,256]{1,0:T(8,128)(2,1)S(1)} %add_convert_fusion.1), channel_id=1, source_target_pairs={{0,4},{4,0},{8,12},{12,8},{1,5},{5,1},{9,13},{13,9},{2,6},{6,2},{1... | collective-permute-start | bytes 196616 | tf_op jit(solution)/shard_map/ppermute | solution.py:153
  26.8 1.7 %collective-permute-done.8 = bf16[128,256]{1,0:T(8,128)(2,1)S(1)} collective-permute-done((bf16[128,256]{1,0:T(8,128)(2,1)S(1)}, bf16[128,256]{1,0:T(8,128)(2,1)S(1)}, u32[]{:S(2)}, u32[]{:S(2)}) %collective-permute-start.8) | collective-permute-done | bytes 65568 | tf_op jit(solution)/shard_map/ppermute | solution.py:153
  28.5 2.9 %collective-permute-done.7 = bf16[128,256]{1,0:T(8,128)(2,1)S(1)} collective-permute-done((bf16[128,256]{1,0:T(8,128)(2,1)S(1)}, bf16[128,256]{1,0:T(8,128)(2,1)S(1)}, u32[]{:S(2)}, u32[]{:S(2)}) %collective-permute-start.7) | collective-permute-done | bytes 65568 | tf_op jit(solution)/shard_map/ppermute | solution.py:153
  31.6 1.5 %collective-permute-done.9.other_ref = bf16[4,128,256]{2,1,0:T(8,128)(2,1)S(1)} collective-permute-done((bf16[4,128,256]{2,1,0:T(8,128)(2,1)S(1)}, bf16[4,128,256]{2,1,0:T(8,128)(2,1)S(1)}, u32[]{:S(2)}, u32[]{:S(2)}) %collective-permute-start.9) | collective-permute-done | bytes 262176 | tf_op jit(solution)/shard_map/ppermute | solution.py:153
  33.2 7.9 %shard_map.120 = (f32[128,1024]{1,0:T(8,128)S(1)}, bf16[128,1024]{1,0:T(8,128)(2,1)S(1)}, bf16[32,512]{1,0:T(8,128)(2,1)S(1)}) custom-call(s32[2]{0:T(128)} %copy-done, bf16[4,128,256]{2,1,0:T(8,128)(2,1)S(1)} %pad_maximum_fusion.mine_ref, bf16[4,128,256]{2,1,0:T(8,128)(2,1)S(1)} %collective-permute-done.9.other_ref, ...), custom_call_target="tpu_custom_call" | custom-call | tf_op jit(solution)/shard_map/pallas_call | solution.py:376
  41.4 1.4 %collective-permute-done.10 = bf16[128,1024]{1,0:T(8,128)(2,1)S(1)} collective-permute-done((bf16[128,1024]{1,0:T(8,128)(2,1)S(1)}, bf16[128,1024]{1,0:T(8,128)(2,1)S(1)}, u32[]{:S(2)}, u32[]{:S(2)}) %collective-permute-start.10) | collective-permute-done | bytes 262176 | tf_op jit(solution)/shard_map/ppermute | solution.py:153
  42.9 1.9 %collective-permute-start.11 = (bf16[32,1024]{1,0:T(8,128)(2,1)S(1)}, bf16[32,1024]{1,0:T(8,128)(2,1)S(1)}, u32[]{:S(2)}, u32[]{:S(2)}) collective-permute-start(bf16[32,1024]{1,0:T(8,128)(2,1)S(1)} %get-tuple-element.17), channel_id=1, source_target_pairs={{0,8},{1,11},{2,10},{3,9},{4,12},{5,15},{6,14},{7,13},{8,0},{9,3},... | collective-permute-start | bytes 196616 | tf_op jit(solution)/shard_map/ppermute | solution.py:400
  44.8 0.7 %collective-permute-start.14 = (bf16[32,1024]{1,0:T(8,128)(2,1)S(1)}, bf16[32,1024]{1,0:T(8,128)(2,1)S(1)}, u32[]{:S(2)}, u32[]{:S(2)}) collective-permute-start(bf16[32,1024]{1,0:T(8,128)(2,1)S(1)} %get-tuple-element.18), channel_id=1, source_target_pairs={{0,0},{1,3},{2,2},{3,1},{4,4},{5,7},{6,6},{7,5},{8,8},{9,11},{10,1... | collective-permute-start | bytes 196616 | tf_op jit(solution)/shard_map/ppermute | solution.py:400
  45.4 1.1 %collective-permute-start.13 = (bf16[32,1024]{1,0:T(8,128)(2,1)S(1)}, bf16[32,1024]{1,0:T(8,128)(2,1)S(1)}, u32[]{:S(2)}, u32[]{:S(2)}) collective-permute-start(bf16[32,1024]{1,0:T(8,128)(2,1)S(1)} %get-tuple-element.19), channel_id=1, source_target_pairs={{0,12},{1,15},{2,14},{3,13},{4,8},{5,11},{6,10},{7,9},{8,4},{9,7},... | collective-permute-start | bytes 196616 | tf_op jit(solution)/shard_map/ppermute | solution.py:400
  47.2 2.1 %collective-permute-done.11 = bf16[32,1024]{1,0:T(8,128)(2,1)S(1)} collective-permute-done((bf16[32,1024]{1,0:T(8,128)(2,1)S(1)}, bf16[32,1024]{1,0:T(8,128)(2,1)S(1)}, u32[]{:S(2)}, u32[]{:S(2)}) %collective-permute-start.11) | collective-permute-done | bytes 65568 | tf_op jit(solution)/shard_map/ppermute | solution.py:400
  49.3 2.4 %collective-permute-done.13 = bf16[32,1024]{1,0:T(8,128)(2,1)S(1)} collective-permute-done((bf16[32,1024]{1,0:T(8,128)(2,1)S(1)}, bf16[32,1024]{1,0:T(8,128)(2,1)S(1)}, u32[]{:S(2)}, u32[]{:S(2)}) %collective-permute-start.13) | collective-permute-done | bytes 65568 | tf_op jit(solution)/shard_map/ppermute | solution.py:400
  51.7 2.0 %collective-permute-start.15 = (bf16[32,512]{1,0:T(8,128)(2,1)S(1)}, bf16[32,512]{1,0:T(8,128)(2,1)S(1)}, u32[]{:S(2)}, u32[]{:S(2)}) collective-permute-start(bf16[32,512]{1,0:T(8,128)(2,1)S(1)} %select_convert_fusion), channel_id=1, source_target_pairs={{0,1},{1,0},{2,3},{3,2},{4,5},{5,4},{6,7},{7,6},{8,9},{9,8},{10,11... | collective-permute-start | bytes 98312 | tf_op jit(solution)/shard_map/ppermute | solution.py:153
  53.7 0.9 %collective-permute-done.15 = bf16[32,512]{1,0:T(8,128)(2,1)S(1)} collective-permute-done((bf16[32,512]{1,0:T(8,128)(2,1)S(1)}, bf16[32,512]{1,0:T(8,128)(2,1)S(1)}, u32[]{:S(2)}, u32[]{:S(2)}) %collective-permute-start.15) | collective-permute-done | bytes 32800 | tf_op jit(solution)/shard_map/ppermute | solution.py:153
  (53 shorter events, 2.1 us)
Async XLA Ops:
  2.0 7.9 %collective-permute-start.2 = (bf16[32,1152]{1,0:T(8,128)(2,1)S(1)}, bf16[32,1152]{1,0:T(8,128)(2,1)S(1)}, u32[]{:S(2)}, u32[]{:S(2)}) collective-permute-start(bf16[32,1152]{1,0:T(8,128)(2,1)S(1)} %shard_map.118.own_ref), channel_id=1, source_target_pairs={{0,12},{4,8},{8,4},{12,0},{1,13},{5,9},{9,5},{13,1},{2,14},{6,10},... | collective-permute-start | bytes 221192 | tf_op jit(solution)/shard_map/ppermute | solution.py:153
  7.1 6.3 %collective-permute-start.1 = (bf16[32,1152]{1,0:T(8,128)(2,1)S(1)}, bf16[32,1152]{1,0:T(8,128)(2,1)S(1)}, u32[]{:S(2)}, u32[]{:S(2)}) collective-permute-start(bf16[32,1152]{1,0:T(8,128)(2,1)S(1)} %shard_map.118.own_ref), channel_id=1, source_target_pairs={{0,8},{4,12},{8,0},{12,4},{1,9},{5,13},{9,1},{13,5},{2,10},{6,14},... | collective-permute-start | bytes 221192 | tf_op jit(solution)/shard_map/ppermute | solution.py:153
  7.1 6.3 %collective-permute-start = (bf16[32,1152]{1,0:T(8,128)(2,1)S(1)}, bf16[32,1152]{1,0:T(8,128)(2,1)S(1)}, u32[]{:S(2)}, u32[]{:S(2)}) collective-permute-start(bf16[32,1152]{1,0:T(8,128)(2,1)S(1)} %shard_map.118.own_ref), channel_id=1, source_target_pairs={{0,4},{4,0},{8,12},{12,8},{1,5},{5,1},{9,13},{13,9},{2,6},{6,2},{1... | collective-permute-start | bytes 221192 | tf_op jit(solution)/shard_map/ppermute | solution.py:153
  7.8 0.9 %collective-permute-start.3 = (bf16[32,512]{1,0:T(8,128)(2,1)S(1)}, bf16[32,512]{1,0:T(8,128)(2,1)S(1)}, u32[]{:S(2)}, u32[]{:S(2)}) collective-permute-start(bf16[32,512]{1,0:T(8,128)(2,1)S(1)} %bitcast.30), channel_id=1, source_target_pairs={{0,0},{1,4},{2,8},{3,12},{4,1},{5,5},{6,9},{7,13},{8,2},{9,6},{10,... | collective-permute-start | bytes 98312 | tf_op jit(solution)/shard_map/ppermute | solution.py:328
  8.4 24.7 %slice-start = ((s8[16777216]{0:T(1024)(128)(4,1)}), s8[4194304]{0:T(1024)(128)(4,1)S(1)}, s32[]{:S(2)}) async-start(s8[16777216]{0:T(1024)(128)(4,1)} %bitcast.15), calls=%async_computation | async-start | bytes 8388608
  8.5 24.7 %slice-start.4 = ((s8[16777216]{0:T(1024)(128)(4,1)}), s8[4194304]{0:T(1024)(128)(4,1)S(1)}, s32[]{:S(2)}) async-start(s8[16777216]{0:T(1024)(128)(4,1)} %bitcast.17), calls=%async_computation.4 | async-start | bytes 8388608
  8.5 24.7 %slice-start.8 = ((s8[16777216]{0:T(1024)(128)(4,1)}), s8[4194304]{0:T(1024)(128)(4,1)S(1)}, s32[]{:S(2)}) async-start(s8[16777216]{0:T(1024)(128)(4,1)} %bitcast.19), calls=%async_computation.8 | async-start | bytes 8388608
  8.6 24.6 %slice-start.3 = ((s8[16777216]{0:T(1024)(128)(4,1)}), s8[4194304]{0:T(1024)(128)(4,1)S(1)}, s32[]{:S(2)}) async-start(s8[16777216]{0:T(1024)(128)(4,1)} %bitcast.15), calls=%async_computation.3 | async-start | bytes 8388608
  8.6 24.6 %slice-start.5 = ((s8[16777216]{0:T(1024)(128)(4,1)}), s8[4194304]{0:T(1024)(128)(4,1)S(1)}, s32[]{:S(2)}) async-start(s8[16777216]{0:T(1024)(128)(4,1)} %bitcast.17), calls=%async_computation.5 | async-start | bytes 8388608
  8.6 24.6 %slice-start.6 = ((s8[16777216]{0:T(1024)(128)(4,1)}), s8[4194304]{0:T(1024)(128)(4,1)S(1)}, s32[]{:S(2)}) async-start(s8[16777216]{0:T(1024)(128)(4,1)} %bitcast.17), calls=%async_computation.6 | async-start | bytes 8388608
  8.6 24.6 %slice-start.7 = ((s8[16777216]{0:T(1024)(128)(4,1)}), s8[4194304]{0:T(1024)(128)(4,1)S(1)}, s32[]{:S(2)}) async-start(s8[16777216]{0:T(1024)(128)(4,1)} %bitcast.17), calls=%async_computation.7 | async-start | bytes 8388608
  8.6 24.6 %slice-start.9 = ((s8[16777216]{0:T(1024)(128)(4,1)}), s8[4194304]{0:T(1024)(128)(4,1)S(1)}, s32[]{:S(2)}) async-start(s8[16777216]{0:T(1024)(128)(4,1)} %bitcast.19), calls=%async_computation.9 | async-start | bytes 8388608
  14.3 1.3 %collective-permute-start.4 = (bf16[128,256]{1,0:T(8,128)(2,1)S(1)}, bf16[128,256]{1,0:T(8,128)(2,1)S(1)}, u32[]{:S(2)}, u32[]{:S(2)}) collective-permute-start(bf16[128,256]{1,0:T(8,128)(2,1)S(1)} %get-tuple-element.12), channel_id=1, source_target_pairs={{0,1},{1,0},{2,3},{3,2},{4,5},{5,4},{6,7},{7,6},{8,9},{9,8},{10,11... | collective-permute-start | bytes 196616 | tf_op jit(solution)/shard_map/ppermute | solution.py:153
  15.7 6.2 %collective-permute-start.5 = (bf16[128,256]{1,0:T(8,128)(2,1)S(1)}, bf16[128,256]{1,0:T(8,128)(2,1)S(1)}, u32[]{:S(2)}, u32[]{:S(2)}) collective-permute-start(bf16[128,256]{1,0:T(8,128)(2,1)S(1)} %add_convert_fusion.2), channel_id=1, source_target_pairs={{0,2},{1,3},{2,0},{3,1},{4,6},{5,7},{6,4},{7,5},{8,10},{9,11},{10,... | collective-permute-start | bytes 196616 | tf_op jit(solution)/shard_map/ppermute | solution.py:153
  21.9 6.6 %collective-permute-start.8 = (bf16[128,256]{1,0:T(8,128)(2,1)S(1)}, bf16[128,256]{1,0:T(8,128)(2,1)S(1)}, u32[]{:S(2)}, u32[]{:S(2)}) collective-permute-start(bf16[128,256]{1,0:T(8,128)(2,1)S(1)} %add_convert_fusion.1), channel_id=1, source_target_pairs={{0,12},{4,8},{8,4},{12,0},{1,13},{5,9},{9,5},{13,1},{2,14},{6,10},... | collective-permute-start | bytes 196616 | tf_op jit(solution)/shard_map/ppermute | solution.py:153
  26.1 5.3 %collective-permute-start.7 = (bf16[128,256]{1,0:T(8,128)(2,1)S(1)}, bf16[128,256]{1,0:T(8,128)(2,1)S(1)}, u32[]{:S(2)}, u32[]{:S(2)}) collective-permute-start(bf16[128,256]{1,0:T(8,128)(2,1)S(1)} %add_convert_fusion.1), channel_id=1, source_target_pairs={{0,8},{4,12},{8,0},{12,4},{1,9},{5,13},{9,1},{13,5},{2,10},{6,14},... | collective-permute-start | bytes 196616 | tf_op jit(solution)/shard_map/ppermute | solution.py:153
  26.1 5.4 %collective-permute-start.6 = (bf16[128,256]{1,0:T(8,128)(2,1)S(1)}, bf16[128,256]{1,0:T(8,128)(2,1)S(1)}, u32[]{:S(2)}, u32[]{:S(2)}) collective-permute-start(bf16[128,256]{1,0:T(8,128)(2,1)S(1)} %add_convert_fusion.1), channel_id=1, source_target_pairs={{0,4},{4,0},{8,12},{12,8},{1,5},{5,1},{9,13},{13,9},{2,6},{6,2},{1... | collective-permute-start | bytes 196616 | tf_op jit(solution)/shard_map/ppermute | solution.py:153
  31.5 1.6 %collective-permute-start.9 = (bf16[4,128,256]{2,1,0:T(8,128)(2,1)S(1)}, bf16[4,128,256]{2,1,0:T(8,128)(2,1)S(1)}, u32[]{:S(2)}, u32[]{:S(2)}) collective-permute-start(bf16[4,128,256]{2,1,0:T(8,128)(2,1)S(1)} %pad_maximum_fusion.mine_ref), channel_id=1, source_target_pairs={{0,1},{1,0},{2,3},{3,2},{4,5},{5,4},{6,7},{7,6},{8,9},{9,8},{10,11... | collective-permute-start | bytes 786440 | tf_op jit(solution)/shard_map/ppermute | solution.py:153
  41.2 1.6 %collective-permute-start.10 = (bf16[128,1024]{1,0:T(8,128)(2,1)S(1)}, bf16[128,1024]{1,0:T(8,128)(2,1)S(1)}, u32[]{:S(2)}, u32[]{:S(2)}) collective-permute-start(bf16[128,1024]{1,0:T(8,128)(2,1)S(1)} %get-tuple-element.16), channel_id=1, source_target_pairs={{0,1},{1,0},{2,3},{3,2},{4,5},{5,4},{6,7},{7,6},{8,9},{9,8},{10,11... | collective-permute-start | bytes 786440 | tf_op jit(solution)/shard_map/ppermute | solution.py:153
  42.9 6.4 %collective-permute-start.11 = (bf16[32,1024]{1,0:T(8,128)(2,1)S(1)}, bf16[32,1024]{1,0:T(8,128)(2,1)S(1)}, u32[]{:S(2)}, u32[]{:S(2)}) collective-permute-start(bf16[32,1024]{1,0:T(8,128)(2,1)S(1)} %get-tuple-element.17), channel_id=1, source_target_pairs={{0,8},{1,11},{2,10},{3,9},{4,12},{5,15},{6,14},{7,13},{8,0},{9,3},... | collective-permute-start | bytes 196616 | tf_op jit(solution)/shard_map/ppermute | solution.py:400
  44.8 4.5 %collective-permute-start.14 = (bf16[32,1024]{1,0:T(8,128)(2,1)S(1)}, bf16[32,1024]{1,0:T(8,128)(2,1)S(1)}, u32[]{:S(2)}, u32[]{:S(2)}) collective-permute-start(bf16[32,1024]{1,0:T(8,128)(2,1)S(1)} %get-tuple-element.18), channel_id=1, source_target_pairs={{0,0},{1,3},{2,2},{3,1},{4,4},{5,7},{6,6},{7,5},{8,8},{9,11},{10,1... | collective-permute-start | bytes 196616 | tf_op jit(solution)/shard_map/ppermute | solution.py:400
  45.4 6.2 %collective-permute-start.13 = (bf16[32,1024]{1,0:T(8,128)(2,1)S(1)}, bf16[32,1024]{1,0:T(8,128)(2,1)S(1)}, u32[]{:S(2)}, u32[]{:S(2)}) collective-permute-start(bf16[32,1024]{1,0:T(8,128)(2,1)S(1)} %get-tuple-element.19), channel_id=1, source_target_pairs={{0,12},{1,15},{2,14},{3,13},{4,8},{5,11},{6,10},{7,9},{8,4},{9,7},... | collective-permute-start | bytes 196616 | tf_op jit(solution)/shard_map/ppermute | solution.py:400
  46.6 5.1 %collective-permute-start.12 = (bf16[32,1024]{1,0:T(8,128)(2,1)S(1)}, bf16[32,1024]{1,0:T(8,128)(2,1)S(1)}, u32[]{:S(2)}, u32[]{:S(2)}) collective-permute-start(bf16[32,1024]{1,0:T(8,128)(2,1)S(1)} %get-tuple-element.20), channel_id=1, source_target_pairs={{0,4},{1,7},{2,6},{3,5},{4,0},{5,3},{6,2},{7,1},{8,12},{9,15},{10,... | collective-permute-start | bytes 196616 | tf_op jit(solution)/shard_map/ppermute | solution.py:400
  51.7 2.9 %collective-permute-start.15 = (bf16[32,512]{1,0:T(8,128)(2,1)S(1)}, bf16[32,512]{1,0:T(8,128)(2,1)S(1)}, u32[]{:S(2)}, u32[]{:S(2)}) collective-permute-start(bf16[32,512]{1,0:T(8,128)(2,1)S(1)} %select_convert_fusion), channel_id=1, source_target_pairs={{0,1},{1,0},{2,3},{3,2},{4,5},{5,4},{6,7},{7,6},{8,9},{9,8},{10,11... | collective-permute-start | bytes 98312 | tf_op jit(solution)/shard_map/ppermute | solution.py:153
  (7 other events, 125.3 us)

commit v6 on v5

--- a/solution.py
+++ b/solution.py
@@ -350,6 +350,7 @@
         cost_estimate=pl.CostEstimate(flops=20000000000, bytes_accessed=1000000, transcendentals=0),
         compiler_params=pltpu.CompilerParams(vmem_limit_bytes=6 * 2**20),
     )(*[pltpu.with_memory_space_constraint(g, pltpu.HBM) for g in given])
+    payload, turned = lax.optimization_barrier((payload, turned))
     others = spread(payload)
     keep, send, mix = pl.pallas_call(
         project_kernel,

time: 55.4 us -> 57.3 us (1.034)
  starting transfers between devices: 21.8 us -> 24 us
    ppermute x11, starting transfers between devices: 16.8 us -> 18.3 us  [flip_permute(): return lax.ppermute(value, axis, [(i, i ^ mask) for i in range(size)])]
    ppermute x1, starting transfers between devices: 0.65 us -> 1.4 us  [local_small(): lax.ppermute(residual.reshape(rows, columns), ('wide', 'narrow'), [(i, i...]
  transfers between devices with their start and end apart: 16 -> 16, of which waited for: 12 -> 12; matrix products, arithmetic and copies ran while one was open for 0% -> 0% of each run, Pallas kernels for 0% -> 4%
where the time goes in v6:
time: 57.3 us; the launch traced here: 57 us
  starting transfers between devices  24 us (42%)
  waiting for transfers between devices  21 us (37%)
  Pallas kernels  10.8 us (19%)
  other arithmetic  0.87 us (2%)
    ppermute x11, starting transfers between devices, flip_permute(): return lax.ppermute(value, axis, [(i, i ^ mask) for i in range(size)])  18.3 us
    ppermute x11, waiting for transfers between devices, flip_permute(): return lax.ppermute(value, axis, [(i, i ^ mask) for i in range(size)])  16.8 us
    pallas_call x1, Pallas kernels, local_small(): pl.pallas_call(expert_kernel, out_shape=(pltpu.VMEM((size * rows, model /...  7.94 us
    ppermute x4, starting transfers between devices, local_small(): lax.ppermute(total[s], ('wide', 'narrow'), [(i, i ^ s * size ^ (2 if i &...  4.27 us
    ppermute x4, waiting for transfers between devices, local_small(): lax.ppermute(total[s], ('wide', 'narrow'), [(i, i ^ s * size ^ (2 if i &...  4.17 us
    pallas_call x1, Pallas kernels, local_small(): pl.pallas_call(attend_kernel, out_shape=jax.ShapeDtypeStruct((rows, depth...  2 us
    ppermute x1, starting transfers between devices, local_small(): lax.ppermute(residual.reshape(rows, columns), ('wide', 'narrow'), [(i, i...  1.4 us
  transfers between devices with their start and end apart: 16, of which 12 were waited for; matrix products, arithmetic and copies ran while one was open for 0% of the time, Pallas kernels for 4%

profile of v6, /device:TPU:0, one launch (start us, length us, event | category | flops | bytes accessed | tf_op | source)
XLA Modules:
  0.0 57.0 jit_solution(11595892833299261997)
XLA Ops:
  0.0 1.4 %collective-permute-start = (bf16[32,512]{1,0:T(8,128)(2,1)}, bf16[32,512]{1,0:T(8,128)(2,1)S(1)}, u32[]{:S(2)}, u32[]{:S(2)}) collective-permute-start(bf16[32,512]{1,0:T(8,128)(2,1)} %bitcast.30), channel_id=1, source_target_pairs={{0,0},{1,4},{2,8},{3,12},{4,1},{5,5},{6,9},{7,13},{8,2},{9,6},{10,... | collective-permute-start | bytes 98312 | tf_op jit(solution)/shard_map/ppermute | solution.py:328
  1.4 2.0 %shard_map.118.own_ref = bf16[32,1152]{1,0:T(8,128)(2,1)S(1)} custom-call(s32[2,16]{1,0:T(2,128)} %refs_0_.1, bf16[256,128]{1,0:T(8,128)(2,1)} %bitcast.29, bf16[2048,128]{1,0:T(8,128)(2,1)} %bitcast.27, bf16[2048,128]{1,0:T(8,128)(2,1)} %bitcast.28, s32[2,8,16]{2,1,0:T(8,128)} %bitcast.31, f32[2,8,16]{2,1,0:T(8,128)} %bitcast.32), custom_call_target="tpu_custom_call" | custom-call | flops 20000000000 | bytes 1000000 | tf_op jit(solution)/shard_map/pallas_call | solution.py:341
  3.4 9.7 %collective-permute-start.3 = (bf16[32,1152]{1,0:T(8,128)(2,1)S(1)}, bf16[32,1152]{1,0:T(8,128)(2,1)S(1)}, u32[]{:S(2)}, u32[]{:S(2)}) collective-permute-start(bf16[32,1152]{1,0:T(8,128)(2,1)S(1)} %shard_map.118.own_ref), channel_id=1, source_target_pairs={{0,12},{4,8},{8,4},{12,0},{1,13},{5,9},{9,5},{13,1},{2,14},{6,10},... | collective-permute-start | bytes 221192 | tf_op jit(solution)/shard_map/ppermute | solution.py:153
  13.9 1.6 %collective-permute-done.3.got3_ref = bf16[32,1152]{1,0:T(8,128)(2,1)S(1)} collective-permute-done((bf16[32,1152]{1,0:T(8,128)(2,1)S(1)}, bf16[32,1152]{1,0:T(8,128)(2,1)S(1)}, u32[]{:S(2)}, u32[]{:S(2)}) %collective-permute-start.3) | collective-permute-done | bytes 73760 | tf_op jit(solution)/shard_map/ppermute | solution.py:153
  15.5 2.9 %collective-permute-done.2.got2_ref = bf16[32,1152]{1,0:T(8,128)(2,1)S(1)} collective-permute-done((bf16[32,1152]{1,0:T(8,128)(2,1)S(1)}, bf16[32,1152]{1,0:T(8,128)(2,1)S(1)}, u32[]{:S(2)}, u32[]{:S(2)}) %collective-permute-start.2) | collective-permute-done | bytes 73760 | tf_op jit(solution)/shard_map/ppermute | solution.py:153
  18.4 0.9 %shard_map.119 = (f32[128,256]{1,0:T(8,128)S(1)}, bf16[128,256]{1,0:T(8,128)(2,1)S(1)}, bf16[128,128]{1,0:T(8,128)(2,1)S(1)}) custom-call(s32[2]{0:T(128)S(1)} %pad_add_fusion.where_ref, bf16[32,1152]{1,0:T(8,128)(2,1)S(1)} %shard_map.118.own_ref, bf16[32,1152]{1,0:T(8,128)(2,1)S(1)} %collective-permute-done.1.got1_ref, ...), custom_call_target="tpu_custom_call" | custom-call | flops 30000001024 | bytes 1000000 | tf_op jit(solution)/shard_map/pallas_call | solution.py:355
  19.4 1.2 %collective-permute-done.4 = bf16[128,256]{1,0:T(8,128)(2,1)S(1)} collective-permute-done((bf16[128,256]{1,0:T(8,128)(2,1)S(1)}, bf16[128,256]{1,0:T(8,128)(2,1)S(1)}, u32[]{:S(2)}, u32[]{:S(2)}) %collective-permute-start.4) | collective-permute-done | bytes 65568 | tf_op jit(solution)/shard_map/ppermute | solution.py:153
  20.7 1.0 %collective-permute-start.5 = (bf16[128,256]{1,0:T(8,128)(2,1)S(1)}, bf16[128,256]{1,0:T(8,128)(2,1)S(1)}, u32[]{:S(2)}, u32[]{:S(2)}) collective-permute-start(bf16[128,256]{1,0:T(8,128)(2,1)S(1)} %add_convert_fusion.2), channel_id=1, source_target_pairs={{0,2},{1,3},{2,0},{3,1},{4,6},{5,7},{6,4},{7,5},{8,10},{9,11},{10,... | collective-permute-start | bytes 196616 | tf_op jit(solution)/shard_map/ppermute | solution.py:153
  21.7 3.3 %collective-permute-done.5 = bf16[128,256]{1,0:T(8,128)(2,1)S(1)} collective-permute-done((bf16[128,256]{1,0:T(8,128)(2,1)S(1)}, bf16[128,256]{1,0:T(8,128)(2,1)S(1)}, u32[]{:S(2)}, u32[]{:S(2)}) %collective-permute-start.5) | collective-permute-done | bytes 65568 | tf_op jit(solution)/shard_map/ppermute | solution.py:153
  25.0 2.3 %collective-permute-start.8 = (bf16[128,256]{1,0:T(8,128)(2,1)S(1)}, bf16[128,256]{1,0:T(8,128)(2,1)S(1)}, u32[]{:S(2)}, u32[]{:S(2)}) collective-permute-start(bf16[128,256]{1,0:T(8,128)(2,1)S(1)} %add_convert_fusion.1), channel_id=1, source_target_pairs={{0,12},{4,8},{8,4},{12,0},{1,13},{5,9},{9,5},{13,1},{2,14},{6,10},... | collective-permute-start | bytes 196616 | tf_op jit(solution)/shard_map/ppermute | solution.py:153
  27.4 2.1 %collective-permute-start.6 = (bf16[128,256]{1,0:T(8,128)(2,1)S(1)}, bf16[128,256]{1,0:T(8,128)(2,1)S(1)}, u32[]{:S(2)}, u32[]{:S(2)}) collective-permute-start(bf16[128,256]{1,0:T(8,128)(2,1)S(1)} %add_convert_fusion.1), channel_id=1, source_target_pairs={{0,4},{4,0},{8,12},{12,8},{1,5},{5,1},{9,13},{13,9},{2,6},{6,2},{1... | collective-permute-start | bytes 196616 | tf_op jit(solution)/shard_map/ppermute | solution.py:153
  29.5 2.1 %collective-permute-done.8 = bf16[128,256]{1,0:T(8,128)(2,1)S(1)} collective-permute-done((bf16[128,256]{1,0:T(8,128)(2,1)S(1)}, bf16[128,256]{1,0:T(8,128)(2,1)S(1)}, u32[]{:S(2)}, u32[]{:S(2)}) %collective-permute-start.8) | collective-permute-done | bytes 65568 | tf_op jit(solution)/shard_map/ppermute | solution.py:153
  31.5 1.9 %collective-permute-done.7 = bf16[128,256]{1,0:T(8,128)(2,1)S(1)} collective-permute-done((bf16[128,256]{1,0:T(8,128)(2,1)S(1)}, bf16[128,256]{1,0:T(8,128)(2,1)S(1)}, u32[]{:S(2)}, u32[]{:S(2)}) %collective-permute-start.7) | collective-permute-done | bytes 65568 | tf_op jit(solution)/shard_map/ppermute | solution.py:153
  33.5 1.5 %collective-permute-done.9.other_ref = bf16[4,128,256]{2,1,0:T(8,128)(2,1)S(1)} collective-permute-done((bf16[4,128,256]{2,1,0:T(8,128)(2,1)S(1)}, bf16[4,128,256]{2,1,0:T(8,128)(2,1)S(1)}, u32[]{:S(2)}, u32[]{:S(2)}) %collective-permute-start.9) | collective-permute-done | bytes 262176 | tf_op jit(solution)/shard_map/ppermute | solution.py:153
  35.2 7.9 %shard_map.120 = (f32[128,1024]{1,0:T(8,128)S(1)}, bf16[128,1024]{1,0:T(8,128)(2,1)S(1)}, bf16[32,512]{1,0:T(8,128)(2,1)S(1)}) custom-call(s32[2]{0:T(128)} %copy-done, bf16[4,128,256]{2,1,0:T(8,128)(2,1)S(1)} %pad_maximum_fusion.mine_ref, bf16[4,128,256]{2,1,0:T(8,128)(2,1)S(1)} %collective-permute-done.9.other_ref, ...), custom_call_target="tpu_custom_call" | custom-call | tf_op jit(solution)/shard_map/pallas_call | solution.py:377
  43.3 1.4 %collective-permute-done.10 = bf16[128,1024]{1,0:T(8,128)(2,1)S(1)} collective-permute-done((bf16[128,1024]{1,0:T(8,128)(2,1)S(1)}, bf16[128,1024]{1,0:T(8,128)(2,1)S(1)}, u32[]{:S(2)}, u32[]{:S(2)}) %collective-permute-start.10) | collective-permute-done | bytes 262176 | tf_op jit(solution)/shard_map/ppermute | solution.py:153
  44.8 1.2 %collective-permute-start.11 = (bf16[32,1024]{1,0:T(8,128)(2,1)S(1)}, bf16[32,1024]{1,0:T(8,128)(2,1)S(1)}, u32[]{:S(2)}, u32[]{:S(2)}) collective-permute-start(bf16[32,1024]{1,0:T(8,128)(2,1)S(1)} %get-tuple-element.21), channel_id=1, source_target_pairs={{0,8},{1,11},{2,10},{3,9},{4,12},{5,15},{6,14},{7,13},{8,0},{9,3},... | collective-permute-start | bytes 196616 | tf_op jit(solution)/shard_map/ppermute | solution.py:401
  46.0 0.7 %collective-permute-start.14 = (bf16[32,1024]{1,0:T(8,128)(2,1)S(1)}, bf16[32,1024]{1,0:T(8,128)(2,1)S(1)}, u32[]{:S(2)}, u32[]{:S(2)}) collective-permute-start(bf16[32,1024]{1,0:T(8,128)(2,1)S(1)} %get-tuple-element.22), channel_id=1, source_target_pairs={{0,0},{1,3},{2,2},{3,1},{4,4},{5,7},{6,6},{7,5},{8,8},{9,11},{10,1... | collective-permute-start | bytes 196616 | tf_op jit(solution)/shard_map/ppermute | solution.py:401
  46.7 1.6 %collective-permute-start.13 = (bf16[32,1024]{1,0:T(8,128)(2,1)S(1)}, bf16[32,1024]{1,0:T(8,128)(2,1)S(1)}, u32[]{:S(2)}, u32[]{:S(2)}) collective-permute-start(bf16[32,1024]{1,0:T(8,128)(2,1)S(1)} %get-tuple-element.23), channel_id=1, source_target_pairs={{0,12},{1,15},{2,14},{3,13},{4,8},{5,11},{6,10},{7,9},{8,4},{9,7},... | collective-permute-start | bytes 196616 | tf_op jit(solution)/shard_map/ppermute | solution.py:401
  48.3 0.8 %collective-permute-start.12 = (bf16[32,1024]{1,0:T(8,128)(2,1)S(1)}, bf16[32,1024]{1,0:T(8,128)(2,1)S(1)}, u32[]{:S(2)}, u32[]{:S(2)}) collective-permute-start(bf16[32,1024]{1,0:T(8,128)(2,1)S(1)} %get-tuple-element.24), channel_id=1, source_target_pairs={{0,4},{1,7},{2,6},{3,5},{4,0},{5,3},{6,2},{7,1},{8,12},{9,15},{10,... | collective-permute-start | bytes 196616 | tf_op jit(solution)/shard_map/ppermute | solution.py:401
  49.1 2.4 %collective-permute-done.11 = bf16[32,1024]{1,0:T(8,128)(2,1)S(1)} collective-permute-done((bf16[32,1024]{1,0:T(8,128)(2,1)S(1)}, bf16[32,1024]{1,0:T(8,128)(2,1)S(1)}, u32[]{:S(2)}, u32[]{:S(2)}) %collective-permute-start.11) | collective-permute-done | bytes 65568 | tf_op jit(solution)/shard_map/ppermute | solution.py:401
  51.5 1.5 %collective-permute-done.13 = bf16[32,1024]{1,0:T(8,128)(2,1)S(1)} collective-permute-done((bf16[32,1024]{1,0:T(8,128)(2,1)S(1)}, bf16[32,1024]{1,0:T(8,128)(2,1)S(1)}, u32[]{:S(2)}, u32[]{:S(2)}) %collective-permute-start.13) | collective-permute-done | bytes 65568 | tf_op jit(solution)/shard_map/ppermute | solution.py:401
  53.3 2.2 %collective-permute-start.15 = (bf16[32,512]{1,0:T(8,128)(2,1)S(1)}, bf16[32,512]{1,0:T(8,128)(2,1)S(1)}, u32[]{:S(2)}, u32[]{:S(2)}) collective-permute-start(bf16[32,512]{1,0:T(8,128)(2,1)S(1)} %select_convert_fusion), channel_id=1, source_target_pairs={{0,1},{1,0},{2,3},{3,2},{4,5},{5,4},{6,7},{7,6},{8,9},{9,8},{10,11... | collective-permute-start | bytes 98312 | tf_op jit(solution)/shard_map/ppermute | solution.py:153
  55.5 0.9 %collective-permute-done.15 = bf16[32,512]{1,0:T(8,128)(2,1)S(1)} collective-permute-done((bf16[32,512]{1,0:T(8,128)(2,1)S(1)}, bf16[32,512]{1,0:T(8,128)(2,1)S(1)}, u32[]{:S(2)}, u32[]{:S(2)}) %collective-permute-start.15) | collective-permute-done | bytes 32800 | tf_op jit(solution)/shard_map/ppermute | solution.py:153
  (51 shorter events, 2.2 us)
Async XLA Ops:
  0.0 3.4 %collective-permute-start = (bf16[32,512]{1,0:T(8,128)(2,1)}, bf16[32,512]{1,0:T(8,128)(2,1)S(1)}, u32[]{:S(2)}, u32[]{:S(2)}) collective-permute-start(bf16[32,512]{1,0:T(8,128)(2,1)} %bitcast.30), channel_id=1, source_target_pairs={{0,0},{1,4},{2,8},{3,12},{4,1},{5,5},{6,9},{7,13},{8,2},{9,6},{10,... | collective-permute-start | bytes 98312 | tf_op jit(solution)/shard_map/ppermute | solution.py:328
  3.4 12.1 %collective-permute-start.3 = (bf16[32,1152]{1,0:T(8,128)(2,1)S(1)}, bf16[32,1152]{1,0:T(8,128)(2,1)S(1)}, u32[]{:S(2)}, u32[]{:S(2)}) collective-permute-start(bf16[32,1152]{1,0:T(8,128)(2,1)S(1)} %shard_map.118.own_ref), channel_id=1, source_target_pairs={{0,12},{4,8},{8,4},{12,0},{1,13},{5,9},{9,5},{13,1},{2,14},{6,10},... | collective-permute-start | bytes 221192 | tf_op jit(solution)/shard_map/ppermute | solution.py:153
  13.2 5.3 %collective-permute-start.2 = (bf16[32,1152]{1,0:T(8,128)(2,1)S(1)}, bf16[32,1152]{1,0:T(8,128)(2,1)S(1)}, u32[]{:S(2)}, u32[]{:S(2)}) collective-permute-start(bf16[32,1152]{1,0:T(8,128)(2,1)S(1)} %shard_map.118.own_ref), channel_id=1, source_target_pairs={{0,8},{4,12},{8,0},{12,4},{1,9},{5,13},{9,1},{13,5},{2,10},{6,14},... | collective-permute-start | bytes 221192 | tf_op jit(solution)/shard_map/ppermute | solution.py:153
  13.2 5.3 %collective-permute-start.1 = (bf16[32,1152]{1,0:T(8,128)(2,1)S(1)}, bf16[32,1152]{1,0:T(8,128)(2,1)S(1)}, u32[]{:S(2)}, u32[]{:S(2)}) collective-permute-start(bf16[32,1152]{1,0:T(8,128)(2,1)S(1)} %shard_map.118.own_ref), channel_id=1, source_target_pairs={{0,4},{4,0},{8,12},{12,8},{1,5},{5,1},{9,13},{13,9},{2,6},{6,2},{1... | collective-permute-start | bytes 221192 | tf_op jit(solution)/shard_map/ppermute | solution.py:153
  13.7 21.3 %slice-start = ((s8[16777216]{0:T(1024)(128)(4,1)}), s8[4194304]{0:T(1024)(128)(4,1)S(1)}, s32[]{:S(2)}) async-start(s8[16777216]{0:T(1024)(128)(4,1)} %bitcast.15), calls=%async_computation | async-start | bytes 8388608
  13.7 21.3 %slice-start.4 = ((s8[16777216]{0:T(1024)(128)(4,1)}), s8[4194304]{0:T(1024)(128)(4,1)S(1)}, s32[]{:S(2)}) async-start(s8[16777216]{0:T(1024)(128)(4,1)} %bitcast.17), calls=%async_computation.4 | async-start | bytes 8388608
  13.8 21.3 %slice-start.8 = ((s8[16777216]{0:T(1024)(128)(4,1)}), s8[4194304]{0:T(1024)(128)(4,1)S(1)}, s32[]{:S(2)}) async-start(s8[16777216]{0:T(1024)(128)(4,1)} %bitcast.19), calls=%async_computation.8 | async-start | bytes 8388608
  13.8 21.2 %slice-start.3 = ((s8[16777216]{0:T(1024)(128)(4,1)}), s8[4194304]{0:T(1024)(128)(4,1)S(1)}, s32[]{:S(2)}) async-start(s8[16777216]{0:T(1024)(128)(4,1)} %bitcast.15), calls=%async_computation.3 | async-start | bytes 8388608
  13.8 21.2 %slice-start.5 = ((s8[16777216]{0:T(1024)(128)(4,1)}), s8[4194304]{0:T(1024)(128)(4,1)S(1)}, s32[]{:S(2)}) async-start(s8[16777216]{0:T(1024)(128)(4,1)} %bitcast.17), calls=%async_computation.5 | async-start | bytes 8388608
  13.9 21.2 %slice-start.6 = ((s8[16777216]{0:T(1024)(128)(4,1)}), s8[4194304]{0:T(1024)(128)(4,1)S(1)}, s32[]{:S(2)}) async-start(s8[16777216]{0:T(1024)(128)(4,1)} %bitcast.17), calls=%async_computation.6 | async-start | bytes 8388608
  13.9 21.2 %slice-start.7 = ((s8[16777216]{0:T(1024)(128)(4,1)}), s8[4194304]{0:T(1024)(128)(4,1)S(1)}, s32[]{:S(2)}) async-start(s8[16777216]{0:T(1024)(128)(4,1)} %bitcast.17), calls=%async_computation.7 | async-start | bytes 8388608
  13.9 21.2 %slice-start.9 = ((s8[16777216]{0:T(1024)(128)(4,1)}), s8[4194304]{0:T(1024)(128)(4,1)S(1)}, s32[]{:S(2)}) async-start(s8[16777216]{0:T(1024)(128)(4,1)} %bitcast.19), calls=%async_computation.9 | async-start | bytes 8388608
  19.3 1.3 %collective-permute-start.4 = (bf16[128,256]{1,0:T(8,128)(2,1)S(1)}, bf16[128,256]{1,0:T(8,128)(2,1)S(1)}, u32[]{:S(2)}, u32[]{:S(2)}) collective-permute-start(bf16[128,256]{1,0:T(8,128)(2,1)S(1)} %get-tuple-element.16), channel_id=1, source_target_pairs={{0,1},{1,0},{2,3},{3,2},{4,5},{5,4},{6,7},{7,6},{8,9},{9,8},{10,11... | collective-permute-start | bytes 196616 | tf_op jit(solution)/shard_map/ppermute | solution.py:153
  20.7 4.3 %collective-permute-start.5 = (bf16[128,256]{1,0:T(8,128)(2,1)S(1)}, bf16[128,256]{1,0:T(8,128)(2,1)S(1)}, u32[]{:S(2)}, u32[]{:S(2)}) collective-permute-start(bf16[128,256]{1,0:T(8,128)(2,1)S(1)} %add_convert_fusion.2), channel_id=1, source_target_pairs={{0,2},{1,3},{2,0},{3,1},{4,6},{5,7},{6,4},{7,5},{8,10},{9,11},{10,... | collective-permute-start | bytes 196616 | tf_op jit(solution)/shard_map/ppermute | solution.py:153
  25.0 6.5 %collective-permute-start.8 = (bf16[128,256]{1,0:T(8,128)(2,1)S(1)}, bf16[128,256]{1,0:T(8,128)(2,1)S(1)}, u32[]{:S(2)}, u32[]{:S(2)}) collective-permute-start(bf16[128,256]{1,0:T(8,128)(2,1)S(1)} %add_convert_fusion.1), channel_id=1, source_target_pairs={{0,12},{4,8},{8,4},{12,0},{1,13},{5,9},{9,5},{13,1},{2,14},{6,10},... | collective-permute-start | bytes 196616 | tf_op jit(solution)/shard_map/ppermute | solution.py:153
  27.4 6.0 %collective-permute-start.7 = (bf16[128,256]{1,0:T(8,128)(2,1)S(1)}, bf16[128,256]{1,0:T(8,128)(2,1)S(1)}, u32[]{:S(2)}, u32[]{:S(2)}) collective-permute-start(bf16[128,256]{1,0:T(8,128)(2,1)S(1)} %add_convert_fusion.1), channel_id=1, source_target_pairs={{0,8},{4,12},{8,0},{12,4},{1,9},{5,13},{9,1},{13,5},{2,10},{6,14},... | collective-permute-start | bytes 196616 | tf_op jit(solution)/shard_map/ppermute | solution.py:153
  27.4 6.0 %collective-permute-start.6 = (bf16[128,256]{1,0:T(8,128)(2,1)S(1)}, bf16[128,256]{1,0:T(8,128)(2,1)S(1)}, u32[]{:S(2)}, u32[]{:S(2)}) collective-permute-start(bf16[128,256]{1,0:T(8,128)(2,1)S(1)} %add_convert_fusion.1), channel_id=1, source_target_pairs={{0,4},{4,0},{8,12},{12,8},{1,5},{5,1},{9,13},{13,9},{2,6},{6,2},{1... | collective-permute-start | bytes 196616 | tf_op jit(solution)/shard_map/ppermute | solution.py:153
  33.4 1.6 %collective-permute-start.9 = (bf16[4,128,256]{2,1,0:T(8,128)(2,1)S(1)}, bf16[4,128,256]{2,1,0:T(8,128)(2,1)S(1)}, u32[]{:S(2)}, u32[]{:S(2)}) collective-permute-start(bf16[4,128,256]{2,1,0:T(8,128)(2,1)S(1)} %pad_maximum_fusion.mine_ref), channel_id=1, source_target_pairs={{0,1},{1,0},{2,3},{3,2},{4,5},{5,4},{6,7},{7,6},{8,9},{9,8},{10,11... | collective-permute-start | bytes 786440 | tf_op jit(solution)/shard_map/ppermute | solution.py:153
  43.1 1.6 %collective-permute-start.10 = (bf16[128,1024]{1,0:T(8,128)(2,1)S(1)}, bf16[128,1024]{1,0:T(8,128)(2,1)S(1)}, u32[]{:S(2)}, u32[]{:S(2)}) collective-permute-start(bf16[128,1024]{1,0:T(8,128)(2,1)S(1)} %get-tuple-element.20), channel_id=1, source_target_pairs={{0,1},{1,0},{2,3},{3,2},{4,5},{5,4},{6,7},{7,6},{8,9},{9,8},{10,11... | collective-permute-start | bytes 786440 | tf_op jit(solution)/shard_map/ppermute | solution.py:153
  44.8 6.7 %collective-permute-start.11 = (bf16[32,1024]{1,0:T(8,128)(2,1)S(1)}, bf16[32,1024]{1,0:T(8,128)(2,1)S(1)}, u32[]{:S(2)}, u32[]{:S(2)}) collective-permute-start(bf16[32,1024]{1,0:T(8,128)(2,1)S(1)} %get-tuple-element.21), channel_id=1, source_target_pairs={{0,8},{1,11},{2,10},{3,9},{4,12},{5,15},{6,14},{7,13},{8,0},{9,3},... | collective-permute-start | bytes 196616 | tf_op jit(solution)/shard_map/ppermute | solution.py:401
  46.0 5.5 %collective-permute-start.14 = (bf16[32,1024]{1,0:T(8,128)(2,1)S(1)}, bf16[32,1024]{1,0:T(8,128)(2,1)S(1)}, u32[]{:S(2)}, u32[]{:S(2)}) collective-permute-start(bf16[32,1024]{1,0:T(8,128)(2,1)S(1)} %get-tuple-element.22), channel_id=1, source_target_pairs={{0,0},{1,3},{2,2},{3,1},{4,4},{5,7},{6,6},{7,5},{8,8},{9,11},{10,1... | collective-permute-start | bytes 196616 | tf_op jit(solution)/shard_map/ppermute | solution.py:401
  46.7 6.3 %collective-permute-start.13 = (bf16[32,1024]{1,0:T(8,128)(2,1)S(1)}, bf16[32,1024]{1,0:T(8,128)(2,1)S(1)}, u32[]{:S(2)}, u32[]{:S(2)}) collective-permute-start(bf16[32,1024]{1,0:T(8,128)(2,1)S(1)} %get-tuple-element.23), channel_id=1, source_target_pairs={{0,12},{1,15},{2,14},{3,13},{4,8},{5,11},{6,10},{7,9},{8,4},{9,7},... | collective-permute-start | bytes 196616 | tf_op jit(solution)/shard_map/ppermute | solution.py:401
  48.3 5.0 %collective-permute-start.12 = (bf16[32,1024]{1,0:T(8,128)(2,1)S(1)}, bf16[32,1024]{1,0:T(8,128)(2,1)S(1)}, u32[]{:S(2)}, u32[]{:S(2)}) collective-permute-start(bf16[32,1024]{1,0:T(8,128)(2,1)S(1)} %get-tuple-element.24), channel_id=1, source_target_pairs={{0,4},{1,7},{2,6},{3,5},{4,0},{5,3},{6,2},{7,1},{8,12},{9,15},{10,... | collective-permute-start | bytes 196616 | tf_op jit(solution)/shard_map/ppermute | solution.py:401
  53.3 3.1 %collective-permute-start.15 = (bf16[32,512]{1,0:T(8,128)(2,1)S(1)}, bf16[32,512]{1,0:T(8,128)(2,1)S(1)}, u32[]{:S(2)}, u32[]{:S(2)}) collective-permute-start(bf16[32,512]{1,0:T(8,128)(2,1)S(1)} %select_convert_fusion), channel_id=1, source_target_pairs={{0,1},{1,0},{2,3},{3,2},{4,5},{5,4},{6,7},{7,6},{8,9},{9,8},{10,11... | collective-permute-start | bytes 98312 | tf_op jit(solution)/shard_map/ppermute | solution.py:153
  (6 other events, 107.4 us)

commit v7 on v5

--- a/solution.py
+++ b/solution.py
@@ -240,14 +240,14 @@
     )
     mine = pl.ds(pl.multiple_of((narrow & 1) * half, half), half)
     other = pl.ds(pl.multiple_of((1 - (narrow & 1)) * half, half), half)
-    spot = pl.ds(pl.multiple_of((wide ^ narrow) * rows, rows), rows)
+    spot = pl.ds(pl.multiple_of((wide ^ where_ref[2]) * rows, rows), rows)
     keep_ref[...] = jnp.dot(features, w_ref[:, mine], preferred_element_type=jnp.float32)
     keep_ref[spot, :] += res_ref[:, mine].astype(jnp.float32)
     part = jnp.dot(features, w_ref[:, other], preferred_element_type=jnp.float32)
     part_rows = lax.broadcasted_iota(jnp.int32, part.shape, 0) // rows
     extra = res_ref[:, other].astype(jnp.float32)
     extra = jnp.concatenate([extra] * (part.shape[0] // rows), axis=0)
-    part = jnp.where(part_rows == (wide ^ narrow), part + extra, part)
+    part = jnp.where(part_rows == (wide ^ where_ref[2]), part + extra, part)
     send_ref[...] = part.astype(jnp.bfloat16)
     mix_ref[...] = jnp.concatenate(
         [r[:, depth:] for r in (own_ref, got1_ref, got2_ref, got3_ref)], axis=0
@@ -301,6 +301,16 @@
             target[:, k * block:(k + 1) * block] = out.astype(target.dtype)
 
 
+def residual_route(size):
+    route = []
+    for n in range(size):
+        near = sorted(range(size), key=lambda w: abs(w - n))
+        column = n >> 1
+        places = [2 * (column ^ 1), 2 * (column ^ 1) + 1, 2 * column, 2 * column + 1]
+        route += [(w, n, to) for w, to in zip(near, places)]
+    return route
+
+
 def local_small(
     queries,
     key_cache,
@@ -323,12 +333,16 @@
     vmem = pl.BlockSpec(memory_space=pltpu.VMEM)
     smem = pl.BlockSpec(memory_space=pltpu.SMEM)
     wide, narrow = lax.axis_index("wide"), lax.axis_index("narrow")
-    where = jnp.stack([wide, narrow]).astype(jnp.int32)
     size = lax.axis_size("wide")
+    route = residual_route(size)
+    source = jnp.zeros((), jnp.int32)
+    for w, n, to in route:
+        source = jnp.where((wide == n) & (narrow == to), w, source)
+    where = jnp.stack([wide, narrow, source]).astype(jnp.int32)
     turned = lax.ppermute(
         residual.reshape(rows, columns),
         ("wide", "narrow"),
-        [(i, (i % size) * size + i // size) for i in range(size * size)],
+        [(w * size + n, n * size + to) for w, n, to in route],
     )
     given = (
         lengths,

time: 55.4 us -> 53.7 us (0.969)
  starting transfers between devices: 21.8 us -> 18.9 us
  waiting for transfers between devices: 21.4 us -> 22.5 us
    ppermute x1, waiting for transfers between devices: 0.01 us -> 5.18 us  [local_small(): lax.ppermute(residual.reshape(rows, columns), ('wide', 'narrow'), [(w * s...]
    ppermute x11, starting transfers between devices: 16.8 us -> 13 us  [flip_permute(): return lax.ppermute(value, axis, [(i, i ^ mask) for i in range(size)])]
    ppermute x11, waiting for transfers between devices: 16.9 us -> 13.2 us  [flip_permute(): return lax.ppermute(value, axis, [(i, i ^ mask) for i in range(size)])]
    ppermute x1, starting transfers between devices: 0.65 us -> 1.63 us  [local_small(): lax.ppermute(residual.reshape(rows, columns), ('wide', 'narrow'), [(w * s...]
  transfers between devices with their start and end apart: 16 -> 16, of which waited for: 12 -> 11; matrix products, arithmetic and copies ran while one was open for 0% -> 0% of each run, Pallas kernels for 0% -> 0%
where the time goes in v7:
time: 53.7 us; the launch traced here: 53.4 us
  waiting for transfers between devices  22.5 us (42%)
  starting transfers between devices  18.9 us (35%)
  Pallas kernels  10.8 us (20%)
  other arithmetic  0.87 us (2%)
    ppermute x11, waiting for transfers between devices, flip_permute(): return lax.ppermute(value, axis, [(i, i ^ mask) for i in range(size)])  13.2 us
    ppermute x11, starting transfers between devices, flip_permute(): return lax.ppermute(value, axis, [(i, i ^ mask) for i in range(size)])  13 us
    pallas_call x1, Pallas kernels, local_small(): pl.pallas_call(expert_kernel, out_shape=(pltpu.VMEM((size * rows, model /...  7.94 us
    ppermute x1, waiting for transfers between devices, local_small(): lax.ppermute(residual.reshape(rows, columns), ('wide', 'narrow'), [(w * s...  5.18 us
    ppermute x4, starting transfers between devices, local_small(): lax.ppermute(total[s], ('wide', 'narrow'), [(i, i ^ s * size ^ (2 if i &...  4.27 us
    ppermute x4, waiting for transfers between devices, local_small(): lax.ppermute(total[s], ('wide', 'narrow'), [(i, i ^ s * size ^ (2 if i &...  4.13 us
    pallas_call x1, Pallas kernels, local_small(): pl.pallas_call(attend_kernel, out_shape=jax.ShapeDtypeStruct((rows, depth...  2 us
    ppermute x1, starting transfers between devices, local_small(): lax.ppermute(residual.reshape(rows, columns), ('wide', 'narrow'), [(w * s...  1.63 us
  transfers between devices with their start and end apart: 16, of which 11 were waited for; matrix products, arithmetic and copies ran while one was open for 0% of the time, Pallas kernels for 0%

profile of v7, /device:TPU:0, one launch (start us, length us, event | category | flops | bytes accessed | tf_op | source)
XLA Modules:
  0.0 53.4 jit_solution(12622138367211580507)
XLA Ops:
  0.0 2.0 %shard_map.118.own_ref = bf16[32,1152]{1,0:T(8,128)(2,1)S(1)} custom-call(s32[2,16]{1,0:T(2,128)} %refs_0_.1, bf16[256,128]{1,0:T(8,128)(2,1)} %bitcast.30, bf16[2048,128]{1,0:T(8,128)(2,1)} %bitcast.28, bf16[2048,128]{1,0:T(8,128)(2,1)} %bitcast.29, s32[2,8,16]{2,1,0:T(8,128)} %bitcast.32, f32[2,8,16]{2,1,0:T(8,128)} %bitcast.33), custom_call_target="tpu_custom_call" | custom-call | flops 20000000000 | bytes 1000000 | tf_op jit(solution)/shard_map/pallas_call | solution.py:355
  2.0 5.1 %collective-permute-start.2 = (bf16[32,1152]{1,0:T(8,128)(2,1)S(1)}, bf16[32,1152]{1,0:T(8,128)(2,1)S(1)}, u32[]{:S(2)}, u32[]{:S(2)}) collective-permute-start(bf16[32,1152]{1,0:T(8,128)(2,1)S(1)} %shard_map.118.own_ref), channel_id=1, source_target_pairs={{0,12},{4,8},{8,4},{12,0},{1,13},{5,9},{9,5},{13,1},{2,14},{6,10},... | collective-permute-start | bytes 221192 | tf_op jit(solution)/shard_map/ppermute | solution.py:153
  7.1 0.6 %collective-permute-start = (bf16[32,1152]{1,0:T(8,128)(2,1)S(1)}, bf16[32,1152]{1,0:T(8,128)(2,1)S(1)}, u32[]{:S(2)}, u32[]{:S(2)}) collective-permute-start(bf16[32,1152]{1,0:T(8,128)(2,1)S(1)} %shard_map.118.own_ref), channel_id=1, source_target_pairs={{0,4},{4,0},{8,12},{12,8},{1,5},{5,1},{9,13},{13,9},{2,6},{6,2},{1... | collective-permute-start | bytes 221192 | tf_op jit(solution)/shard_map/ppermute | solution.py:153
  7.8 1.6 %collective-permute-start.3 = (bf16[32,512]{1,0:T(8,128)(2,1)S(1)}, bf16[32,512]{1,0:T(8,128)(2,1)S(1)}, u32[]{:S(2)}, u32[]{:S(2)}) collective-permute-start(bf16[32,512]{1,0:T(8,128)(2,1)S(1)} %bitcast.31), channel_id=1, source_target_pairs={{0,2},{4,3},{8,0},{12,1},{5,6},{1,7},{9,4},{13,5},{10,8},{6,9},{14... | collective-permute-start | bytes 98312 | tf_op jit(solution)/shard_map/ppermute | solution.py:342
  9.6 5.2 %collective-permute-done.3.res_ref = bf16[32,512]{1,0:T(8,128)(2,1)S(1)} collective-permute-done((bf16[32,512]{1,0:T(8,128)(2,1)S(1)}, bf16[32,512]{1,0:T(8,128)(2,1)S(1)}, u32[]{:S(2)}, u32[]{:S(2)}) %collective-permute-start.3) | collective-permute-done | bytes 32800 | tf_op jit(solution)/shard_map/ppermute | solution.py:342
  14.8 0.9 %shard_map.119 = (f32[128,256]{1,0:T(8,128)S(1)}, bf16[128,256]{1,0:T(8,128)(2,1)S(1)}, bf16[128,128]{1,0:T(8,128)(2,1)S(1)}) custom-call(s32[3]{0:T(128)S(1)} %pad_add_fusion.where_ref, bf16[32,1152]{1,0:T(8,128)(2,1)S(1)} %shard_map.118.own_ref, bf16[32,1152]{1,0:T(8,128)(2,1)S(1)} %collective-permute-done.got1_ref, ...), custom_call_target="tpu_custom_call" | custom-call | flops 30000001024 | bytes 1000000 | tf_op jit(solution)/shard_map/pallas_call | solution.py:368
  15.7 1.2 %collective-permute-done.4 = bf16[128,256]{1,0:T(8,128)(2,1)S(1)} collective-permute-done((bf16[128,256]{1,0:T(8,128)(2,1)S(1)}, bf16[128,256]{1,0:T(8,128)(2,1)S(1)}, u32[]{:S(2)}, u32[]{:S(2)}) %collective-permute-start.4) | collective-permute-done | bytes 65568 | tf_op jit(solution)/shard_map/ppermute | solution.py:153
  17.1 4.2 %collective-permute-done.5 = bf16[128,256]{1,0:T(8,128)(2,1)S(1)} collective-permute-done((bf16[128,256]{1,0:T(8,128)(2,1)S(1)}, bf16[128,256]{1,0:T(8,128)(2,1)S(1)}, u32[]{:S(2)}, u32[]{:S(2)}) %collective-permute-start.5) | collective-permute-done | bytes 65568 | tf_op jit(solution)/shard_map/ppermute | solution.py:153
  21.4 2.1 %collective-permute-start.8 = (bf16[128,256]{1,0:T(8,128)(2,1)S(1)}, bf16[128,256]{1,0:T(8,128)(2,1)S(1)}, u32[]{:S(2)}, u32[]{:S(2)}) collective-permute-start(bf16[128,256]{1,0:T(8,128)(2,1)S(1)} %add_convert_fusion.1), channel_id=1, source_target_pairs={{0,12},{4,8},{8,4},{12,0},{1,13},{5,9},{9,5},{13,1},{2,14},{6,10},... | collective-permute-start | bytes 196616 | tf_op jit(solution)/shard_map/ppermute | solution.py:153
  23.8 2.0 %collective-permute-start.6 = (bf16[128,256]{1,0:T(8,128)(2,1)S(1)}, bf16[128,256]{1,0:T(8,128)(2,1)S(1)}, u32[]{:S(2)}, u32[]{:S(2)}) collective-permute-start(bf16[128,256]{1,0:T(8,128)(2,1)S(1)} %add_convert_fusion.1), channel_id=1, source_target_pairs={{0,4},{4,0},{8,12},{12,8},{1,5},{5,1},{9,13},{13,9},{2,6},{6,2},{1... | collective-permute-start | bytes 196616 | tf_op jit(solution)/shard_map/ppermute | solution.py:153
  25.8 2.5 %collective-permute-done.8 = bf16[128,256]{1,0:T(8,128)(2,1)S(1)} collective-permute-done((bf16[128,256]{1,0:T(8,128)(2,1)S(1)}, bf16[128,256]{1,0:T(8,128)(2,1)S(1)}, u32[]{:S(2)}, u32[]{:S(2)}) %collective-permute-start.8) | collective-permute-done | bytes 65568 | tf_op jit(solution)/shard_map/ppermute | solution.py:153
  28.3 1.5 %collective-permute-done.7 = bf16[128,256]{1,0:T(8,128)(2,1)S(1)} collective-permute-done((bf16[128,256]{1,0:T(8,128)(2,1)S(1)}, bf16[128,256]{1,0:T(8,128)(2,1)S(1)}, u32[]{:S(2)}, u32[]{:S(2)}) %collective-permute-start.7) | collective-permute-done | bytes 65568 | tf_op jit(solution)/shard_map/ppermute | solution.py:153
  29.9 1.5 %collective-permute-done.9.other_ref = bf16[4,128,256]{2,1,0:T(8,128)(2,1)S(1)} collective-permute-done((bf16[4,128,256]{2,1,0:T(8,128)(2,1)S(1)}, bf16[4,128,256]{2,1,0:T(8,128)(2,1)S(1)}, u32[]{:S(2)}, u32[]{:S(2)}) %collective-permute-start.9) | collective-permute-done | bytes 262176 | tf_op jit(solution)/shard_map/ppermute | solution.py:153
  31.5 7.9 %shard_map.120 = (f32[128,1024]{1,0:T(8,128)S(1)}, bf16[128,1024]{1,0:T(8,128)(2,1)S(1)}, bf16[32,512]{1,0:T(8,128)(2,1)S(1)}) custom-call(s32[3]{0:T(128)} %copy-done, bf16[4,128,256]{2,1,0:T(8,128)(2,1)S(1)} %pad_maximum_fusion.mine_ref, bf16[4,128,256]{2,1,0:T(8,128)(2,1)S(1)} %collective-permute-done.9.other_ref, ...), custom_call_target="tpu_custom_call" | custom-call | tf_op jit(solution)/shard_map/pallas_call | solution.py:390
  39.7 1.4 %collective-permute-done.10 = bf16[128,1024]{1,0:T(8,128)(2,1)S(1)} collective-permute-done((bf16[128,1024]{1,0:T(8,128)(2,1)S(1)}, bf16[128,1024]{1,0:T(8,128)(2,1)S(1)}, u32[]{:S(2)}, u32[]{:S(2)}) %collective-permute-start.10) | collective-permute-done | bytes 262176 | tf_op jit(solution)/shard_map/ppermute | solution.py:153
  41.2 1.1 %collective-permute-start.11 = (bf16[32,1024]{1,0:T(8,128)(2,1)S(1)}, bf16[32,1024]{1,0:T(8,128)(2,1)S(1)}, u32[]{:S(2)}, u32[]{:S(2)}) collective-permute-start(bf16[32,1024]{1,0:T(8,128)(2,1)S(1)} %get-tuple-element.17), channel_id=1, source_target_pairs={{0,8},{1,11},{2,10},{3,9},{4,12},{5,15},{6,14},{7,13},{8,0},{9,3},... | collective-permute-start | bytes 196616 | tf_op jit(solution)/shard_map/ppermute | solution.py:414
  42.2 0.7 %collective-permute-start.14 = (bf16[32,1024]{1,0:T(8,128)(2,1)S(1)}, bf16[32,1024]{1,0:T(8,128)(2,1)S(1)}, u32[]{:S(2)}, u32[]{:S(2)}) collective-permute-start(bf16[32,1024]{1,0:T(8,128)(2,1)S(1)} %get-tuple-element.18), channel_id=1, source_target_pairs={{0,0},{1,3},{2,2},{3,1},{4,4},{5,7},{6,6},{7,5},{8,8},{9,11},{10,1... | collective-permute-start | bytes 196616 | tf_op jit(solution)/shard_map/ppermute | solution.py:414
  42.9 1.7 %collective-permute-start.13 = (bf16[32,1024]{1,0:T(8,128)(2,1)S(1)}, bf16[32,1024]{1,0:T(8,128)(2,1)S(1)}, u32[]{:S(2)}, u32[]{:S(2)}) collective-permute-start(bf16[32,1024]{1,0:T(8,128)(2,1)S(1)} %get-tuple-element.19), channel_id=1, source_target_pairs={{0,12},{1,15},{2,14},{3,13},{4,8},{5,11},{6,10},{7,9},{8,4},{9,7},... | collective-permute-start | bytes 196616 | tf_op jit(solution)/shard_map/ppermute | solution.py:414
  44.6 0.8 %collective-permute-start.12 = (bf16[32,1024]{1,0:T(8,128)(2,1)S(1)}, bf16[32,1024]{1,0:T(8,128)(2,1)S(1)}, u32[]{:S(2)}, u32[]{:S(2)}) collective-permute-start(bf16[32,1024]{1,0:T(8,128)(2,1)S(1)} %get-tuple-element.20), channel_id=1, source_target_pairs={{0,4},{1,7},{2,6},{3,5},{4,0},{5,3},{6,2},{7,1},{8,12},{9,15},{10,... | collective-permute-start | bytes 196616 | tf_op jit(solution)/shard_map/ppermute | solution.py:414
  45.5 2.5 %collective-permute-done.11 = bf16[32,1024]{1,0:T(8,128)(2,1)S(1)} collective-permute-done((bf16[32,1024]{1,0:T(8,128)(2,1)S(1)}, bf16[32,1024]{1,0:T(8,128)(2,1)S(1)}, u32[]{:S(2)}, u32[]{:S(2)}) %collective-permute-start.11) | collective-permute-done | bytes 65568 | tf_op jit(solution)/shard_map/ppermute | solution.py:414
  47.9 1.3 %collective-permute-done.13 = bf16[32,1024]{1,0:T(8,128)(2,1)S(1)} collective-permute-done((bf16[32,1024]{1,0:T(8,128)(2,1)S(1)}, bf16[32,1024]{1,0:T(8,128)(2,1)S(1)}, u32[]{:S(2)}, u32[]{:S(2)}) %collective-permute-start.13) | collective-permute-done | bytes 65568 | tf_op jit(solution)/shard_map/ppermute | solution.py:414
  49.6 2.3 %collective-permute-start.15 = (bf16[32,512]{1,0:T(8,128)(2,1)S(1)}, bf16[32,512]{1,0:T(8,128)(2,1)S(1)}, u32[]{:S(2)}, u32[]{:S(2)}) collective-permute-start(bf16[32,512]{1,0:T(8,128)(2,1)S(1)} %select_convert_fusion), channel_id=1, source_target_pairs={{0,1},{1,0},{2,3},{3,2},{4,5},{5,4},{6,7},{7,6},{8,9},{9,8},{10,11... | collective-permute-start | bytes 98312 | tf_op jit(solution)/shard_map/ppermute | solution.py:153
  51.9 0.9 %collective-permute-done.15 = bf16[32,512]{1,0:T(8,128)(2,1)S(1)} collective-permute-done((bf16[32,512]{1,0:T(8,128)(2,1)S(1)}, bf16[32,512]{1,0:T(8,128)(2,1)S(1)}, u32[]{:S(2)}, u32[]{:S(2)}) %collective-permute-start.15) | collective-permute-done | bytes 32800 | tf_op jit(solution)/shard_map/ppermute | solution.py:153
  52.8 0.6 %add_convert_fusion.3 = bf16[32,512]{1,0:T(8,128)(2,1)} fusion(bf16[32,512]{1,0:T(8,128)(2,1)S(1)} %collective-permute-done.15, bf16[32,512]{1,0:T(8,128)(2,1)S(1)} %get-tuple-element.14, f32[32,1024]{1,0:T(8,128)S(1)} %convert_add_fusion, pred[]{:T(512)S(6)} %eq.26), kind=kLoop, calls=%fused_computation.5 | loop fusion | flops 98304 | bytes 229377 | tf_op jit(solution)/shard_map/convert_element_type | solution.py:426
  (53 shorter events, 1.6 us)
Async XLA Ops:
  2.0 12.7 %collective-permute-start.2 = (bf16[32,1152]{1,0:T(8,128)(2,1)S(1)}, bf16[32,1152]{1,0:T(8,128)(2,1)S(1)}, u32[]{:S(2)}, u32[]{:S(2)}) collective-permute-start(bf16[32,1152]{1,0:T(8,128)(2,1)S(1)} %shard_map.118.own_ref), channel_id=1, source_target_pairs={{0,12},{4,8},{8,4},{12,0},{1,13},{5,9},{9,5},{13,1},{2,14},{6,10},... | collective-permute-start | bytes 221192 | tf_op jit(solution)/shard_map/ppermute | solution.py:153
  7.1 7.6 %collective-permute-start.1 = (bf16[32,1152]{1,0:T(8,128)(2,1)S(1)}, bf16[32,1152]{1,0:T(8,128)(2,1)S(1)}, u32[]{:S(2)}, u32[]{:S(2)}) collective-permute-start(bf16[32,1152]{1,0:T(8,128)(2,1)S(1)} %shard_map.118.own_ref), channel_id=1, source_target_pairs={{0,8},{4,12},{8,0},{12,4},{1,9},{5,13},{9,1},{13,5},{2,10},{6,14},... | collective-permute-start | bytes 221192 | tf_op jit(solution)/shard_map/ppermute | solution.py:153
  7.1 7.6 %collective-permute-start = (bf16[32,1152]{1,0:T(8,128)(2,1)S(1)}, bf16[32,1152]{1,0:T(8,128)(2,1)S(1)}, u32[]{:S(2)}, u32[]{:S(2)}) collective-permute-start(bf16[32,1152]{1,0:T(8,128)(2,1)S(1)} %shard_map.118.own_ref), channel_id=1, source_target_pairs={{0,4},{4,0},{8,12},{12,8},{1,5},{5,1},{9,13},{13,9},{2,6},{6,2},{1... | collective-permute-start | bytes 221192 | tf_op jit(solution)/shard_map/ppermute | solution.py:153
  7.8 7.0 %collective-permute-start.3 = (bf16[32,512]{1,0:T(8,128)(2,1)S(1)}, bf16[32,512]{1,0:T(8,128)(2,1)S(1)}, u32[]{:S(2)}, u32[]{:S(2)}) collective-permute-start(bf16[32,512]{1,0:T(8,128)(2,1)S(1)} %bitcast.31), channel_id=1, source_target_pairs={{0,2},{4,3},{8,0},{12,1},{5,6},{1,7},{9,4},{13,5},{10,8},{6,9},{14... | collective-permute-start | bytes 98312 | tf_op jit(solution)/shard_map/ppermute | solution.py:342
  9.4 22.0 %slice-start = ((s8[16777216]{0:T(1024)(128)(4,1)}), s8[4194304]{0:T(1024)(128)(4,1)S(1)}, s32[]{:S(2)}) async-start(s8[16777216]{0:T(1024)(128)(4,1)} %bitcast.16), calls=%async_computation | async-start | bytes 8388608
  9.4 22.0 %slice-start.4 = ((s8[16777216]{0:T(1024)(128)(4,1)}), s8[4194304]{0:T(1024)(128)(4,1)S(1)}, s32[]{:S(2)}) async-start(s8[16777216]{0:T(1024)(128)(4,1)} %bitcast.18), calls=%async_computation.4 | async-start | bytes 8388608
  9.4 22.0 %slice-start.8 = ((s8[16777216]{0:T(1024)(128)(4,1)}), s8[4194304]{0:T(1024)(128)(4,1)S(1)}, s32[]{:S(2)}) async-start(s8[16777216]{0:T(1024)(128)(4,1)} %bitcast.20), calls=%async_computation.8 | async-start | bytes 8388608
  9.5 22.0 %slice-start.3 = ((s8[16777216]{0:T(1024)(128)(4,1)}), s8[4194304]{0:T(1024)(128)(4,1)S(1)}, s32[]{:S(2)}) async-start(s8[16777216]{0:T(1024)(128)(4,1)} %bitcast.16), calls=%async_computation.3 | async-start | bytes 8388608
  9.5 22.0 %slice-start.5 = ((s8[16777216]{0:T(1024)(128)(4,1)}), s8[4194304]{0:T(1024)(128)(4,1)S(1)}, s32[]{:S(2)}) async-start(s8[16777216]{0:T(1024)(128)(4,1)} %bitcast.18), calls=%async_computation.5 | async-start | bytes 8388608
  9.5 22.0 %slice-start.6 = ((s8[16777216]{0:T(1024)(128)(4,1)}), s8[4194304]{0:T(1024)(128)(4,1)S(1)}, s32[]{:S(2)}) async-start(s8[16777216]{0:T(1024)(128)(4,1)} %bitcast.18), calls=%async_computation.6 | async-start | bytes 8388608
  9.5 22.0 %slice-start.7 = ((s8[16777216]{0:T(1024)(128)(4,1)}), s8[4194304]{0:T(1024)(128)(4,1)S(1)}, s32[]{:S(2)}) async-start(s8[16777216]{0:T(1024)(128)(4,1)} %bitcast.18), calls=%async_computation.7 | async-start | bytes 8388608
  9.5 22.0 %slice-start.9 = ((s8[16777216]{0:T(1024)(128)(4,1)}), s8[4194304]{0:T(1024)(128)(4,1)S(1)}, s32[]{:S(2)}) async-start(s8[16777216]{0:T(1024)(128)(4,1)} %bitcast.20), calls=%async_computation.9 | async-start | bytes 8388608
  15.7 1.3 %collective-permute-start.4 = (bf16[128,256]{1,0:T(8,128)(2,1)S(1)}, bf16[128,256]{1,0:T(8,128)(2,1)S(1)}, u32[]{:S(2)}, u32[]{:S(2)}) collective-permute-start(bf16[128,256]{1,0:T(8,128)(2,1)S(1)} %get-tuple-element.12), channel_id=1, source_target_pairs={{0,1},{1,0},{2,3},{3,2},{4,5},{5,4},{6,7},{7,6},{8,9},{9,8},{10,11... | collective-permute-start | bytes 196616 | tf_op jit(solution)/shard_map/ppermute | solution.py:153
  17.0 4.3 %collective-permute-start.5 = (bf16[128,256]{1,0:T(8,128)(2,1)S(1)}, bf16[128,256]{1,0:T(8,128)(2,1)S(1)}, u32[]{:S(2)}, u32[]{:S(2)}) collective-permute-start(bf16[128,256]{1,0:T(8,128)(2,1)S(1)} %add_convert_fusion.2), channel_id=1, source_target_pairs={{0,2},{1,3},{2,0},{3,1},{4,6},{5,7},{6,4},{7,5},{8,10},{9,11},{10,... | collective-permute-start | bytes 196616 | tf_op jit(solution)/shard_map/ppermute | solution.py:153
  21.4 6.9 %collective-permute-start.8 = (bf16[128,256]{1,0:T(8,128)(2,1)S(1)}, bf16[128,256]{1,0:T(8,128)(2,1)S(1)}, u32[]{:S(2)}, u32[]{:S(2)}) collective-permute-start(bf16[128,256]{1,0:T(8,128)(2,1)S(1)} %add_convert_fusion.1), channel_id=1, source_target_pairs={{0,12},{4,8},{8,4},{12,0},{1,13},{5,9},{9,5},{13,1},{2,14},{6,10},... | collective-permute-start | bytes 196616 | tf_op jit(solution)/shard_map/ppermute | solution.py:153
  23.4 6.4 %collective-permute-start.7 = (bf16[128,256]{1,0:T(8,128)(2,1)S(1)}, bf16[128,256]{1,0:T(8,128)(2,1)S(1)}, u32[]{:S(2)}, u32[]{:S(2)}) collective-permute-start(bf16[128,256]{1,0:T(8,128)(2,1)S(1)} %add_convert_fusion.1), channel_id=1, source_target_pairs={{0,8},{4,12},{8,0},{12,4},{1,9},{5,13},{9,1},{13,5},{2,10},{6,14},... | collective-permute-start | bytes 196616 | tf_op jit(solution)/shard_map/ppermute | solution.py:153
  23.8 6.0 %collective-permute-start.6 = (bf16[128,256]{1,0:T(8,128)(2,1)S(1)}, bf16[128,256]{1,0:T(8,128)(2,1)S(1)}, u32[]{:S(2)}, u32[]{:S(2)}) collective-permute-start(bf16[128,256]{1,0:T(8,128)(2,1)S(1)} %add_convert_fusion.1), channel_id=1, source_target_pairs={{0,4},{4,0},{8,12},{12,8},{1,5},{5,1},{9,13},{13,9},{2,6},{6,2},{1... | collective-permute-start | bytes 196616 | tf_op jit(solution)/shard_map/ppermute | solution.py:153
  29.8 1.6 %collective-permute-start.9 = (bf16[4,128,256]{2,1,0:T(8,128)(2,1)S(1)}, bf16[4,128,256]{2,1,0:T(8,128)(2,1)S(1)}, u32[]{:S(2)}, u32[]{:S(2)}) collective-permute-start(bf16[4,128,256]{2,1,0:T(8,128)(2,1)S(1)} %pad_maximum_fusion.mine_ref), channel_id=1, source_target_pairs={{0,1},{1,0},{2,3},{3,2},{4,5},{5,4},{6,7},{7,6},{8,9},{9,8},{10,11... | collective-permute-start | bytes 786440 | tf_op jit(solution)/shard_map/ppermute | solution.py:153
  39.5 1.6 %collective-permute-start.10 = (bf16[128,1024]{1,0:T(8,128)(2,1)S(1)}, bf16[128,1024]{1,0:T(8,128)(2,1)S(1)}, u32[]{:S(2)}, u32[]{:S(2)}) collective-permute-start(bf16[128,1024]{1,0:T(8,128)(2,1)S(1)} %get-tuple-element.16), channel_id=1, source_target_pairs={{0,1},{1,0},{2,3},{3,2},{4,5},{5,4},{6,7},{7,6},{8,9},{9,8},{10,11... | collective-permute-start | bytes 786440 | tf_op jit(solution)/shard_map/ppermute | solution.py:153
  41.2 6.8 %collective-permute-start.11 = (bf16[32,1024]{1,0:T(8,128)(2,1)S(1)}, bf16[32,1024]{1,0:T(8,128)(2,1)S(1)}, u32[]{:S(2)}, u32[]{:S(2)}) collective-permute-start(bf16[32,1024]{1,0:T(8,128)(2,1)S(1)} %get-tuple-element.17), channel_id=1, source_target_pairs={{0,8},{1,11},{2,10},{3,9},{4,12},{5,15},{6,14},{7,13},{8,0},{9,3},... | collective-permute-start | bytes 196616 | tf_op jit(solution)/shard_map/ppermute | solution.py:414
  42.2 5.7 %collective-permute-start.14 = (bf16[32,1024]{1,0:T(8,128)(2,1)S(1)}, bf16[32,1024]{1,0:T(8,128)(2,1)S(1)}, u32[]{:S(2)}, u32[]{:S(2)}) collective-permute-start(bf16[32,1024]{1,0:T(8,128)(2,1)S(1)} %get-tuple-element.18), channel_id=1, source_target_pairs={{0,0},{1,3},{2,2},{3,1},{4,4},{5,7},{6,6},{7,5},{8,8},{9,11},{10,1... | collective-permute-start | bytes 196616 | tf_op jit(solution)/shard_map/ppermute | solution.py:414
  42.9 6.3 %collective-permute-start.13 = (bf16[32,1024]{1,0:T(8,128)(2,1)S(1)}, bf16[32,1024]{1,0:T(8,128)(2,1)S(1)}, u32[]{:S(2)}, u32[]{:S(2)}) collective-permute-start(bf16[32,1024]{1,0:T(8,128)(2,1)S(1)} %get-tuple-element.19), channel_id=1, source_target_pairs={{0,12},{1,15},{2,14},{3,13},{4,8},{5,11},{6,10},{7,9},{8,4},{9,7},... | collective-permute-start | bytes 196616 | tf_op jit(solution)/shard_map/ppermute | solution.py:414
  44.6 5.0 %collective-permute-start.12 = (bf16[32,1024]{1,0:T(8,128)(2,1)S(1)}, bf16[32,1024]{1,0:T(8,128)(2,1)S(1)}, u32[]{:S(2)}, u32[]{:S(2)}) collective-permute-start(bf16[32,1024]{1,0:T(8,128)(2,1)S(1)} %get-tuple-element.20), channel_id=1, source_target_pairs={{0,4},{1,7},{2,6},{3,5},{4,0},{5,3},{6,2},{7,1},{8,12},{9,15},{10,... | collective-permute-start | bytes 196616 | tf_op jit(solution)/shard_map/ppermute | solution.py:414
  49.6 3.2 %collective-permute-start.15 = (bf16[32,512]{1,0:T(8,128)(2,1)S(1)}, bf16[32,512]{1,0:T(8,128)(2,1)S(1)}, u32[]{:S(2)}, u32[]{:S(2)}) collective-permute-start(bf16[32,512]{1,0:T(8,128)(2,1)S(1)} %select_convert_fusion), channel_id=1, source_target_pairs={{0,1},{1,0},{2,3},{3,2},{4,5},{5,4},{6,7},{7,6},{8,9},{9,8},{10,11... | collective-permute-start | bytes 98312 | tf_op jit(solution)/shard_map/ppermute | solution.py:153
  (7 other events, 116.5 us)

commit v8 on v7

--- a/solution.py
+++ b/solution.py
@@ -416,7 +416,7 @@
             ("wide", "narrow"),
             [(i, i ^ (s * size) ^ (2 if i & 1 else 0)) for i in devices],
         ).astype(jnp.float32)
-        for s in (2, 1, 3, 0)
+        for s in (2, 0, 1, 3)
     ]
     summed = got[0] + got[1] + got[2] + got[3]
     first = (narrow & 1) == 0

time: 53.7 us -> 52.9 us (0.985)
  starting transfers between devices: 18.9 us -> 16.8 us
  waiting for transfers between devices: 22.5 us -> 23.9 us
    ppermute x11, starting transfers between devices: 13 us -> 10.9 us  [flip_permute(): return lax.ppermute(value, axis, [(i, i ^ mask) for i in range(size)])]
    ppermute x4, waiting for transfers between devices: 4.13 us -> 5.34 us  [local_small(): lax.ppermute(total[s], ('wide', 'narrow'), [(i, i ^ s * size ^ (2 if i &...]
  transfers between devices with their start and end apart: 16 -> 16, of which waited for: 11 -> 10; matrix products, arithmetic and copies ran while one was open for 0% -> 0% of each run, Pallas kernels for 0% -> 0%
where the time goes in v8:
time: 52.9 us; the launch traced here: 52.7 us
  waiting for transfers between devices  23.9 us (45%)
  starting transfers between devices  16.8 us (32%)
  Pallas kernels  10.8 us (20%)
  other arithmetic  0.87 us (2%)
    ppermute x11, waiting for transfers between devices, flip_permute(): return lax.ppermute(value, axis, [(i, i ^ mask) for i in range(size)])  13.4 us
    ppermute x11, starting transfers between devices, flip_permute(): return lax.ppermute(value, axis, [(i, i ^ mask) for i in range(size)])  10.9 us
    pallas_call x1, Pallas kernels, local_small(): pl.pallas_call(expert_kernel, out_shape=(pltpu.VMEM((size * rows, model /...  7.94 us
    ppermute x4, waiting for transfers between devices, local_small(): lax.ppermute(total[s], ('wide', 'narrow'), [(i, i ^ s * size ^ (2 if i &...  5.34 us
    ppermute x1, waiting for transfers between devices, local_small(): lax.ppermute(residual.reshape(rows, columns), ('wide', 'narrow'), [(w * s...  5.18 us
    ppermute x4, starting transfers between devices, local_small(): lax.ppermute(total[s], ('wide', 'narrow'), [(i, i ^ s * size ^ (2 if i &...  4.21 us
    pallas_call x1, Pallas kernels, local_small(): pl.pallas_call(attend_kernel, out_shape=jax.ShapeDtypeStruct((rows, depth...  2 us
    ppermute x1, starting transfers between devices, local_small(): lax.ppermute(residual.reshape(rows, columns), ('wide', 'narrow'), [(w * s...  1.63 us
  transfers between devices with their start and end apart: 16, of which 10 were waited for; matrix products, arithmetic and copies ran while one was open for 0% of the time, Pallas kernels for 0%

profile of v8, /device:TPU:0, one launch (start us, length us, event | category | flops | bytes accessed | tf_op | source)
XLA Modules:
  0.0 52.7 jit_solution(15092236865024993264)
XLA Ops:
  0.0 2.0 %shard_map.118.own_ref = bf16[32,1152]{1,0:T(8,128)(2,1)S(1)} custom-call(s32[2,16]{1,0:T(2,128)} %refs_0_.1, bf16[256,128]{1,0:T(8,128)(2,1)} %bitcast.30, bf16[2048,128]{1,0:T(8,128)(2,1)} %bitcast.28, bf16[2048,128]{1,0:T(8,128)(2,1)} %bitcast.29, s32[2,8,16]{2,1,0:T(8,128)} %bitcast.32, f32[2,8,16]{2,1,0:T(8,128)} %bitcast.33), custom_call_target="tpu_custom_call" | custom-call | flops 20000000000 | bytes 1000000 | tf_op jit(solution)/shard_map/pallas_call | solution.py:355
  2.0 5.1 %collective-permute-start.2 = (bf16[32,1152]{1,0:T(8,128)(2,1)S(1)}, bf16[32,1152]{1,0:T(8,128)(2,1)S(1)}, u32[]{:S(2)}, u32[]{:S(2)}) collective-permute-start(bf16[32,1152]{1,0:T(8,128)(2,1)S(1)} %shard_map.118.own_ref), channel_id=1, source_target_pairs={{0,12},{4,8},{8,4},{12,0},{1,13},{5,9},{9,5},{13,1},{2,14},{6,10},... | collective-permute-start | bytes 221192 | tf_op jit(solution)/shard_map/ppermute | solution.py:153
  7.1 0.6 %collective-permute-start = (bf16[32,1152]{1,0:T(8,128)(2,1)S(1)}, bf16[32,1152]{1,0:T(8,128)(2,1)S(1)}, u32[]{:S(2)}, u32[]{:S(2)}) collective-permute-start(bf16[32,1152]{1,0:T(8,128)(2,1)S(1)} %shard_map.118.own_ref), channel_id=1, source_target_pairs={{0,4},{4,0},{8,12},{12,8},{1,5},{5,1},{9,13},{13,9},{2,6},{6,2},{1... | collective-permute-start | bytes 221192 | tf_op jit(solution)/shard_map/ppermute | solution.py:153
  7.8 1.6 %collective-permute-start.3 = (bf16[32,512]{1,0:T(8,128)(2,1)S(1)}, bf16[32,512]{1,0:T(8,128)(2,1)S(1)}, u32[]{:S(2)}, u32[]{:S(2)}) collective-permute-start(bf16[32,512]{1,0:T(8,128)(2,1)S(1)} %bitcast.31), channel_id=1, source_target_pairs={{0,2},{4,3},{8,0},{12,1},{5,6},{1,7},{9,4},{13,5},{10,8},{6,9},{14... | collective-permute-start | bytes 98312 | tf_op jit(solution)/shard_map/ppermute | solution.py:342
  9.6 5.2 %collective-permute-done.3.res_ref = bf16[32,512]{1,0:T(8,128)(2,1)S(1)} collective-permute-done((bf16[32,512]{1,0:T(8,128)(2,1)S(1)}, bf16[32,512]{1,0:T(8,128)(2,1)S(1)}, u32[]{:S(2)}, u32[]{:S(2)}) %collective-permute-start.3) | collective-permute-done | bytes 32800 | tf_op jit(solution)/shard_map/ppermute | solution.py:342
  14.8 0.9 %shard_map.119 = (f32[128,256]{1,0:T(8,128)S(1)}, bf16[128,256]{1,0:T(8,128)(2,1)S(1)}, bf16[128,128]{1,0:T(8,128)(2,1)S(1)}) custom-call(s32[3]{0:T(128)S(1)} %pad_add_fusion.where_ref, bf16[32,1152]{1,0:T(8,128)(2,1)S(1)} %shard_map.118.own_ref, bf16[32,1152]{1,0:T(8,128)(2,1)S(1)} %collective-permute-done.got1_ref, ...), custom_call_target="tpu_custom_call" | custom-call | flops 30000001024 | bytes 1000000 | tf_op jit(solution)/shard_map/pallas_call | solution.py:368
  15.7 1.2 %collective-permute-done.4 = bf16[128,256]{1,0:T(8,128)(2,1)S(1)} collective-permute-done((bf16[128,256]{1,0:T(8,128)(2,1)S(1)}, bf16[128,256]{1,0:T(8,128)(2,1)S(1)}, u32[]{:S(2)}, u32[]{:S(2)}) %collective-permute-start.4) | collective-permute-done | bytes 65568 | tf_op jit(solution)/shard_map/ppermute | solution.py:153
  17.1 4.2 %collective-permute-done.5 = bf16[128,256]{1,0:T(8,128)(2,1)S(1)} collective-permute-done((bf16[128,256]{1,0:T(8,128)(2,1)S(1)}, bf16[128,256]{1,0:T(8,128)(2,1)S(1)}, u32[]{:S(2)}, u32[]{:S(2)}) %collective-permute-start.5) | collective-permute-done | bytes 65568 | tf_op jit(solution)/shard_map/ppermute | solution.py:153
  21.4 2.1 %collective-permute-start.8 = (bf16[128,256]{1,0:T(8,128)(2,1)S(1)}, bf16[128,256]{1,0:T(8,128)(2,1)S(1)}, u32[]{:S(2)}, u32[]{:S(2)}) collective-permute-start(bf16[128,256]{1,0:T(8,128)(2,1)S(1)} %add_convert_fusion.1), channel_id=1, source_target_pairs={{0,12},{4,8},{8,4},{12,0},{1,13},{5,9},{9,5},{13,1},{2,14},{6,10},... | collective-permute-start | bytes 196616 | tf_op jit(solution)/shard_map/ppermute | solution.py:153
  23.4 0.4 collective-permute-start.7
  23.8 2.0 %collective-permute-start.6 = (bf16[128,256]{1,0:T(8,128)(2,1)S(1)}, bf16[128,256]{1,0:T(8,128)(2,1)S(1)}, u32[]{:S(2)}, u32[]{:S(2)}) collective-permute-start(bf16[128,256]{1,0:T(8,128)(2,1)S(1)} %add_convert_fusion.1), channel_id=1, source_target_pairs={{0,4},{4,0},{8,12},{12,8},{1,5},{5,1},{9,13},{13,9},{2,6},{6,2},{1... | collective-permute-start | bytes 196616 | tf_op jit(solution)/shard_map/ppermute | solution.py:153
  25.8 2.5 %collective-permute-done.8 = bf16[128,256]{1,0:T(8,128)(2,1)S(1)} collective-permute-done((bf16[128,256]{1,0:T(8,128)(2,1)S(1)}, bf16[128,256]{1,0:T(8,128)(2,1)S(1)}, u32[]{:S(2)}, u32[]{:S(2)}) %collective-permute-start.8) | collective-permute-done | bytes 65568 | tf_op jit(solution)/shard_map/ppermute | solution.py:153
  28.3 1.5 %collective-permute-done.7 = bf16[128,256]{1,0:T(8,128)(2,1)S(1)} collective-permute-done((bf16[128,256]{1,0:T(8,128)(2,1)S(1)}, bf16[128,256]{1,0:T(8,128)(2,1)S(1)}, u32[]{:S(2)}, u32[]{:S(2)}) %collective-permute-start.7) | collective-permute-done | bytes 65568 | tf_op jit(solution)/shard_map/ppermute | solution.py:153
  29.9 1.5 %collective-permute-done.9.other_ref = bf16[4,128,256]{2,1,0:T(8,128)(2,1)S(1)} collective-permute-done((bf16[4,128,256]{2,1,0:T(8,128)(2,1)S(1)}, bf16[4,128,256]{2,1,0:T(8,128)(2,1)S(1)}, u32[]{:S(2)}, u32[]{:S(2)}) %collective-permute-start.9) | collective-permute-done | bytes 262176 | tf_op jit(solution)/shard_map/ppermute | solution.py:153
  31.5 7.9 %shard_map.120 = (f32[128,1024]{1,0:T(8,128)S(1)}, bf16[128,1024]{1,0:T(8,128)(2,1)S(1)}, bf16[32,512]{1,0:T(8,128)(2,1)S(1)}) custom-call(s32[3]{0:T(128)} %copy-done, bf16[4,128,256]{2,1,0:T(8,128)(2,1)S(1)} %pad_maximum_fusion.mine_ref, bf16[4,128,256]{2,1,0:T(8,128)(2,1)S(1)} %collective-permute-done.9.other_ref, ...), custom_call_target="tpu_custom_call" | custom-call | tf_op jit(solution)/shard_map/pallas_call | solution.py:390
  39.7 1.4 %collective-permute-done.10 = bf16[128,1024]{1,0:T(8,128)(2,1)S(1)} collective-permute-done((bf16[128,1024]{1,0:T(8,128)(2,1)S(1)}, bf16[128,1024]{1,0:T(8,128)(2,1)S(1)}, u32[]{:S(2)}, u32[]{:S(2)}) %collective-permute-start.10) | collective-permute-done | bytes 262176 | tf_op jit(solution)/shard_map/ppermute | solution.py:153
  41.2 1.1 %collective-permute-start.11 = (bf16[32,1024]{1,0:T(8,128)(2,1)S(1)}, bf16[32,1024]{1,0:T(8,128)(2,1)S(1)}, u32[]{:S(2)}, u32[]{:S(2)}) collective-permute-start(bf16[32,1024]{1,0:T(8,128)(2,1)S(1)} %get-tuple-element.17), channel_id=1, source_target_pairs={{0,8},{1,11},{2,10},{3,9},{4,12},{5,15},{6,14},{7,13},{8,0},{9,3},... | collective-permute-start | bytes 196616 | tf_op jit(solution)/shard_map/ppermute | solution.py:414
  42.2 1.7 %collective-permute-start.14 = (bf16[32,1024]{1,0:T(8,128)(2,1)S(1)}, bf16[32,1024]{1,0:T(8,128)(2,1)S(1)}, u32[]{:S(2)}, u32[]{:S(2)}) collective-permute-start(bf16[32,1024]{1,0:T(8,128)(2,1)S(1)} %get-tuple-element.18), channel_id=1, source_target_pairs={{0,12},{1,15},{2,14},{3,13},{4,8},{5,11},{6,10},{7,9},{8,4},{9,7},... | collective-permute-start | bytes 196616 | tf_op jit(solution)/shard_map/ppermute | solution.py:414
  43.9 0.8 %collective-permute-start.13 = (bf16[32,1024]{1,0:T(8,128)(2,1)S(1)}, bf16[32,1024]{1,0:T(8,128)(2,1)S(1)}, u32[]{:S(2)}, u32[]{:S(2)}) collective-permute-start(bf16[32,1024]{1,0:T(8,128)(2,1)S(1)} %get-tuple-element.19), channel_id=1, source_target_pairs={{0,4},{1,7},{2,6},{3,5},{4,0},{5,3},{6,2},{7,1},{8,12},{9,15},{10,... | collective-permute-start | bytes 196616 | tf_op jit(solution)/shard_map/ppermute | solution.py:414
  44.7 0.7 %collective-permute-start.12 = (bf16[32,1024]{1,0:T(8,128)(2,1)S(1)}, bf16[32,1024]{1,0:T(8,128)(2,1)S(1)}, u32[]{:S(2)}, u32[]{:S(2)}) collective-permute-start(bf16[32,1024]{1,0:T(8,128)(2,1)S(1)} %get-tuple-element.20), channel_id=1, source_target_pairs={{0,0},{1,3},{2,2},{3,1},{4,4},{5,7},{6,6},{7,5},{8,8},{9,11},{10,1... | collective-permute-start | bytes 196616 | tf_op jit(solution)/shard_map/ppermute | solution.py:414
  45.4 4.0 %collective-permute-done.11 = bf16[32,1024]{1,0:T(8,128)(2,1)S(1)} collective-permute-done((bf16[32,1024]{1,0:T(8,128)(2,1)S(1)}, bf16[32,1024]{1,0:T(8,128)(2,1)S(1)}, u32[]{:S(2)}, u32[]{:S(2)}) %collective-permute-start.11) | collective-permute-done | bytes 65568 | tf_op jit(solution)/shard_map/ppermute | solution.py:414
  49.4 1.3 %collective-permute-done.13 = bf16[32,1024]{1,0:T(8,128)(2,1)S(1)} collective-permute-done((bf16[32,1024]{1,0:T(8,128)(2,1)S(1)}, bf16[32,1024]{1,0:T(8,128)(2,1)S(1)}, u32[]{:S(2)}, u32[]{:S(2)}) %collective-permute-start.13) | collective-permute-done | bytes 65568 | tf_op jit(solution)/shard_map/ppermute | solution.py:414
  51.1 1.0 %collective-permute-done.15 = bf16[32,512]{1,0:T(8,128)(2,1)S(1)} collective-permute-done((bf16[32,512]{1,0:T(8,128)(2,1)S(1)}, bf16[32,512]{1,0:T(8,128)(2,1)S(1)}, u32[]{:S(2)}, u32[]{:S(2)}) %collective-permute-start.15) | collective-permute-done | bytes 32800 | tf_op jit(solution)/shard_map/ppermute | solution.py:153
  52.1 0.6 %add_convert_fusion.3 = bf16[32,512]{1,0:T(8,128)(2,1)} fusion(bf16[32,512]{1,0:T(8,128)(2,1)S(1)} %collective-permute-done.15, bf16[32,512]{1,0:T(8,128)(2,1)S(1)} %get-tuple-element.14, f32[32,1024]{1,0:T(8,128)S(1)} %convert_add_fusion, pred[]{:T(512)S(6)} %eq.26), kind=kLoop, calls=%fused_computation.5 | loop fusion | flops 98304 | bytes 229377 | tf_op jit(solution)/shard_map/convert_element_type | solution.py:426
  (53 shorter events, 1.1 us)
Async XLA Ops:
  2.0 12.7 %collective-permute-start.2 = (bf16[32,1152]{1,0:T(8,128)(2,1)S(1)}, bf16[32,1152]{1,0:T(8,128)(2,1)S(1)}, u32[]{:S(2)}, u32[]{:S(2)}) collective-permute-start(bf16[32,1152]{1,0:T(8,128)(2,1)S(1)} %shard_map.118.own_ref), channel_id=1, source_target_pairs={{0,12},{4,8},{8,4},{12,0},{1,13},{5,9},{9,5},{13,1},{2,14},{6,10},... | collective-permute-start | bytes 221192 | tf_op jit(solution)/shard_map/ppermute | solution.py:153
  7.1 7.6 %collective-permute-start.1 = (bf16[32,1152]{1,0:T(8,128)(2,1)S(1)}, bf16[32,1152]{1,0:T(8,128)(2,1)S(1)}, u32[]{:S(2)}, u32[]{:S(2)}) collective-permute-start(bf16[32,1152]{1,0:T(8,128)(2,1)S(1)} %shard_map.118.own_ref), channel_id=1, source_target_pairs={{0,8},{4,12},{8,0},{12,4},{1,9},{5,13},{9,1},{13,5},{2,10},{6,14},... | collective-permute-start | bytes 221192 | tf_op jit(solution)/shard_map/ppermute | solution.py:153
  7.1 7.6 %collective-permute-start = (bf16[32,1152]{1,0:T(8,128)(2,1)S(1)}, bf16[32,1152]{1,0:T(8,128)(2,1)S(1)}, u32[]{:S(2)}, u32[]{:S(2)}) collective-permute-start(bf16[32,1152]{1,0:T(8,128)(2,1)S(1)} %shard_map.118.own_ref), channel_id=1, source_target_pairs={{0,4},{4,0},{8,12},{12,8},{1,5},{5,1},{9,13},{13,9},{2,6},{6,2},{1... | collective-permute-start | bytes 221192 | tf_op jit(solution)/shard_map/ppermute | solution.py:153
  7.8 7.0 %collective-permute-start.3 = (bf16[32,512]{1,0:T(8,128)(2,1)S(1)}, bf16[32,512]{1,0:T(8,128)(2,1)S(1)}, u32[]{:S(2)}, u32[]{:S(2)}) collective-permute-start(bf16[32,512]{1,0:T(8,128)(2,1)S(1)} %bitcast.31), channel_id=1, source_target_pairs={{0,2},{4,3},{8,0},{12,1},{5,6},{1,7},{9,4},{13,5},{10,8},{6,9},{14... | collective-permute-start | bytes 98312 | tf_op jit(solution)/shard_map/ppermute | solution.py:342
  9.4 22.0 %slice-start = ((s8[16777216]{0:T(1024)(128)(4,1)}), s8[4194304]{0:T(1024)(128)(4,1)S(1)}, s32[]{:S(2)}) async-start(s8[16777216]{0:T(1024)(128)(4,1)} %bitcast.16), calls=%async_computation | async-start | bytes 8388608
  9.4 22.0 %slice-start.4 = ((s8[16777216]{0:T(1024)(128)(4,1)}), s8[4194304]{0:T(1024)(128)(4,1)S(1)}, s32[]{:S(2)}) async-start(s8[16777216]{0:T(1024)(128)(4,1)} %bitcast.18), calls=%async_computation.4 | async-start | bytes 8388608
  9.4 22.0 %slice-start.8 = ((s8[16777216]{0:T(1024)(128)(4,1)}), s8[4194304]{0:T(1024)(128)(4,1)S(1)}, s32[]{:S(2)}) async-start(s8[16777216]{0:T(1024)(128)(4,1)} %bitcast.20), calls=%async_computation.8 | async-start | bytes 8388608
  9.5 22.0 %slice-start.3 = ((s8[16777216]{0:T(1024)(128)(4,1)}), s8[4194304]{0:T(1024)(128)(4,1)S(1)}, s32[]{:S(2)}) async-start(s8[16777216]{0:T(1024)(128)(4,1)} %bitcast.16), calls=%async_computation.3 | async-start | bytes 8388608
  9.5 22.0 %slice-start.5 = ((s8[16777216]{0:T(1024)(128)(4,1)}), s8[4194304]{0:T(1024)(128)(4,1)S(1)}, s32[]{:S(2)}) async-start(s8[16777216]{0:T(1024)(128)(4,1)} %bitcast.18), calls=%async_computation.5 | async-start | bytes 8388608
  9.5 22.0 %slice-start.6 = ((s8[16777216]{0:T(1024)(128)(4,1)}), s8[4194304]{0:T(1024)(128)(4,1)S(1)}, s32[]{:S(2)}) async-start(s8[16777216]{0:T(1024)(128)(4,1)} %bitcast.18), calls=%async_computation.6 | async-start | bytes 8388608
  9.5 22.0 %slice-start.7 = ((s8[16777216]{0:T(1024)(128)(4,1)}), s8[4194304]{0:T(1024)(128)(4,1)S(1)}, s32[]{:S(2)}) async-start(s8[16777216]{0:T(1024)(128)(4,1)} %bitcast.18), calls=%async_computation.7 | async-start | bytes 8388608
  9.5 22.0 %slice-start.9 = ((s8[16777216]{0:T(1024)(128)(4,1)}), s8[4194304]{0:T(1024)(128)(4,1)S(1)}, s32[]{:S(2)}) async-start(s8[16777216]{0:T(1024)(128)(4,1)} %bitcast.20), calls=%async_computation.9 | async-start | bytes 8388608
  15.7 1.3 %collective-permute-start.4 = (bf16[128,256]{1,0:T(8,128)(2,1)S(1)}, bf16[128,256]{1,0:T(8,128)(2,1)S(1)}, u32[]{:S(2)}, u32[]{:S(2)}) collective-permute-start(bf16[128,256]{1,0:T(8,128)(2,1)S(1)} %get-tuple-element.12), channel_id=1, source_target_pairs={{0,1},{1,0},{2,3},{3,2},{4,5},{5,4},{6,7},{7,6},{8,9},{9,8},{10,11... | collective-permute-start | bytes 196616 | tf_op jit(solution)/shard_map/ppermute | solution.py:153
  17.0 4.3 %collective-permute-start.5 = (bf16[128,256]{1,0:T(8,128)(2,1)S(1)}, bf16[128,256]{1,0:T(8,128)(2,1)S(1)}, u32[]{:S(2)}, u32[]{:S(2)}) collective-permute-start(bf16[128,256]{1,0:T(8,128)(2,1)S(1)} %add_convert_fusion.2), channel_id=1, source_target_pairs={{0,2},{1,3},{2,0},{3,1},{4,6},{5,7},{6,4},{7,5},{8,10},{9,11},{10,... | collective-permute-start | bytes 196616 | tf_op jit(solution)/shard_map/ppermute | solution.py:153
  21.4 6.9 %collective-permute-start.8 = (bf16[128,256]{1,0:T(8,128)(2,1)S(1)}, bf16[128,256]{1,0:T(8,128)(2,1)S(1)}, u32[]{:S(2)}, u32[]{:S(2)}) collective-permute-start(bf16[128,256]{1,0:T(8,128)(2,1)S(1)} %add_convert_fusion.1), channel_id=1, source_target_pairs={{0,12},{4,8},{8,4},{12,0},{1,13},{5,9},{9,5},{13,1},{2,14},{6,10},... | collective-permute-start | bytes 196616 | tf_op jit(solution)/shard_map/ppermute | solution.py:153
  23.4 6.4 %collective-permute-start.7 = (bf16[128,256]{1,0:T(8,128)(2,1)S(1)}, bf16[128,256]{1,0:T(8,128)(2,1)S(1)}, u32[]{:S(2)}, u32[]{:S(2)}) collective-permute-start(bf16[128,256]{1,0:T(8,128)(2,1)S(1)} %add_convert_fusion.1), channel_id=1, source_target_pairs={{0,8},{4,12},{8,0},{12,4},{1,9},{5,13},{9,1},{13,5},{2,10},{6,14},... | collective-permute-start | bytes 196616 | tf_op jit(solution)/shard_map/ppermute | solution.py:153
  23.8 6.0 %collective-permute-start.6 = (bf16[128,256]{1,0:T(8,128)(2,1)S(1)}, bf16[128,256]{1,0:T(8,128)(2,1)S(1)}, u32[]{:S(2)}, u32[]{:S(2)}) collective-permute-start(bf16[128,256]{1,0:T(8,128)(2,1)S(1)} %add_convert_fusion.1), channel_id=1, source_target_pairs={{0,4},{4,0},{8,12},{12,8},{1,5},{5,1},{9,13},{13,9},{2,6},{6,2},{1... | collective-permute-start | bytes 196616 | tf_op jit(solution)/shard_map/ppermute | solution.py:153
  29.8 1.6 %collective-permute-start.9 = (bf16[4,128,256]{2,1,0:T(8,128)(2,1)S(1)}, bf16[4,128,256]{2,1,0:T(8,128)(2,1)S(1)}, u32[]{:S(2)}, u32[]{:S(2)}) collective-permute-start(bf16[4,128,256]{2,1,0:T(8,128)(2,1)S(1)} %pad_maximum_fusion.mine_ref), channel_id=1, source_target_pairs={{0,1},{1,0},{2,3},{3,2},{4,5},{5,4},{6,7},{7,6},{8,9},{9,8},{10,11... | collective-permute-start | bytes 786440 | tf_op jit(solution)/shard_map/ppermute | solution.py:153
  39.5 1.6 %collective-permute-start.10 = (bf16[128,1024]{1,0:T(8,128)(2,1)S(1)}, bf16[128,1024]{1,0:T(8,128)(2,1)S(1)}, u32[]{:S(2)}, u32[]{:S(2)}) collective-permute-start(bf16[128,1024]{1,0:T(8,128)(2,1)S(1)} %get-tuple-element.16), channel_id=1, source_target_pairs={{0,1},{1,0},{2,3},{3,2},{4,5},{5,4},{6,7},{7,6},{8,9},{9,8},{10,11... | collective-permute-start | bytes 786440 | tf_op jit(solution)/shard_map/ppermute | solution.py:153
  41.2 8.3 %collective-permute-start.11 = (bf16[32,1024]{1,0:T(8,128)(2,1)S(1)}, bf16[32,1024]{1,0:T(8,128)(2,1)S(1)}, u32[]{:S(2)}, u32[]{:S(2)}) collective-permute-start(bf16[32,1024]{1,0:T(8,128)(2,1)S(1)} %get-tuple-element.17), channel_id=1, source_target_pairs={{0,8},{1,11},{2,10},{3,9},{4,12},{5,15},{6,14},{7,13},{8,0},{9,3},... | collective-permute-start | bytes 196616 | tf_op jit(solution)/shard_map/ppermute | solution.py:414
  42.2 7.2 %collective-permute-start.14 = (bf16[32,1024]{1,0:T(8,128)(2,1)S(1)}, bf16[32,1024]{1,0:T(8,128)(2,1)S(1)}, u32[]{:S(2)}, u32[]{:S(2)}) collective-permute-start(bf16[32,1024]{1,0:T(8,128)(2,1)S(1)} %get-tuple-element.18), channel_id=1, source_target_pairs={{0,12},{1,15},{2,14},{3,13},{4,8},{5,11},{6,10},{7,9},{8,4},{9,7},... | collective-permute-start | bytes 196616 | tf_op jit(solution)/shard_map/ppermute | solution.py:414
  43.9 6.8 %collective-permute-start.13 = (bf16[32,1024]{1,0:T(8,128)(2,1)S(1)}, bf16[32,1024]{1,0:T(8,128)(2,1)S(1)}, u32[]{:S(2)}, u32[]{:S(2)}) collective-permute-start(bf16[32,1024]{1,0:T(8,128)(2,1)S(1)} %get-tuple-element.19), channel_id=1, source_target_pairs={{0,4},{1,7},{2,6},{3,5},{4,0},{5,3},{6,2},{7,1},{8,12},{9,15},{10,... | collective-permute-start | bytes 196616 | tf_op jit(solution)/shard_map/ppermute | solution.py:414
  44.7 6.0 %collective-permute-start.12 = (bf16[32,1024]{1,0:T(8,128)(2,1)S(1)}, bf16[32,1024]{1,0:T(8,128)(2,1)S(1)}, u32[]{:S(2)}, u32[]{:S(2)}) collective-permute-start(bf16[32,1024]{1,0:T(8,128)(2,1)S(1)} %get-tuple-element.20), channel_id=1, source_target_pairs={{0,0},{1,3},{2,2},{3,1},{4,4},{5,7},{6,6},{7,5},{8,8},{9,11},{10,1... | collective-permute-start | bytes 196616 | tf_op jit(solution)/shard_map/ppermute | solution.py:414
  50.8 1.3 %collective-permute-start.15 = (bf16[32,512]{1,0:T(8,128)(2,1)S(1)}, bf16[32,512]{1,0:T(8,128)(2,1)S(1)}, u32[]{:S(2)}, u32[]{:S(2)}) collective-permute-start(bf16[32,512]{1,0:T(8,128)(2,1)S(1)} %select_convert_fusion), channel_id=1, source_target_pairs={{0,1},{1,0},{2,3},{3,2},{4,5},{5,4},{6,7},{7,6},{8,9},{9,8},{10,11... | collective-permute-start | bytes 98312 | tf_op jit(solution)/shard_map/ppermute | solution.py:153
  (7 other events, 116.5 us)

commit v9 on v8

--- a/solution.py
+++ b/solution.py
@@ -254,9 +254,18 @@
     )
 
 
+def down_columns(hid_ref, wd_ref, out_ref, place, block):
+    for k in range(2):
+        start = pl.multiple_of((2 * place + k) * block, block)
+        out = jnp.dot(
+            hid_ref[...], wd_ref[:, pl.ds(start, block)], preferred_element_type=jnp.float32
+        )
+        out_ref[:, k * block:(k + 1) * block] = out.astype(out_ref.dtype)
+
+
 def expert_kernel(where_ref, mine_ref, other_ref, mix_ref, gain_ref,
-                  wg_ref, wu_ref, wd_ref, keep_ref, send_ref, stream_ref,
-                  x_ref, hid_ref):
+                  wg_ref, wu_ref, wd_ref, hid_ref, send_ref, stream_ref,
+                  x_ref):
     wide, narrow = where_ref[0], where_ref[1]
     core = narrow & 1
     blocks, total, half = mine_ref.shape
@@ -291,14 +300,12 @@
         share = jnp.dot(mix, pick, preferred_element_type=jnp.float32)
         hidden = gate / (1.0 + jnp.exp(-gate)) * upper * share
         hid_ref[:, e * width:(e + 1) * width] = hidden.astype(jnp.bfloat16)
-    side = (narrow >> 1) ^ core
-    for target, place in ((send_ref, 1 - side), (keep_ref, side)):
-        for k in range(2):
-            start = pl.multiple_of((2 * place + k) * block, block)
-            out = jnp.dot(
-                hid_ref[...], wd_ref[:, pl.ds(start, block)], preferred_element_type=jnp.float32
-            )
-            target[:, k * block:(k + 1) * block] = out.astype(target.dtype)
+    down_columns(hid_ref, wd_ref, send_ref, 1 - ((narrow >> 1) ^ core), block)
+
+
+def keep_kernel(where_ref, hid_ref, wd_ref, keep_ref):
+    narrow = where_ref[1]
+    down_columns(hid_ref, wd_ref, keep_ref, (narrow >> 1) ^ (narrow & 1), keep_ref.shape[1] // 2)
 
 
 def residual_route(size):
@@ -387,10 +394,10 @@
         pltpu.with_memory_space_constraint(w, pltpu.VMEM)
         for w in (w_gate, w_up, w_down.reshape(experts * hidden, model))
     ]
-    keep, send, own = pl.pallas_call(
+    hid, send, own = pl.pallas_call(
         expert_kernel,
         out_shape=(
-            pltpu.VMEM((size * rows, model // 2), jnp.float32),
+            pltpu.VMEM((size * rows, experts * hidden), jnp.bfloat16),
             pltpu.VMEM((size * rows, model // 2), jnp.bfloat16),
             pltpu.VMEM((rows, columns), jnp.bfloat16),
         ),
@@ -398,7 +405,6 @@
         out_specs=(vmem, vmem, vmem),
         scratch_shapes=[
             pltpu.VMEM((size * rows, model), jnp.bfloat16),
-            pltpu.VMEM((size * rows, experts * hidden), jnp.bfloat16),
         ],
         compiler_params=pltpu.CompilerParams(vmem_limit_bytes=11 * 2**20),
     )(
@@ -407,6 +413,14 @@
         norm_gain.reshape(1, model),
         *weights,
     )
+    keep = pl.pallas_call(
+        keep_kernel,
+        out_shape=pltpu.VMEM((size * rows, model // 2), jnp.float32),
+        in_specs=[smem] + [vmem] * 2,
+        out_specs=vmem,
+        cost_estimate=pl.CostEstimate(flops=2 * 10**9, bytes_accessed=10**6, transcendentals=0),
+        compiler_params=pltpu.CompilerParams(vmem_limit_bytes=4 * 2**20),
+    )(where, pltpu.with_memory_space_constraint(hid, pltpu.VMEM), weights[2])
     total = (keep + flip_permute(send, "narrow", 1).astype(jnp.float32)).astype(jnp.bfloat16)
     total = total.reshape(size, rows, model // 2)
     devices = range(size * size)

time: 52.9 us -> 52.6 us (level)
  waiting for transfers between devices: 23.9 us -> 22.6 us
  Pallas kernels: 10.8 us -> 11.6 us
    ppermute x11, waiting for transfers between devices: 13.4 us -> 11.9 us  [flip_permute(): return lax.ppermute(value, axis, [(i, i ^ mask) for i in range(size)])]
    pallas_call x1 -> x2, Pallas kernels: 7.94 us -> 8.75 us  [the longest x1 6.94 us: local_small(): pl.pallas_call(expert_kernel, out_shape=(pltpu.VMEM((size * rows, experts...]
  transfers between devices with their start and end apart: 16 -> 16, of which waited for: 10 -> 9; matrix products, arithmetic and copies ran while one was open for 0% -> 0% of each run, Pallas kernels for 0% -> 3%
where the time goes in v9:
time: 52.6 us; the launch traced here: 52.4 us
  waiting for transfers between devices  22.6 us (43%)
  starting transfers between devices  16.9 us (32%)
  Pallas kernels  11.6 us (22%)
  other arithmetic  0.88 us (2%)
    ppermute x11, waiting for transfers between devices, flip_permute(): return lax.ppermute(value, axis, [(i, i ^ mask) for i in range(size)])  11.9 us
    ppermute x11, starting transfers between devices, flip_permute(): return lax.ppermute(value, axis, [(i, i ^ mask) for i in range(size)])  11 us
    pallas_call x1, Pallas kernels, local_small(): pl.pallas_call(expert_kernel, out_shape=(pltpu.VMEM((size * rows, experts...  6.94 us
    ppermute x4, waiting for transfers between devices, local_small(): lax.ppermute(total[s], ('wide', 'narrow'), [(i, i ^ s * size ^ (2 if i &...  5.57 us
    ppermute x1, waiting for transfers between devices, local_small(): lax.ppermute(residual.reshape(rows, columns), ('wide', 'narrow'), [(w * s...  5.18 us
    ppermute x4, starting transfers between devices, local_small(): lax.ppermute(total[s], ('wide', 'narrow'), [(i, i ^ s * size ^ (2 if i &...  4.21 us
    pallas_call x1, Pallas kernels, local_small(): pl.pallas_call(attend_kernel, out_shape=jax.ShapeDtypeStruct((rows, depth...  2 us
    pallas_call x1, Pallas kernels, local_small(): pl.pallas_call(keep_kernel, out_shape=pltpu.VMEM((size * rows, model // 2...  1.82 us
  transfers between devices with their start and end apart: 16, of which 9 were waited for; matrix products, arithmetic and copies ran while one was open for 0% of the time, Pallas kernels for 3%

profile of v9, /device:TPU:0, one launch (start us, length us, event | category | flops | bytes accessed | tf_op | source)
XLA Modules:
  0.0 52.4 jit_solution(13555197453674588585)
XLA Ops:
  0.0 2.0 %shard_map.118.own_ref = bf16[32,1152]{1,0:T(8,128)(2,1)S(1)} custom-call(s32[2,16]{1,0:T(2,128)} %refs_0_.1, bf16[256,128]{1,0:T(8,128)(2,1)} %bitcast.31, bf16[2048,128]{1,0:T(8,128)(2,1)} %bitcast.29, bf16[2048,128]{1,0:T(8,128)(2,1)} %bitcast.30, s32[2,8,16]{2,1,0:T(8,128)} %bitcast.33, f32[2,8,16]{2,1,0:T(8,128)} %bitcast.34), custom_call_target="tpu_custom_call" | custom-call | flops 20000000000 | bytes 1000000 | tf_op jit(solution)/shard_map/pallas_call | solution.py:362
  2.0 5.1 %collective-permute-start.2 = (bf16[32,1152]{1,0:T(8,128)(2,1)S(1)}, bf16[32,1152]{1,0:T(8,128)(2,1)S(1)}, u32[]{:S(2)}, u32[]{:S(2)}) collective-permute-start(bf16[32,1152]{1,0:T(8,128)(2,1)S(1)} %shard_map.118.own_ref), channel_id=1, source_target_pairs={{0,12},{4,8},{8,4},{12,0},{1,13},{5,9},{9,5},{13,1},{2,14},{6,10},... | collective-permute-start | bytes 221192 | tf_op jit(solution)/shard_map/ppermute | solution.py:153
  7.1 0.6 %collective-permute-start = (bf16[32,1152]{1,0:T(8,128)(2,1)S(1)}, bf16[32,1152]{1,0:T(8,128)(2,1)S(1)}, u32[]{:S(2)}, u32[]{:S(2)}) collective-permute-start(bf16[32,1152]{1,0:T(8,128)(2,1)S(1)} %shard_map.118.own_ref), channel_id=1, source_target_pairs={{0,4},{4,0},{8,12},{12,8},{1,5},{5,1},{9,13},{13,9},{2,6},{6,2},{1... | collective-permute-start | bytes 221192 | tf_op jit(solution)/shard_map/ppermute | solution.py:153
  7.8 1.6 %collective-permute-start.3 = (bf16[32,512]{1,0:T(8,128)(2,1)S(1)}, bf16[32,512]{1,0:T(8,128)(2,1)S(1)}, u32[]{:S(2)}, u32[]{:S(2)}) collective-permute-start(bf16[32,512]{1,0:T(8,128)(2,1)S(1)} %bitcast.32), channel_id=1, source_target_pairs={{0,2},{4,3},{8,0},{12,1},{5,6},{1,7},{9,4},{13,5},{10,8},{6,9},{14... | collective-permute-start | bytes 98312 | tf_op jit(solution)/shard_map/ppermute | solution.py:349
  9.6 5.2 %collective-permute-done.3.res_ref = bf16[32,512]{1,0:T(8,128)(2,1)S(1)} collective-permute-done((bf16[32,512]{1,0:T(8,128)(2,1)S(1)}, bf16[32,512]{1,0:T(8,128)(2,1)S(1)}, u32[]{:S(2)}, u32[]{:S(2)}) %collective-permute-start.3) | collective-permute-done | bytes 32800 | tf_op jit(solution)/shard_map/ppermute | solution.py:349
  14.8 0.9 %shard_map.119 = (f32[128,256]{1,0:T(8,128)S(1)}, bf16[128,256]{1,0:T(8,128)(2,1)S(1)}, bf16[128,128]{1,0:T(8,128)(2,1)S(1)}) custom-call(s32[3]{0:T(128)S(1)} %pad_add_fusion.where_ref, bf16[32,1152]{1,0:T(8,128)(2,1)S(1)} %shard_map.118.own_ref, bf16[32,1152]{1,0:T(8,128)(2,1)S(1)} %collective-permute-done.got1_ref, ...), custom_call_target="tpu_custom_call" | custom-call | flops 30000001024 | bytes 1000000 | tf_op jit(solution)/shard_map/pallas_call | solution.py:375
  15.7 1.2 %collective-permute-done.4 = bf16[128,256]{1,0:T(8,128)(2,1)S(1)} collective-permute-done((bf16[128,256]{1,0:T(8,128)(2,1)S(1)}, bf16[128,256]{1,0:T(8,128)(2,1)S(1)}, u32[]{:S(2)}, u32[]{:S(2)}) %collective-permute-start.4) | collective-permute-done | bytes 65568 | tf_op jit(solution)/shard_map/ppermute | solution.py:153
  17.1 4.2 %collective-permute-done.5 = bf16[128,256]{1,0:T(8,128)(2,1)S(1)} collective-permute-done((bf16[128,256]{1,0:T(8,128)(2,1)S(1)}, bf16[128,256]{1,0:T(8,128)(2,1)S(1)}, u32[]{:S(2)}, u32[]{:S(2)}) %collective-permute-start.5) | collective-permute-done | bytes 65568 | tf_op jit(solution)/shard_map/ppermute | solution.py:153
  21.4 2.1 %collective-permute-start.8 = (bf16[128,256]{1,0:T(8,128)(2,1)S(1)}, bf16[128,256]{1,0:T(8,128)(2,1)S(1)}, u32[]{:S(2)}, u32[]{:S(2)}) collective-permute-start(bf16[128,256]{1,0:T(8,128)(2,1)S(1)} %add_convert_fusion.1), channel_id=1, source_target_pairs={{0,12},{4,8},{8,4},{12,0},{1,13},{5,9},{9,5},{13,1},{2,14},{6,10},... | collective-permute-start | bytes 196616 | tf_op jit(solution)/shard_map/ppermute | solution.py:153
  23.4 0.4 collective-permute-start.7
  23.8 2.0 %collective-permute-start.6 = (bf16[128,256]{1,0:T(8,128)(2,1)S(1)}, bf16[128,256]{1,0:T(8,128)(2,1)S(1)}, u32[]{:S(2)}, u32[]{:S(2)}) collective-permute-start(bf16[128,256]{1,0:T(8,128)(2,1)S(1)} %add_convert_fusion.1), channel_id=1, source_target_pairs={{0,4},{4,0},{8,12},{12,8},{1,5},{5,1},{9,13},{13,9},{2,6},{6,2},{1... | collective-permute-start | bytes 196616 | tf_op jit(solution)/shard_map/ppermute | solution.py:153
  25.8 2.5 %collective-permute-done.8 = bf16[128,256]{1,0:T(8,128)(2,1)S(1)} collective-permute-done((bf16[128,256]{1,0:T(8,128)(2,1)S(1)}, bf16[128,256]{1,0:T(8,128)(2,1)S(1)}, u32[]{:S(2)}, u32[]{:S(2)}) %collective-permute-start.8) | collective-permute-done | bytes 65568 | tf_op jit(solution)/shard_map/ppermute | solution.py:153
  28.3 1.5 %collective-permute-done.7 = bf16[128,256]{1,0:T(8,128)(2,1)S(1)} collective-permute-done((bf16[128,256]{1,0:T(8,128)(2,1)S(1)}, bf16[128,256]{1,0:T(8,128)(2,1)S(1)}, u32[]{:S(2)}, u32[]{:S(2)}) %collective-permute-start.7) | collective-permute-done | bytes 65568 | tf_op jit(solution)/shard_map/ppermute | solution.py:153
  29.9 1.5 %collective-permute-done.9.other_ref = bf16[4,128,256]{2,1,0:T(8,128)(2,1)S(1)} collective-permute-done((bf16[4,128,256]{2,1,0:T(8,128)(2,1)S(1)}, bf16[4,128,256]{2,1,0:T(8,128)(2,1)S(1)}, u32[]{:S(2)}, u32[]{:S(2)}) %collective-permute-start.9) | collective-permute-done | bytes 262176 | tf_op jit(solution)/shard_map/ppermute | solution.py:153
  31.6 6.9 %shard_map.120 = (bf16[128,4096]{1,0:T(8,128)(2,1)S(1)}, bf16[128,1024]{1,0:T(8,128)(2,1)S(1)}, bf16[32,512]{1,0:T(8,128)(2,1)S(1)}) custom-call(s32[3]{0:T(128)} %copy-done, bf16[4,128,256]{2,1,0:T(8,128)(2,1)S(1)} %pad_maximum_fusion.mine_ref, bf16[4,128,256]{2,1,0:T(8,128)(2,1)S(1)} %collective-permute-done.9.other_ref, ...), custom_call_target="tpu_custom_call" | custom-call | tf_op jit(solution)/shard_map/pallas_call | solution.py:397
  38.7 1.8 %shard_map.121 = f32[128,1024]{1,0:T(8,128)S(1)} custom-call(s32[3]{0:T(128)S(1)} %copy-done.1, bf16[128,4096]{1,0:T(8,128)(2,1)S(1)} %get-tuple-element.15.hid_ref, bf16[4096,2048]{1,0:T(8,128)(2,1)S(1)} %bitcast.19), custom_call_target="tpu_custom_call" | custom-call | flops 2000000000 | bytes 1000000 | tf_op jit(solution)/shard_map/pallas_call | solution.py:416
  40.6 1.1 %collective-permute-start.11 = (bf16[32,1024]{1,0:T(8,128)(2,1)S(1)}, bf16[32,1024]{1,0:T(8,128)(2,1)S(1)}, u32[]{:S(2)}, u32[]{:S(2)}) collective-permute-start(bf16[32,1024]{1,0:T(8,128)(2,1)S(1)} %get-tuple-element.17), channel_id=1, source_target_pairs={{0,8},{1,11},{2,10},{3,9},{4,12},{5,15},{6,14},{7,13},{8,0},{9,3},... | collective-permute-start | bytes 196616 | tf_op jit(solution)/shard_map/ppermute | solution.py:428
  41.7 1.7 %collective-permute-start.14 = (bf16[32,1024]{1,0:T(8,128)(2,1)S(1)}, bf16[32,1024]{1,0:T(8,128)(2,1)S(1)}, u32[]{:S(2)}, u32[]{:S(2)}) collective-permute-start(bf16[32,1024]{1,0:T(8,128)(2,1)S(1)} %get-tuple-element.18), channel_id=1, source_target_pairs={{0,12},{1,15},{2,14},{3,13},{4,8},{5,11},{6,10},{7,9},{8,4},{9,7},... | collective-permute-start | bytes 196616 | tf_op jit(solution)/shard_map/ppermute | solution.py:428
  43.4 0.8 %collective-permute-start.13 = (bf16[32,1024]{1,0:T(8,128)(2,1)S(1)}, bf16[32,1024]{1,0:T(8,128)(2,1)S(1)}, u32[]{:S(2)}, u32[]{:S(2)}) collective-permute-start(bf16[32,1024]{1,0:T(8,128)(2,1)S(1)} %get-tuple-element.19), channel_id=1, source_target_pairs={{0,4},{1,7},{2,6},{3,5},{4,0},{5,3},{6,2},{7,1},{8,12},{9,15},{10,... | collective-permute-start | bytes 196616 | tf_op jit(solution)/shard_map/ppermute | solution.py:428
  44.2 0.7 %collective-permute-start.12 = (bf16[32,1024]{1,0:T(8,128)(2,1)S(1)}, bf16[32,1024]{1,0:T(8,128)(2,1)S(1)}, u32[]{:S(2)}, u32[]{:S(2)}) collective-permute-start(bf16[32,1024]{1,0:T(8,128)(2,1)S(1)} %get-tuple-element.20), channel_id=1, source_target_pairs={{0,0},{1,3},{2,2},{3,1},{4,4},{5,7},{6,6},{7,5},{8,8},{9,11},{10,1... | collective-permute-start | bytes 196616 | tf_op jit(solution)/shard_map/ppermute | solution.py:428
  44.9 4.3 %collective-permute-done.11 = bf16[32,1024]{1,0:T(8,128)(2,1)S(1)} collective-permute-done((bf16[32,1024]{1,0:T(8,128)(2,1)S(1)}, bf16[32,1024]{1,0:T(8,128)(2,1)S(1)}, u32[]{:S(2)}, u32[]{:S(2)}) %collective-permute-start.11) | collective-permute-done | bytes 65568 | tf_op jit(solution)/shard_map/ppermute | solution.py:428
  49.1 1.3 %collective-permute-done.13 = bf16[32,1024]{1,0:T(8,128)(2,1)S(1)} collective-permute-done((bf16[32,1024]{1,0:T(8,128)(2,1)S(1)}, bf16[32,1024]{1,0:T(8,128)(2,1)S(1)}, u32[]{:S(2)}, u32[]{:S(2)}) %collective-permute-start.13) | collective-permute-done | bytes 65568 | tf_op jit(solution)/shard_map/ppermute | solution.py:428
  50.8 0.9 %collective-permute-done.15 = bf16[32,512]{1,0:T(8,128)(2,1)S(1)} collective-permute-done((bf16[32,512]{1,0:T(8,128)(2,1)S(1)}, bf16[32,512]{1,0:T(8,128)(2,1)S(1)}, u32[]{:S(2)}, u32[]{:S(2)}) %collective-permute-start.15) | collective-permute-done | bytes 32800 | tf_op jit(solution)/shard_map/ppermute | solution.py:153
  51.7 0.6 %add_convert_fusion.3 = bf16[32,512]{1,0:T(8,128)(2,1)} fusion(bf16[32,512]{1,0:T(8,128)(2,1)S(1)} %collective-permute-done.15, bf16[32,512]{1,0:T(8,128)(2,1)S(1)} %get-tuple-element.14, f32[32,1024]{1,0:T(8,128)S(1)} %convert_add_fusion, pred[]{:T(512)S(6)} %eq.26), kind=kLoop, calls=%fused_computation.5 | loop fusion | flops 98304 | bytes 229377 | tf_op jit(solution)/shard_map/convert_element_type | solution.py:440
  (56 shorter events, 1.2 us)
Async XLA Ops:
  2.0 12.7 %collective-permute-start.2 = (bf16[32,1152]{1,0:T(8,128)(2,1)S(1)}, bf16[32,1152]{1,0:T(8,128)(2,1)S(1)}, u32[]{:S(2)}, u32[]{:S(2)}) collective-permute-start(bf16[32,1152]{1,0:T(8,128)(2,1)S(1)} %shard_map.118.own_ref), channel_id=1, source_target_pairs={{0,12},{4,8},{8,4},{12,0},{1,13},{5,9},{9,5},{13,1},{2,14},{6,10},... | collective-permute-start | bytes 221192 | tf_op jit(solution)/shard_map/ppermute | solution.py:153
  7.1 7.6 %collective-permute-start.1 = (bf16[32,1152]{1,0:T(8,128)(2,1)S(1)}, bf16[32,1152]{1,0:T(8,128)(2,1)S(1)}, u32[]{:S(2)}, u32[]{:S(2)}) collective-permute-start(bf16[32,1152]{1,0:T(8,128)(2,1)S(1)} %shard_map.118.own_ref), channel_id=1, source_target_pairs={{0,8},{4,12},{8,0},{12,4},{1,9},{5,13},{9,1},{13,5},{2,10},{6,14},... | collective-permute-start | bytes 221192 | tf_op jit(solution)/shard_map/ppermute | solution.py:153
  7.1 7.6 %collective-permute-start = (bf16[32,1152]{1,0:T(8,128)(2,1)S(1)}, bf16[32,1152]{1,0:T(8,128)(2,1)S(1)}, u32[]{:S(2)}, u32[]{:S(2)}) collective-permute-start(bf16[32,1152]{1,0:T(8,128)(2,1)S(1)} %shard_map.118.own_ref), channel_id=1, source_target_pairs={{0,4},{4,0},{8,12},{12,8},{1,5},{5,1},{9,13},{13,9},{2,6},{6,2},{1... | collective-permute-start | bytes 221192 | tf_op jit(solution)/shard_map/ppermute | solution.py:153
  7.8 7.0 %collective-permute-start.3 = (bf16[32,512]{1,0:T(8,128)(2,1)S(1)}, bf16[32,512]{1,0:T(8,128)(2,1)S(1)}, u32[]{:S(2)}, u32[]{:S(2)}) collective-permute-start(bf16[32,512]{1,0:T(8,128)(2,1)S(1)} %bitcast.32), channel_id=1, source_target_pairs={{0,2},{4,3},{8,0},{12,1},{5,6},{1,7},{9,4},{13,5},{10,8},{6,9},{14... | collective-permute-start | bytes 98312 | tf_op jit(solution)/shard_map/ppermute | solution.py:349
  9.4 22.0 %slice-start = ((s8[16777216]{0:T(1024)(128)(4,1)}), s8[4194304]{0:T(1024)(128)(4,1)S(1)}, s32[]{:S(2)}) async-start(s8[16777216]{0:T(1024)(128)(4,1)} %bitcast.16), calls=%async_computation | async-start | bytes 8388608
  9.4 22.0 %slice-start.4 = ((s8[16777216]{0:T(1024)(128)(4,1)}), s8[4194304]{0:T(1024)(128)(4,1)S(1)}, s32[]{:S(2)}) async-start(s8[16777216]{0:T(1024)(128)(4,1)} %bitcast.20), calls=%async_computation.4 | async-start | bytes 8388608
  9.4 22.0 %slice-start.8 = ((s8[16777216]{0:T(1024)(128)(4,1)}), s8[4194304]{0:T(1024)(128)(4,1)S(1)}, s32[]{:S(2)}) async-start(s8[16777216]{0:T(1024)(128)(4,1)} %bitcast.22), calls=%async_computation.8 | async-start | bytes 8388608
  9.5 22.0 %slice-start.3 = ((s8[16777216]{0:T(1024)(128)(4,1)}), s8[4194304]{0:T(1024)(128)(4,1)S(1)}, s32[]{:S(2)}) async-start(s8[16777216]{0:T(1024)(128)(4,1)} %bitcast.16), calls=%async_computation.3 | async-start | bytes 8388608
  9.5 22.0 %slice-start.5 = ((s8[16777216]{0:T(1024)(128)(4,1)}), s8[4194304]{0:T(1024)(128)(4,1)S(1)}, s32[]{:S(2)}) async-start(s8[16777216]{0:T(1024)(128)(4,1)} %bitcast.20), calls=%async_computation.5 | async-start | bytes 8388608
  9.5 22.0 %slice-start.6 = ((s8[16777216]{0:T(1024)(128)(4,1)}), s8[4194304]{0:T(1024)(128)(4,1)S(1)}, s32[]{:S(2)}) async-start(s8[16777216]{0:T(1024)(128)(4,1)} %bitcast.20), calls=%async_computation.6 | async-start | bytes 8388608
  9.5 22.0 %slice-start.7 = ((s8[16777216]{0:T(1024)(128)(4,1)}), s8[4194304]{0:T(1024)(128)(4,1)S(1)}, s32[]{:S(2)}) async-start(s8[16777216]{0:T(1024)(128)(4,1)} %bitcast.20), calls=%async_computation.7 | async-start | bytes 8388608
  9.5 22.0 %slice-start.9 = ((s8[16777216]{0:T(1024)(128)(4,1)}), s8[4194304]{0:T(1024)(128)(4,1)S(1)}, s32[]{:S(2)}) async-start(s8[16777216]{0:T(1024)(128)(4,1)} %bitcast.22), calls=%async_computation.9 | async-start | bytes 8388608
  15.7 1.3 %collective-permute-start.4 = (bf16[128,256]{1,0:T(8,128)(2,1)S(1)}, bf16[128,256]{1,0:T(8,128)(2,1)S(1)}, u32[]{:S(2)}, u32[]{:S(2)}) collective-permute-start(bf16[128,256]{1,0:T(8,128)(2,1)S(1)} %get-tuple-element.12), channel_id=1, source_target_pairs={{0,1},{1,0},{2,3},{3,2},{4,5},{5,4},{6,7},{7,6},{8,9},{9,8},{10,11... | collective-permute-start | bytes 196616 | tf_op jit(solution)/shard_map/ppermute | solution.py:153
  17.0 4.3 %collective-permute-start.5 = (bf16[128,256]{1,0:T(8,128)(2,1)S(1)}, bf16[128,256]{1,0:T(8,128)(2,1)S(1)}, u32[]{:S(2)}, u32[]{:S(2)}) collective-permute-start(bf16[128,256]{1,0:T(8,128)(2,1)S(1)} %add_convert_fusion.2), channel_id=1, source_target_pairs={{0,2},{1,3},{2,0},{3,1},{4,6},{5,7},{6,4},{7,5},{8,10},{9,11},{10,... | collective-permute-start | bytes 196616 | tf_op jit(solution)/shard_map/ppermute | solution.py:153
  21.4 6.9 %collective-permute-start.8 = (bf16[128,256]{1,0:T(8,128)(2,1)S(1)}, bf16[128,256]{1,0:T(8,128)(2,1)S(1)}, u32[]{:S(2)}, u32[]{:S(2)}) collective-permute-start(bf16[128,256]{1,0:T(8,128)(2,1)S(1)} %add_convert_fusion.1), channel_id=1, source_target_pairs={{0,12},{4,8},{8,4},{12,0},{1,13},{5,9},{9,5},{13,1},{2,14},{6,10},... | collective-permute-start | bytes 196616 | tf_op jit(solution)/shard_map/ppermute | solution.py:153
  23.4 6.4 %collective-permute-start.7 = (bf16[128,256]{1,0:T(8,128)(2,1)S(1)}, bf16[128,256]{1,0:T(8,128)(2,1)S(1)}, u32[]{:S(2)}, u32[]{:S(2)}) collective-permute-start(bf16[128,256]{1,0:T(8,128)(2,1)S(1)} %add_convert_fusion.1), channel_id=1, source_target_pairs={{0,8},{4,12},{8,0},{12,4},{1,9},{5,13},{9,1},{13,5},{2,10},{6,14},... | collective-permute-start | bytes 196616 | tf_op jit(solution)/shard_map/ppermute | solution.py:153
  23.8 6.0 %collective-permute-start.6 = (bf16[128,256]{1,0:T(8,128)(2,1)S(1)}, bf16[128,256]{1,0:T(8,128)(2,1)S(1)}, u32[]{:S(2)}, u32[]{:S(2)}) collective-permute-start(bf16[128,256]{1,0:T(8,128)(2,1)S(1)} %add_convert_fusion.1), channel_id=1, source_target_pairs={{0,4},{4,0},{8,12},{12,8},{1,5},{5,1},{9,13},{13,9},{2,6},{6,2},{1... | collective-permute-start | bytes 196616 | tf_op jit(solution)/shard_map/ppermute | solution.py:153
  29.8 1.6 %collective-permute-start.9 = (bf16[4,128,256]{2,1,0:T(8,128)(2,1)S(1)}, bf16[4,128,256]{2,1,0:T(8,128)(2,1)S(1)}, u32[]{:S(2)}, u32[]{:S(2)}) collective-permute-start(bf16[4,128,256]{2,1,0:T(8,128)(2,1)S(1)} %pad_maximum_fusion.mine_ref), channel_id=1, source_target_pairs={{0,1},{1,0},{2,3},{3,2},{4,5},{5,4},{6,7},{7,6},{8,9},{9,8},{10,11... | collective-permute-start | bytes 786440 | tf_op jit(solution)/shard_map/ppermute | solution.py:153
  38.5 2.0 %collective-permute-start.10 = (bf16[128,1024]{1,0:T(8,128)(2,1)S(1)}, bf16[128,1024]{1,0:T(8,128)(2,1)S(1)}, u32[]{:S(2)}, u32[]{:S(2)}) collective-permute-start(bf16[128,1024]{1,0:T(8,128)(2,1)S(1)} %get-tuple-element.16), channel_id=1, source_target_pairs={{0,1},{1,0},{2,3},{3,2},{4,5},{5,4},{6,7},{7,6},{8,9},{9,8},{10,11... | collective-permute-start | bytes 786440 | tf_op jit(solution)/shard_map/ppermute | solution.py:153
  40.6 8.5 %collective-permute-start.11 = (bf16[32,1024]{1,0:T(8,128)(2,1)S(1)}, bf16[32,1024]{1,0:T(8,128)(2,1)S(1)}, u32[]{:S(2)}, u32[]{:S(2)}) collective-permute-start(bf16[32,1024]{1,0:T(8,128)(2,1)S(1)} %get-tuple-element.17), channel_id=1, source_target_pairs={{0,8},{1,11},{2,10},{3,9},{4,12},{5,15},{6,14},{7,13},{8,0},{9,3},... | collective-permute-start | bytes 196616 | tf_op jit(solution)/shard_map/ppermute | solution.py:428
  41.7 7.4 %collective-permute-start.14 = (bf16[32,1024]{1,0:T(8,128)(2,1)S(1)}, bf16[32,1024]{1,0:T(8,128)(2,1)S(1)}, u32[]{:S(2)}, u32[]{:S(2)}) collective-permute-start(bf16[32,1024]{1,0:T(8,128)(2,1)S(1)} %get-tuple-element.18), channel_id=1, source_target_pairs={{0,12},{1,15},{2,14},{3,13},{4,8},{5,11},{6,10},{7,9},{8,4},{9,7},... | collective-permute-start | bytes 196616 | tf_op jit(solution)/shard_map/ppermute | solution.py:428
  43.4 7.0 %collective-permute-start.13 = (bf16[32,1024]{1,0:T(8,128)(2,1)S(1)}, bf16[32,1024]{1,0:T(8,128)(2,1)S(1)}, u32[]{:S(2)}, u32[]{:S(2)}) collective-permute-start(bf16[32,1024]{1,0:T(8,128)(2,1)S(1)} %get-tuple-element.19), channel_id=1, source_target_pairs={{0,4},{1,7},{2,6},{3,5},{4,0},{5,3},{6,2},{7,1},{8,12},{9,15},{10,... | collective-permute-start | bytes 196616 | tf_op jit(solution)/shard_map/ppermute | solution.py:428
  44.2 6.2 %collective-permute-start.12 = (bf16[32,1024]{1,0:T(8,128)(2,1)S(1)}, bf16[32,1024]{1,0:T(8,128)(2,1)S(1)}, u32[]{:S(2)}, u32[]{:S(2)}) collective-permute-start(bf16[32,1024]{1,0:T(8,128)(2,1)S(1)} %get-tuple-element.20), channel_id=1, source_target_pairs={{0,0},{1,3},{2,2},{3,1},{4,4},{5,7},{6,6},{7,5},{8,8},{9,11},{10,1... | collective-permute-start | bytes 196616 | tf_op jit(solution)/shard_map/ppermute | solution.py:428
  50.5 1.3 %collective-permute-start.15 = (bf16[32,512]{1,0:T(8,128)(2,1)S(1)}, bf16[32,512]{1,0:T(8,128)(2,1)S(1)}, u32[]{:S(2)}, u32[]{:S(2)}) collective-permute-start(bf16[32,512]{1,0:T(8,128)(2,1)S(1)} %select_convert_fusion), channel_id=1, source_target_pairs={{0,1},{1,0},{2,3},{3,2},{4,5},{5,4},{6,7},{7,6},{8,9},{9,8},{10,11... | collective-permute-start | bytes 98312 | tf_op jit(solution)/shard_map/ppermute | solution.py:153
  (8 other events, 123.6 us)

commit v10 on v9

--- a/solution.py
+++ b/solution.py
@@ -388,8 +388,10 @@
     stream = (
         part.astype(jnp.float32) + flip_permute(part, "narrow", 2).astype(jnp.float32)
     ).astype(jnp.bfloat16)
-    mine = jnp.stack([stream] + spread(stream))
-    other = flip_permute(mine, "narrow", 1)
+    got = jnp.stack(spread(stream))
+    twin = flip_permute(stream, "narrow", 1)
+    mine = jnp.concatenate([stream[None], got])
+    other = jnp.concatenate([twin[None], flip_permute(got, "narrow", 1)])
     weights = [
         pltpu.with_memory_space_constraint(w, pltpu.VMEM)
         for w in (w_gate, w_up, w_down.reshape(experts * hidden, model))
@@ -406,7 +408,7 @@
         scratch_shapes=[
             pltpu.VMEM((size * rows, model), jnp.bfloat16),
         ],
-        compiler_params=pltpu.CompilerParams(vmem_limit_bytes=11 * 2**20),
+        compiler_params=pltpu.CompilerParams(vmem_limit_bytes=12 * 2**20),
     )(
         where,
         *[pltpu.with_memory_space_constraint(p, pltpu.VMEM) for p in (mine, other, mix)],

time: 52.6 us -> 52.6 us (level)
  waiting for transfers between devices: 22.6 us -> 22 us
    ppermute x11 -> x12, starting transfers between devices: 11 us -> 11.6 us  [flip_permute(): return lax.ppermute(value, axis, [(i, i ^ mask) for i in range(size)])]
    ppermute x11 -> x12, waiting for transfers between devices: 11.9 us -> 11.4 us  [flip_permute(): return lax.ppermute(value, axis, [(i, i ^ mask) for i in range(size)])]
  transfers between devices with their start and end apart: 16 -> 17, of which waited for: 9 -> 9; matrix products, arithmetic and copies ran while one was open for 0% -> 0% of each run, Pallas kernels for 3% -> 3%
where the time goes in v10:
time: 52.6 us; the launch traced here: 52.4 us
  waiting for transfers between devices  22 us (42%)
  starting transfers between devices  17.4 us (33%)
  Pallas kernels  11.6 us (22%)
  other arithmetic  0.93 us (2%)
    ppermute x12, starting transfers between devices, flip_permute(): return lax.ppermute(value, axis, [(i, i ^ mask) for i in range(size)])  11.6 us
    ppermute x12, waiting for transfers between devices, flip_permute(): return lax.ppermute(value, axis, [(i, i ^ mask) for i in range(size)])  11.4 us
    pallas_call x1, Pallas kernels, local_small(): pl.pallas_call(expert_kernel, out_shape=(pltpu.VMEM((size * rows, experts...  6.95 us
    ppermute x4, waiting for transfers between devices, local_small(): lax.ppermute(total[s], ('wide', 'narrow'), [(i, i ^ s * size ^ (2 if i &...  5.47 us
    ppermute x1, waiting for transfers between devices, local_small(): lax.ppermute(residual.reshape(rows, columns), ('wide', 'narrow'), [(w * s...  5.18 us
    ppermute x4, starting transfers between devices, local_small(): lax.ppermute(total[s], ('wide', 'narrow'), [(i, i ^ s * size ^ (2 if i &...  4.21 us
    pallas_call x1, Pallas kernels, local_small(): pl.pallas_call(attend_kernel, out_shape=jax.ShapeDtypeStruct((rows, depth...  2 us
    pallas_call x1, Pallas kernels, local_small(): pl.pallas_call(keep_kernel, out_shape=pltpu.VMEM((size * rows, model // 2...  1.82 us
  transfers between devices with their start and end apart: 17, of which 9 were waited for; matrix products, arithmetic and copies ran while one was open for 0% of the time, Pallas kernels for 3%

profile of v10, /device:TPU:0, one launch (start us, length us, event | category | flops | bytes accessed | tf_op | source)
XLA Modules:
  0.0 52.4 jit_solution(2291579939940447820)
XLA Ops:
  0.0 2.0 %shard_map.118.own_ref = bf16[32,1152]{1,0:T(8,128)(2,1)S(1)} custom-call(s32[2,16]{1,0:T(2,128)} %refs_0_.1, bf16[256,128]{1,0:T(8,128)(2,1)} %bitcast.36, bf16[2048,128]{1,0:T(8,128)(2,1)} %bitcast.34, bf16[2048,128]{1,0:T(8,128)(2,1)} %bitcast.35, s32[2,8,16]{2,1,0:T(8,128)} %bitcast.38, f32[2,8,16]{2,1,0:T(8,128)} %bitcast.39), custom_call_target="tpu_custom_call" | custom-call | flops 20000000000 | bytes 1000000 | tf_op jit(solution)/shard_map/pallas_call | solution.py:362
  2.0 5.1 %collective-permute-start.2 = (bf16[32,1152]{1,0:T(8,128)(2,1)S(1)}, bf16[32,1152]{1,0:T(8,128)(2,1)S(1)}, u32[]{:S(2)}, u32[]{:S(2)}) collective-permute-start(bf16[32,1152]{1,0:T(8,128)(2,1)S(1)} %shard_map.118.own_ref), channel_id=1, source_target_pairs={{0,12},{4,8},{8,4},{12,0},{1,13},{5,9},{9,5},{13,1},{2,14},{6,10},... | collective-permute-start | bytes 221192 | tf_op jit(solution)/shard_map/ppermute | solution.py:153
  7.1 0.6 %collective-permute-start = (bf16[32,1152]{1,0:T(8,128)(2,1)S(1)}, bf16[32,1152]{1,0:T(8,128)(2,1)S(1)}, u32[]{:S(2)}, u32[]{:S(2)}) collective-permute-start(bf16[32,1152]{1,0:T(8,128)(2,1)S(1)} %shard_map.118.own_ref), channel_id=1, source_target_pairs={{0,4},{4,0},{8,12},{12,8},{1,5},{5,1},{9,13},{13,9},{2,6},{6,2},{1... | collective-permute-start | bytes 221192 | tf_op jit(solution)/shard_map/ppermute | solution.py:153
  7.8 1.6 %collective-permute-start.3 = (bf16[32,512]{1,0:T(8,128)(2,1)S(1)}, bf16[32,512]{1,0:T(8,128)(2,1)S(1)}, u32[]{:S(2)}, u32[]{:S(2)}) collective-permute-start(bf16[32,512]{1,0:T(8,128)(2,1)S(1)} %bitcast.37), channel_id=1, source_target_pairs={{0,2},{4,3},{8,0},{12,1},{5,6},{1,7},{9,4},{13,5},{10,8},{6,9},{14... | collective-permute-start | bytes 98312 | tf_op jit(solution)/shard_map/ppermute | solution.py:349
  9.6 5.2 %collective-permute-done.3.res_ref = bf16[32,512]{1,0:T(8,128)(2,1)S(1)} collective-permute-done((bf16[32,512]{1,0:T(8,128)(2,1)S(1)}, bf16[32,512]{1,0:T(8,128)(2,1)S(1)}, u32[]{:S(2)}, u32[]{:S(2)}) %collective-permute-start.3) | collective-permute-done | bytes 32800 | tf_op jit(solution)/shard_map/ppermute | solution.py:349
  14.8 0.9 %shard_map.119 = (f32[128,256]{1,0:T(8,128)S(1)}, bf16[128,256]{1,0:T(8,128)(2,1)S(1)}, bf16[128,128]{1,0:T(8,128)(2,1)S(1)}) custom-call(s32[3]{0:T(128)S(1)} %pad_add_fusion.where_ref, bf16[32,1152]{1,0:T(8,128)(2,1)S(1)} %shard_map.118.own_ref, bf16[32,1152]{1,0:T(8,128)(2,1)S(1)} %collective-permute-done.got1_ref, ...), custom_call_target="tpu_custom_call" | custom-call | flops 30000001024 | bytes 1000000 | tf_op jit(solution)/shard_map/pallas_call | solution.py:375
  15.7 1.2 %collective-permute-done.4 = bf16[128,256]{1,0:T(8,128)(2,1)S(1)} collective-permute-done((bf16[128,256]{1,0:T(8,128)(2,1)S(1)}, bf16[128,256]{1,0:T(8,128)(2,1)S(1)}, u32[]{:S(2)}, u32[]{:S(2)}) %collective-permute-start.4) | collective-permute-done | bytes 65568 | tf_op jit(solution)/shard_map/ppermute | solution.py:153
  17.1 4.2 %collective-permute-done.5 = bf16[128,256]{1,0:T(8,128)(2,1)S(1)} collective-permute-done((bf16[128,256]{1,0:T(8,128)(2,1)S(1)}, bf16[128,256]{1,0:T(8,128)(2,1)S(1)}, u32[]{:S(2)}, u32[]{:S(2)}) %collective-permute-start.5) | collective-permute-done | bytes 65568 | tf_op jit(solution)/shard_map/ppermute | solution.py:153
  21.4 2.1 %collective-permute-start.8 = (bf16[128,256]{1,0:T(8,128)(2,1)S(1)}, bf16[128,256]{1,0:T(8,128)(2,1)S(1)}, u32[]{:S(2)}, u32[]{:S(2)}) collective-permute-start(bf16[128,256]{1,0:T(8,128)(2,1)S(1)} %add_convert_fusion.1), channel_id=1, source_target_pairs={{0,12},{4,8},{8,4},{12,0},{1,13},{5,9},{9,5},{13,1},{2,14},{6,10},... | collective-permute-start | bytes 196616 | tf_op jit(solution)/shard_map/ppermute | solution.py:153
  23.8 2.0 %collective-permute-start.6 = (bf16[128,256]{1,0:T(8,128)(2,1)S(1)}, bf16[128,256]{1,0:T(8,128)(2,1)S(1)}, u32[]{:S(2)}, u32[]{:S(2)}) collective-permute-start(bf16[128,256]{1,0:T(8,128)(2,1)S(1)} %add_convert_fusion.1), channel_id=1, source_target_pairs={{0,4},{4,0},{8,12},{12,8},{1,5},{5,1},{9,13},{13,9},{2,6},{6,2},{1... | collective-permute-start | bytes 196616 | tf_op jit(solution)/shard_map/ppermute | solution.py:153
  25.8 2.5 %collective-permute-done.8 = bf16[128,256]{1,0:T(8,128)(2,1)S(1)} collective-permute-done((bf16[128,256]{1,0:T(8,128)(2,1)S(1)}, bf16[128,256]{1,0:T(8,128)(2,1)S(1)}, u32[]{:S(2)}, u32[]{:S(2)}) %collective-permute-start.8) | collective-permute-done | bytes 65568 | tf_op jit(solution)/shard_map/ppermute | solution.py:153
  28.3 1.5 %collective-permute-done.7 = bf16[128,256]{1,0:T(8,128)(2,1)S(1)} collective-permute-done((bf16[128,256]{1,0:T(8,128)(2,1)S(1)}, bf16[128,256]{1,0:T(8,128)(2,1)S(1)}, u32[]{:S(2)}, u32[]{:S(2)}) %collective-permute-start.7) | collective-permute-done | bytes 65568 | tf_op jit(solution)/shard_map/ppermute | solution.py:153
  29.9 0.5 collective-permute-start.9
  30.4 1.0 %collective-permute-done.9 = bf16[128,256]{1,0:T(8,128)(2,1)S(1)} collective-permute-done((bf16[128,256]{1,0:T(8,128)(2,1)S(1)}, bf16[128,256]{1,0:T(8,128)(2,1)S(1)}, u32[]{:S(2)}, u32[]{:S(2)}) %collective-permute-start.9) | collective-permute-done | bytes 65568 | tf_op jit(solution)/shard_map/ppermute | solution.py:153
  31.6 6.9 %shard_map.120 = (bf16[128,4096]{1,0:T(8,128)(2,1)S(1)}, bf16[128,1024]{1,0:T(8,128)(2,1)S(1)}, bf16[32,512]{1,0:T(8,128)(2,1)S(1)}) custom-call(s32[3]{0:T(128)} %copy-done, bf16[4,128,256]{2,1,0:T(8,128)(2,1)S(1)} %pad_maximum_fusion.mine_ref, bf16[4,128,256]{2,1,0:T(8,128)(2,1)S(1)} %pad_maximum_fusion.1.other_ref, ...), custom_call_target="tpu_custom_call" | custom-call | tf_op jit(solution)/shard_map/pallas_call | solution.py:399
  38.9 1.8 %shard_map.121 = f32[128,1024]{1,0:T(8,128)S(1)} custom-call(s32[3]{0:T(128)S(1)} %copy-done.1, bf16[128,4096]{1,0:T(8,128)(2,1)S(1)} %get-tuple-element.15.hid_ref, bf16[4096,2048]{1,0:T(8,128)(2,1)S(1)} %bitcast.20), custom_call_target="tpu_custom_call" | custom-call | flops 2000000000 | bytes 1000000 | tf_op jit(solution)/shard_map/pallas_call | solution.py:418
  40.8 1.1 %collective-permute-start.12 = (bf16[32,1024]{1,0:T(8,128)(2,1)S(1)}, bf16[32,1024]{1,0:T(8,128)(2,1)S(1)}, u32[]{:S(2)}, u32[]{:S(2)}) collective-permute-start(bf16[32,1024]{1,0:T(8,128)(2,1)S(1)} %get-tuple-element.17), channel_id=1, source_target_pairs={{0,8},{1,11},{2,10},{3,9},{4,12},{5,15},{6,14},{7,13},{8,0},{9,3},... | collective-permute-start | bytes 196616 | tf_op jit(solution)/shard_map/ppermute | solution.py:430
  41.9 1.7 %collective-permute-start.15 = (bf16[32,1024]{1,0:T(8,128)(2,1)S(1)}, bf16[32,1024]{1,0:T(8,128)(2,1)S(1)}, u32[]{:S(2)}, u32[]{:S(2)}) collective-permute-start(bf16[32,1024]{1,0:T(8,128)(2,1)S(1)} %get-tuple-element.18), channel_id=1, source_target_pairs={{0,12},{1,15},{2,14},{3,13},{4,8},{5,11},{6,10},{7,9},{8,4},{9,7},... | collective-permute-start | bytes 196616 | tf_op jit(solution)/shard_map/ppermute | solution.py:430
  43.5 0.8 %collective-permute-start.14 = (bf16[32,1024]{1,0:T(8,128)(2,1)S(1)}, bf16[32,1024]{1,0:T(8,128)(2,1)S(1)}, u32[]{:S(2)}, u32[]{:S(2)}) collective-permute-start(bf16[32,1024]{1,0:T(8,128)(2,1)S(1)} %get-tuple-element.19), channel_id=1, source_target_pairs={{0,4},{1,7},{2,6},{3,5},{4,0},{5,3},{6,2},{7,1},{8,12},{9,15},{10,... | collective-permute-start | bytes 196616 | tf_op jit(solution)/shard_map/ppermute | solution.py:430
  44.3 0.7 %collective-permute-start.13 = (bf16[32,1024]{1,0:T(8,128)(2,1)S(1)}, bf16[32,1024]{1,0:T(8,128)(2,1)S(1)}, u32[]{:S(2)}, u32[]{:S(2)}) collective-permute-start(bf16[32,1024]{1,0:T(8,128)(2,1)S(1)} %get-tuple-element.20), channel_id=1, source_target_pairs={{0,0},{1,3},{2,2},{3,1},{4,4},{5,7},{6,6},{7,5},{8,8},{9,11},{10,1... | collective-permute-start | bytes 196616 | tf_op jit(solution)/shard_map/ppermute | solution.py:430
  45.0 4.2 %collective-permute-done.12 = bf16[32,1024]{1,0:T(8,128)(2,1)S(1)} collective-permute-done((bf16[32,1024]{1,0:T(8,128)(2,1)S(1)}, bf16[32,1024]{1,0:T(8,128)(2,1)S(1)}, u32[]{:S(2)}, u32[]{:S(2)}) %collective-permute-start.12) | collective-permute-done | bytes 65568 | tf_op jit(solution)/shard_map/ppermute | solution.py:430
  49.2 1.3 %collective-permute-done.14 = bf16[32,1024]{1,0:T(8,128)(2,1)S(1)} collective-permute-done((bf16[32,1024]{1,0:T(8,128)(2,1)S(1)}, bf16[32,1024]{1,0:T(8,128)(2,1)S(1)}, u32[]{:S(2)}, u32[]{:S(2)}) %collective-permute-start.14) | collective-permute-done | bytes 65568 | tf_op jit(solution)/shard_map/ppermute | solution.py:430
  50.8 1.0 %collective-permute-done.16 = bf16[32,512]{1,0:T(8,128)(2,1)S(1)} collective-permute-done((bf16[32,512]{1,0:T(8,128)(2,1)S(1)}, bf16[32,512]{1,0:T(8,128)(2,1)S(1)}, u32[]{:S(2)}, u32[]{:S(2)}) %collective-permute-start.16) | collective-permute-done | bytes 32800 | tf_op jit(solution)/shard_map/ppermute | solution.py:153
  51.8 0.6 %add_convert_fusion.3 = bf16[32,512]{1,0:T(8,128)(2,1)} fusion(bf16[32,512]{1,0:T(8,128)(2,1)S(1)} %collective-permute-done.16, bf16[32,512]{1,0:T(8,128)(2,1)S(1)} %get-tuple-element.14, f32[32,1024]{1,0:T(8,128)S(1)} %convert_add_fusion, pred[]{:T(512)S(6)} %eq.26), kind=kLoop, calls=%fused_computation.7 | loop fusion | flops 98304 | bytes 229377 | tf_op jit(solution)/shard_map/convert_element_type | solution.py:442
  (60 shorter events, 1.7 us)
Async XLA Ops:
  2.0 12.7 %collective-permute-start.2 = (bf16[32,1152]{1,0:T(8,128)(2,1)S(1)}, bf16[32,1152]{1,0:T(8,128)(2,1)S(1)}, u32[]{:S(2)}, u32[]{:S(2)}) collective-permute-start(bf16[32,1152]{1,0:T(8,128)(2,1)S(1)} %shard_map.118.own_ref), channel_id=1, source_target_pairs={{0,12},{4,8},{8,4},{12,0},{1,13},{5,9},{9,5},{13,1},{2,14},{6,10},... | collective-permute-start | bytes 221192 | tf_op jit(solution)/shard_map/ppermute | solution.py:153
  7.1 7.6 %collective-permute-start.1 = (bf16[32,1152]{1,0:T(8,128)(2,1)S(1)}, bf16[32,1152]{1,0:T(8,128)(2,1)S(1)}, u32[]{:S(2)}, u32[]{:S(2)}) collective-permute-start(bf16[32,1152]{1,0:T(8,128)(2,1)S(1)} %shard_map.118.own_ref), channel_id=1, source_target_pairs={{0,8},{4,12},{8,0},{12,4},{1,9},{5,13},{9,1},{13,5},{2,10},{6,14},... | collective-permute-start | bytes 221192 | tf_op jit(solution)/shard_map/ppermute | solution.py:153
  7.1 7.6 %collective-permute-start = (bf16[32,1152]{1,0:T(8,128)(2,1)S(1)}, bf16[32,1152]{1,0:T(8,128)(2,1)S(1)}, u32[]{:S(2)}, u32[]{:S(2)}) collective-permute-start(bf16[32,1152]{1,0:T(8,128)(2,1)S(1)} %shard_map.118.own_ref), channel_id=1, source_target_pairs={{0,4},{4,0},{8,12},{12,8},{1,5},{5,1},{9,13},{13,9},{2,6},{6,2},{1... | collective-permute-start | bytes 221192 | tf_op jit(solution)/shard_map/ppermute | solution.py:153
  7.8 7.0 %collective-permute-start.3 = (bf16[32,512]{1,0:T(8,128)(2,1)S(1)}, bf16[32,512]{1,0:T(8,128)(2,1)S(1)}, u32[]{:S(2)}, u32[]{:S(2)}) collective-permute-start(bf16[32,512]{1,0:T(8,128)(2,1)S(1)} %bitcast.37), channel_id=1, source_target_pairs={{0,2},{4,3},{8,0},{12,1},{5,6},{1,7},{9,4},{13,5},{10,8},{6,9},{14... | collective-permute-start | bytes 98312 | tf_op jit(solution)/shard_map/ppermute | solution.py:349
  9.4 22.0 %slice-start = ((s8[16777216]{0:T(1024)(128)(4,1)}), s8[4194304]{0:T(1024)(128)(4,1)S(1)}, s32[]{:S(2)}) async-start(s8[16777216]{0:T(1024)(128)(4,1)} %bitcast.17), calls=%async_computation | async-start | bytes 8388608
  9.4 22.0 %slice-start.4 = ((s8[16777216]{0:T(1024)(128)(4,1)}), s8[4194304]{0:T(1024)(128)(4,1)S(1)}, s32[]{:S(2)}) async-start(s8[16777216]{0:T(1024)(128)(4,1)} %bitcast.21), calls=%async_computation.4 | async-start | bytes 8388608
  9.4 22.1 %slice-start.8 = ((s8[16777216]{0:T(1024)(128)(4,1)}), s8[4194304]{0:T(1024)(128)(4,1)S(1)}, s32[]{:S(2)}) async-start(s8[16777216]{0:T(1024)(128)(4,1)} %bitcast.23), calls=%async_computation.8 | async-start | bytes 8388608
  9.5 22.0 %slice-start.3 = ((s8[16777216]{0:T(1024)(128)(4,1)}), s8[4194304]{0:T(1024)(128)(4,1)S(1)}, s32[]{:S(2)}) async-start(s8[16777216]{0:T(1024)(128)(4,1)} %bitcast.17), calls=%async_computation.3 | async-start | bytes 8388608
  9.5 22.0 %slice-start.5 = ((s8[16777216]{0:T(1024)(128)(4,1)}), s8[4194304]{0:T(1024)(128)(4,1)S(1)}, s32[]{:S(2)}) async-start(s8[16777216]{0:T(1024)(128)(4,1)} %bitcast.21), calls=%async_computation.5 | async-start | bytes 8388608
  9.5 22.0 %slice-start.6 = ((s8[16777216]{0:T(1024)(128)(4,1)}), s8[4194304]{0:T(1024)(128)(4,1)S(1)}, s32[]{:S(2)}) async-start(s8[16777216]{0:T(1024)(128)(4,1)} %bitcast.21), calls=%async_computation.6 | async-start | bytes 8388608
  9.5 22.0 %slice-start.7 = ((s8[16777216]{0:T(1024)(128)(4,1)}), s8[4194304]{0:T(1024)(128)(4,1)S(1)}, s32[]{:S(2)}) async-start(s8[16777216]{0:T(1024)(128)(4,1)} %bitcast.21), calls=%async_computation.7 | async-start | bytes 8388608
  15.7 1.3 %collective-permute-start.4 = (bf16[128,256]{1,0:T(8,128)(2,1)S(1)}, bf16[128,256]{1,0:T(8,128)(2,1)S(1)}, u32[]{:S(2)}, u32[]{:S(2)}) collective-permute-start(bf16[128,256]{1,0:T(8,128)(2,1)S(1)} %get-tuple-element.12), channel_id=1, source_target_pairs={{0,1},{1,0},{2,3},{3,2},{4,5},{5,4},{6,7},{7,6},{8,9},{9,8},{10,11... | collective-permute-start | bytes 196616 | tf_op jit(solution)/shard_map/ppermute | solution.py:153
  17.0 4.3 %collective-permute-start.5 = (bf16[128,256]{1,0:T(8,128)(2,1)S(1)}, bf16[128,256]{1,0:T(8,128)(2,1)S(1)}, u32[]{:S(2)}, u32[]{:S(2)}) collective-permute-start(bf16[128,256]{1,0:T(8,128)(2,1)S(1)} %add_convert_fusion.2), channel_id=1, source_target_pairs={{0,2},{1,3},{2,0},{3,1},{4,6},{5,7},{6,4},{7,5},{8,10},{9,11},{10,... | collective-permute-start | bytes 196616 | tf_op jit(solution)/shard_map/ppermute | solution.py:153
  21.4 6.9 %collective-permute-start.8 = (bf16[128,256]{1,0:T(8,128)(2,1)S(1)}, bf16[128,256]{1,0:T(8,128)(2,1)S(1)}, u32[]{:S(2)}, u32[]{:S(2)}) collective-permute-start(bf16[128,256]{1,0:T(8,128)(2,1)S(1)} %add_convert_fusion.1), channel_id=1, source_target_pairs={{0,12},{4,8},{8,4},{12,0},{1,13},{5,9},{9,5},{13,1},{2,14},{6,10},... | collective-permute-start | bytes 196616 | tf_op jit(solution)/shard_map/ppermute | solution.py:153
  23.4 6.4 %collective-permute-start.7 = (bf16[128,256]{1,0:T(8,128)(2,1)S(1)}, bf16[128,256]{1,0:T(8,128)(2,1)S(1)}, u32[]{:S(2)}, u32[]{:S(2)}) collective-permute-start(bf16[128,256]{1,0:T(8,128)(2,1)S(1)} %add_convert_fusion.1), channel_id=1, source_target_pairs={{0,8},{4,12},{8,0},{12,4},{1,9},{5,13},{9,1},{13,5},{2,10},{6,14},... | collective-permute-start | bytes 196616 | tf_op jit(solution)/shard_map/ppermute | solution.py:153
  23.8 6.0 %collective-permute-start.6 = (bf16[128,256]{1,0:T(8,128)(2,1)S(1)}, bf16[128,256]{1,0:T(8,128)(2,1)S(1)}, u32[]{:S(2)}, u32[]{:S(2)}) collective-permute-start(bf16[128,256]{1,0:T(8,128)(2,1)S(1)} %add_convert_fusion.1), channel_id=1, source_target_pairs={{0,4},{4,0},{8,12},{12,8},{1,5},{5,1},{9,13},{13,9},{2,6},{6,2},{1... | collective-permute-start | bytes 196616 | tf_op jit(solution)/shard_map/ppermute | solution.py:153
  29.8 1.6 %collective-permute-start.10 = (bf16[3,128,256]{2,1,0:T(8,128)(2,1)S(1)}, bf16[3,128,256]{2,1,0:T(8,128)(2,1)S(1)}, u32[]{:S(2)}, u32[]{:S(2)}) collective-permute-start(bf16[3,128,256]{2,1,0:T(8,128)(2,1)S(1)} %pad_maximum_fusion.2), channel_id=1, source_target_pairs={{0,1},{1,0},{2,3},{3,2},{4,5},{5,4},{6,7},{7,6},{8,9},{9,8},{10,11... | collective-permute-start | bytes 589832 | tf_op jit(solution)/shard_map/ppermute | solution.py:153
  29.9 1.5 %collective-permute-start.9 = (bf16[128,256]{1,0:T(8,128)(2,1)S(1)}, bf16[128,256]{1,0:T(8,128)(2,1)S(1)}, u32[]{:S(2)}, u32[]{:S(2)}) collective-permute-start(bf16[128,256]{1,0:T(8,128)(2,1)S(1)} %add_convert_fusion.1), channel_id=1, source_target_pairs={{0,1},{1,0},{2,3},{3,2},{4,5},{5,4},{6,7},{7,6},{8,9},{9,8},{10,11... | collective-permute-start | bytes 196616 | tf_op jit(solution)/shard_map/ppermute | solution.py:153
  38.6 2.1 %collective-permute-start.11 = (bf16[128,1024]{1,0:T(8,128)(2,1)S(1)}, bf16[128,1024]{1,0:T(8,128)(2,1)S(1)}, u32[]{:S(2)}, u32[]{:S(2)}) collective-permute-start(bf16[128,1024]{1,0:T(8,128)(2,1)S(1)} %get-tuple-element.16), channel_id=1, source_target_pairs={{0,1},{1,0},{2,3},{3,2},{4,5},{5,4},{6,7},{7,6},{8,9},{9,8},{10,11... | collective-permute-start | bytes 786440 | tf_op jit(solution)/shard_map/ppermute | solution.py:153
  40.8 8.4 %collective-permute-start.12 = (bf16[32,1024]{1,0:T(8,128)(2,1)S(1)}, bf16[32,1024]{1,0:T(8,128)(2,1)S(1)}, u32[]{:S(2)}, u32[]{:S(2)}) collective-permute-start(bf16[32,1024]{1,0:T(8,128)(2,1)S(1)} %get-tuple-element.17), channel_id=1, source_target_pairs={{0,8},{1,11},{2,10},{3,9},{4,12},{5,15},{6,14},{7,13},{8,0},{9,3},... | collective-permute-start | bytes 196616 | tf_op jit(solution)/shard_map/ppermute | solution.py:430
  41.9 7.3 %collective-permute-start.15 = (bf16[32,1024]{1,0:T(8,128)(2,1)S(1)}, bf16[32,1024]{1,0:T(8,128)(2,1)S(1)}, u32[]{:S(2)}, u32[]{:S(2)}) collective-permute-start(bf16[32,1024]{1,0:T(8,128)(2,1)S(1)} %get-tuple-element.18), channel_id=1, source_target_pairs={{0,12},{1,15},{2,14},{3,13},{4,8},{5,11},{6,10},{7,9},{8,4},{9,7},... | collective-permute-start | bytes 196616 | tf_op jit(solution)/shard_map/ppermute | solution.py:430
  43.5 7.0 %collective-permute-start.14 = (bf16[32,1024]{1,0:T(8,128)(2,1)S(1)}, bf16[32,1024]{1,0:T(8,128)(2,1)S(1)}, u32[]{:S(2)}, u32[]{:S(2)}) collective-permute-start(bf16[32,1024]{1,0:T(8,128)(2,1)S(1)} %get-tuple-element.19), channel_id=1, source_target_pairs={{0,4},{1,7},{2,6},{3,5},{4,0},{5,3},{6,2},{7,1},{8,12},{9,15},{10,... | collective-permute-start | bytes 196616 | tf_op jit(solution)/shard_map/ppermute | solution.py:430
  44.3 6.1 %collective-permute-start.13 = (bf16[32,1024]{1,0:T(8,128)(2,1)S(1)}, bf16[32,1024]{1,0:T(8,128)(2,1)S(1)}, u32[]{:S(2)}, u32[]{:S(2)}) collective-permute-start(bf16[32,1024]{1,0:T(8,128)(2,1)S(1)} %get-tuple-element.20), channel_id=1, source_target_pairs={{0,0},{1,3},{2,2},{3,1},{4,4},{5,7},{6,6},{7,5},{8,8},{9,11},{10,1... | collective-permute-start | bytes 196616 | tf_op jit(solution)/shard_map/ppermute | solution.py:430
  50.5 1.3 %collective-permute-start.16 = (bf16[32,512]{1,0:T(8,128)(2,1)S(1)}, bf16[32,512]{1,0:T(8,128)(2,1)S(1)}, u32[]{:S(2)}, u32[]{:S(2)}) collective-permute-start(bf16[32,512]{1,0:T(8,128)(2,1)S(1)} %select_convert_fusion), channel_id=1, source_target_pairs={{0,1},{1,0},{2,3},{3,2},{4,5},{5,4},{6,7},{7,6},{8,9},{9,8},{10,11... | collective-permute-start | bytes 98312 | tf_op jit(solution)/shard_map/ppermute | solution.py:153
  (9 other events, 145.9 us)
